TPU v7x, 32 devices: a whole 2x2x4 slice. The times are simulated.
32 devices in a mesh: site: 4 (over y, core), bond: 8 (over z, x).
Axes of the slice: x: 2, y: 2, z: 4, core: 2. Of those that a mesh axis runs over, the one named last changes fastest.
Arguments:
- left_start: float32 [2048, 1024], P('bond'), may hold values from -6 to 6
- site_mats: float32 [4, 2, 2048, 2048], P('site', None, 'bond'), may hold values from -0.125 to 0.125
- clicks: int32 [4, 1024], P('site'), may hold values 0 or 1
Outputs:
- final_states: float32 [2048, 1024], P('bond', 'site')
All inputs are finite; a program needn't handle non-finite values. No bound on the sum of `clicks` on one device may be relied on, other than what follows from the above.
Results may differ from a plain program's by a relative error of at most 0.00026.
Values sent between devices are 32-bit elements; how exact they have to be, the bound alone decides.
No kernel may reach another device: no remote copies, remote signals or barrier semaphores. Data moves between devices by JAX's collectives and lax.ppermute only.
A program may use at most 64 MiB of HBM per device.

v0:
```python
import jax
import jax.numpy as jnp
from jax import lax
from jax.sharding import PartitionSpec as P

BATCH = 64
MICRO = 16


def from_behind(x, axis, by):
    size = lax.axis_size(axis)
    pairs = [(i, i + by) for i in range(size) if 0 <= i + by < size]
    return lax.ppermute(x, axis, pairs)


def local(left_start, site_mats, clicks):
    site_index = lax.axis_index("site")
    owners = lax.axis_size("site")
    out_rows = site_mats.shape[2]
    matrix_pair = site_mats[0]
    click_row = clicks[0]
    ticks = MICRO + owners - 1

    def contract(states, chosen):
        first = jnp.dot(
            matrix_pair[0],
            states,
            precision=lax.Precision.HIGHEST,
            preferred_element_type=jnp.float32,
        )
        second = jnp.dot(
            matrix_pair[1],
            states,
            precision=lax.Precision.HIGHEST,
            preferred_element_type=jnp.float32,
        )
        return jnp.where(chosen[None, :] == 1, second, first)

    def tick(step, carry):
        incoming, finals = carry
        batch = step - site_index
        valid = (batch >= 0) & (batch < MICRO)
        offset = jnp.clip(batch, 0, MICRO - 1) * BATCH
        start_cols = lax.dynamic_slice_in_dim(left_start, offset, BATCH, 1)
        own_cols = jnp.where(site_index == 0, start_cols, incoming)
        chosen = lax.dynamic_slice_in_dim(click_row, offset, BATCH, 0)
        whole = lax.all_gather(own_cols, "bond", axis=0, tiled=True)
        fresh = contract(whole, chosen)
        store = valid & (site_index == owners - 1)
        current = lax.dynamic_slice_in_dim(finals, offset, BATCH, 1)
        finals = lax.dynamic_update_slice_in_dim(
            finals, jnp.where(store, fresh, current), offset, 1
        )
        handed = from_behind(fresh, "site", 1)
        return (handed, finals)

    incoming = jnp.zeros((out_rows, BATCH), jnp.float32)
    finals = jnp.zeros((out_rows, left_start.shape[1]), jnp.float32)
    incoming, finals = lax.fori_loop(0, ticks, tick, (incoming, finals))
    return lax.psum_scatter(finals, "site", scatter_dimension=1, tiled=True)


def solution(mesh):
    return jax.shard_map(
        local,
        mesh=mesh,
        in_specs=(P("bond", None), P("site", None, "bond", None), P("site", None)),
        out_specs=P("bond", "site"),
        check_vma=False,
    )
```

profile of v0, /device:TPU:25, one launch (start us, length us, event | category | flops | bytes accessed | tf_op | source)
XLA Modules:
  0.0 901.0 jit_solution(13099116820459265244)
XLA Ops:
  8.2 855.4 %while.16 = (s32[]{:T(128)}, f32[256,64]{0,1:T(8,128)S(1)}, f32[256,1024]{0,1:T(8,128)S(1)}, s32[]{:T(128)}, s32[1024]{0:T(1024)}, /*index=5*/pred[]{:T(512)}, f...) while((s32[]{:T(128)}, f32[256,64]{0,1:T(8,128)S(1)}, ...), condition=%wide.region_1.2_spmd, body=%wide.region_0.1_spmd.sunk | while | flops 805355584 | bytes 6620269 | solution.py:59
  9.0 23.1 %all_gather.9 = f32[2048,64]{0,1:T(8,128)S(1)} all-gather(f32[256,64]{0,1:T(8,128)S(1)} %dynamic-slice_select_fusion.2), channel_id=1, replica_groups=mesh['site'=4,'bond'=8] {'bond'}, dimensions={0}, use_global_device_ids=true | all-gather | bytes 589824 | tf_op jit(solution)/shard_map/while/body/eval_jaxpr/all_gather | solution.py:47
  50.6 25.7 %all_gather.9 = f32[2048,64]{0,1:T(8,128)S(1)} all-gather(f32[256,64]{0,1:T(8,128)S(1)} %dynamic-slice_select_fusion.2), channel_id=1, replica_groups=mesh['site'=4,'bond'=8] {'bond'}, dimensions={0}, use_global_device_ids=true | all-gather | bytes 589824 | tf_op jit(solution)/shard_map/while/body/eval_jaxpr/all_gather | solution.py:47
  83.5 10.2 %collective-permute-start = (f32[256,64]{0,1:T(8,128)S(1)}, f32[256,64]{0,1:T(8,128)S(1)}, u32[]{:S(2)}, u32[]{:S(2)}) collective-permute-start(f32[256,64]{0,1:T(8,128)S(1)} %get-tuple-element.252), channel_id=1, source_target_pairs={{0,8},{8,16},{16,24},{1,9},{9,17},{17,25},{2,10},{10,18},{18,26},{... | collective-permute-start | bytes 196616 | tf_op jit(solution)/shard_map/while/body/eval_jaxpr/ppermute | solution.py:13
  95.8 25.4 %all_gather.9 = f32[2048,64]{0,1:T(8,128)S(1)} all-gather(f32[256,64]{0,1:T(8,128)S(1)} %dynamic-slice_select_fusion.2), channel_id=1, replica_groups=mesh['site'=4,'bond'=8] {'bond'}, dimensions={0}, use_global_device_ids=true | all-gather | bytes 589824 | tf_op jit(solution)/shard_map/while/body/eval_jaxpr/all_gather | solution.py:47
  128.4 10.5 %collective-permute-start = (f32[256,64]{0,1:T(8,128)S(1)}, f32[256,64]{0,1:T(8,128)S(1)}, u32[]{:S(2)}, u32[]{:S(2)}) collective-permute-start(f32[256,64]{0,1:T(8,128)S(1)} %get-tuple-element.252), channel_id=1, source_target_pairs={{0,8},{8,16},{16,24},{1,9},{9,17},{17,25},{2,10},{10,18},{18,26},{... | collective-permute-start | bytes 196616 | tf_op jit(solution)/shard_map/while/body/eval_jaxpr/ppermute | solution.py:13
  141.0 26.0 %all_gather.9 = f32[2048,64]{0,1:T(8,128)S(1)} all-gather(f32[256,64]{0,1:T(8,128)S(1)} %dynamic-slice_select_fusion.2), channel_id=1, replica_groups=mesh['site'=4,'bond'=8] {'bond'}, dimensions={0}, use_global_device_ids=true | all-gather | bytes 589824 | tf_op jit(solution)/shard_map/while/body/eval_jaxpr/all_gather | solution.py:47
  186.2 25.7 %all_gather.9 = f32[2048,64]{0,1:T(8,128)S(1)} all-gather(f32[256,64]{0,1:T(8,128)S(1)} %dynamic-slice_select_fusion.2), channel_id=1, replica_groups=mesh['site'=4,'bond'=8] {'bond'}, dimensions={0}, use_global_device_ids=true | all-gather | bytes 589824 | tf_op jit(solution)/shard_map/while/body/eval_jaxpr/all_gather | solution.py:47
  219.2 10.2 %collective-permute-start = (f32[256,64]{0,1:T(8,128)S(1)}, f32[256,64]{0,1:T(8,128)S(1)}, u32[]{:S(2)}, u32[]{:S(2)}) collective-permute-start(f32[256,64]{0,1:T(8,128)S(1)} %get-tuple-element.252), channel_id=1, source_target_pairs={{0,8},{8,16},{16,24},{1,9},{9,17},{17,25},{2,10},{10,18},{18,26},{... | collective-permute-start | bytes 196616 | tf_op jit(solution)/shard_map/while/body/eval_jaxpr/ppermute | solution.py:13
  231.4 25.4 %all_gather.9 = f32[2048,64]{0,1:T(8,128)S(1)} all-gather(f32[256,64]{0,1:T(8,128)S(1)} %dynamic-slice_select_fusion.2), channel_id=1, replica_groups=mesh['site'=4,'bond'=8] {'bond'}, dimensions={0}, use_global_device_ids=true | all-gather | bytes 589824 | tf_op jit(solution)/shard_map/while/body/eval_jaxpr/all_gather | solution.py:47
  264.1 10.4 %collective-permute-start = (f32[256,64]{0,1:T(8,128)S(1)}, f32[256,64]{0,1:T(8,128)S(1)}, u32[]{:S(2)}, u32[]{:S(2)}) collective-permute-start(f32[256,64]{0,1:T(8,128)S(1)} %get-tuple-element.252), channel_id=1, source_target_pairs={{0,8},{8,16},{16,24},{1,9},{9,17},{17,25},{2,10},{10,18},{18,26},{... | collective-permute-start | bytes 196616 | tf_op jit(solution)/shard_map/while/body/eval_jaxpr/ppermute | solution.py:13
  276.6 25.9 %all_gather.9 = f32[2048,64]{0,1:T(8,128)S(1)} all-gather(f32[256,64]{0,1:T(8,128)S(1)} %dynamic-slice_select_fusion.2), channel_id=1, replica_groups=mesh['site'=4,'bond'=8] {'bond'}, dimensions={0}, use_global_device_ids=true | all-gather | bytes 589824 | tf_op jit(solution)/shard_map/while/body/eval_jaxpr/all_gather | solution.py:47
  321.8 25.4 %all_gather.9 = f32[2048,64]{0,1:T(8,128)S(1)} all-gather(f32[256,64]{0,1:T(8,128)S(1)} %dynamic-slice_select_fusion.2), channel_id=1, replica_groups=mesh['site'=4,'bond'=8] {'bond'}, dimensions={0}, use_global_device_ids=true | all-gather | bytes 589824 | tf_op jit(solution)/shard_map/while/body/eval_jaxpr/all_gather | solution.py:47
  354.6 10.4 %collective-permute-start = (f32[256,64]{0,1:T(8,128)S(1)}, f32[256,64]{0,1:T(8,128)S(1)}, u32[]{:S(2)}, u32[]{:S(2)}) collective-permute-start(f32[256,64]{0,1:T(8,128)S(1)} %get-tuple-element.252), channel_id=1, source_target_pairs={{0,8},{8,16},{16,24},{1,9},{9,17},{17,25},{2,10},{10,18},{18,26},{... | collective-permute-start | bytes 196616 | tf_op jit(solution)/shard_map/while/body/eval_jaxpr/ppermute | solution.py:13
  367.1 25.8 %all_gather.9 = f32[2048,64]{0,1:T(8,128)S(1)} all-gather(f32[256,64]{0,1:T(8,128)S(1)} %dynamic-slice_select_fusion.2), channel_id=1, replica_groups=mesh['site'=4,'bond'=8] {'bond'}, dimensions={0}, use_global_device_ids=true | all-gather | bytes 589824 | tf_op jit(solution)/shard_map/while/body/eval_jaxpr/all_gather | solution.py:47
  412.3 25.5 %all_gather.9 = f32[2048,64]{0,1:T(8,128)S(1)} all-gather(f32[256,64]{0,1:T(8,128)S(1)} %dynamic-slice_select_fusion.2), channel_id=1, replica_groups=mesh['site'=4,'bond'=8] {'bond'}, dimensions={0}, use_global_device_ids=true | all-gather | bytes 589824 | tf_op jit(solution)/shard_map/while/body/eval_jaxpr/all_gather | solution.py:47
  445.0 10.4 %collective-permute-start = (f32[256,64]{0,1:T(8,128)S(1)}, f32[256,64]{0,1:T(8,128)S(1)}, u32[]{:S(2)}, u32[]{:S(2)}) collective-permute-start(f32[256,64]{0,1:T(8,128)S(1)} %get-tuple-element.252), channel_id=1, source_target_pairs={{0,8},{8,16},{16,24},{1,9},{9,17},{17,25},{2,10},{10,18},{18,26},{... | collective-permute-start | bytes 196616 | tf_op jit(solution)/shard_map/while/body/eval_jaxpr/ppermute | solution.py:13
  457.5 25.8 %all_gather.9 = f32[2048,64]{0,1:T(8,128)S(1)} all-gather(f32[256,64]{0,1:T(8,128)S(1)} %dynamic-slice_select_fusion.2), channel_id=1, replica_groups=mesh['site'=4,'bond'=8] {'bond'}, dimensions={0}, use_global_device_ids=true | all-gather | bytes 589824 | tf_op jit(solution)/shard_map/while/body/eval_jaxpr/all_gather | solution.py:47
  502.7 25.4 %all_gather.9 = f32[2048,64]{0,1:T(8,128)S(1)} all-gather(f32[256,64]{0,1:T(8,128)S(1)} %dynamic-slice_select_fusion.2), channel_id=1, replica_groups=mesh['site'=4,'bond'=8] {'bond'}, dimensions={0}, use_global_device_ids=true | all-gather | bytes 589824 | tf_op jit(solution)/shard_map/while/body/eval_jaxpr/all_gather | solution.py:47
  535.4 10.4 %collective-permute-start = (f32[256,64]{0,1:T(8,128)S(1)}, f32[256,64]{0,1:T(8,128)S(1)}, u32[]{:S(2)}, u32[]{:S(2)}) collective-permute-start(f32[256,64]{0,1:T(8,128)S(1)} %get-tuple-element.252), channel_id=1, source_target_pairs={{0,8},{8,16},{16,24},{1,9},{9,17},{17,25},{2,10},{10,18},{18,26},{... | collective-permute-start | bytes 196616 | tf_op jit(solution)/shard_map/while/body/eval_jaxpr/ppermute | solution.py:13
  547.9 25.8 %all_gather.9 = f32[2048,64]{0,1:T(8,128)S(1)} all-gather(f32[256,64]{0,1:T(8,128)S(1)} %dynamic-slice_select_fusion.2), channel_id=1, replica_groups=mesh['site'=4,'bond'=8] {'bond'}, dimensions={0}, use_global_device_ids=true | all-gather | bytes 589824 | tf_op jit(solution)/shard_map/while/body/eval_jaxpr/all_gather | solution.py:47
  593.1 25.9 %all_gather.9 = f32[2048,64]{0,1:T(8,128)S(1)} all-gather(f32[256,64]{0,1:T(8,128)S(1)} %dynamic-slice_select_fusion.2), channel_id=1, replica_groups=mesh['site'=4,'bond'=8] {'bond'}, dimensions={0}, use_global_device_ids=true | all-gather | bytes 589824 | tf_op jit(solution)/shard_map/while/body/eval_jaxpr/all_gather | solution.py:47
  638.3 25.6 %all_gather.9 = f32[2048,64]{0,1:T(8,128)S(1)} all-gather(f32[256,64]{0,1:T(8,128)S(1)} %dynamic-slice_select_fusion.2), channel_id=1, replica_groups=mesh['site'=4,'bond'=8] {'bond'}, dimensions={0}, use_global_device_ids=true | all-gather | bytes 589824 | tf_op jit(solution)/shard_map/while/body/eval_jaxpr/all_gather | solution.py:47
  671.2 10.3 %collective-permute-start = (f32[256,64]{0,1:T(8,128)S(1)}, f32[256,64]{0,1:T(8,128)S(1)}, u32[]{:S(2)}, u32[]{:S(2)}) collective-permute-start(f32[256,64]{0,1:T(8,128)S(1)} %get-tuple-element.252), channel_id=1, source_target_pairs={{0,8},{8,16},{16,24},{1,9},{9,17},{17,25},{2,10},{10,18},{18,26},{... | collective-permute-start | bytes 196616 | tf_op jit(solution)/shard_map/while/body/eval_jaxpr/ppermute | solution.py:13
  683.5 25.4 %all_gather.9 = f32[2048,64]{0,1:T(8,128)S(1)} all-gather(f32[256,64]{0,1:T(8,128)S(1)} %dynamic-slice_select_fusion.2), channel_id=1, replica_groups=mesh['site'=4,'bond'=8] {'bond'}, dimensions={0}, use_global_device_ids=true | all-gather | bytes 589824 | tf_op jit(solution)/shard_map/while/body/eval_jaxpr/all_gather | solution.py:47
  716.2 10.5 %collective-permute-start = (f32[256,64]{0,1:T(8,128)S(1)}, f32[256,64]{0,1:T(8,128)S(1)}, u32[]{:S(2)}, u32[]{:S(2)}) collective-permute-start(f32[256,64]{0,1:T(8,128)S(1)} %get-tuple-element.252), channel_id=1, source_target_pairs={{0,8},{8,16},{16,24},{1,9},{9,17},{17,25},{2,10},{10,18},{18,26},{... | collective-permute-start | bytes 196616 | tf_op jit(solution)/shard_map/while/body/eval_jaxpr/ppermute | solution.py:13
  728.7 25.8 %all_gather.9 = f32[2048,64]{0,1:T(8,128)S(1)} all-gather(f32[256,64]{0,1:T(8,128)S(1)} %dynamic-slice_select_fusion.2), channel_id=1, replica_groups=mesh['site'=4,'bond'=8] {'bond'}, dimensions={0}, use_global_device_ids=true | all-gather | bytes 589824 | tf_op jit(solution)/shard_map/while/body/eval_jaxpr/all_gather | solution.py:47
  761.7 10.1 %collective-permute-start = (f32[256,64]{0,1:T(8,128)S(1)}, f32[256,64]{0,1:T(8,128)S(1)}, u32[]{:S(2)}, u32[]{:S(2)}) collective-permute-start(f32[256,64]{0,1:T(8,128)S(1)} %get-tuple-element.252), channel_id=1, source_target_pairs={{0,8},{8,16},{16,24},{1,9},{9,17},{17,25},{2,10},{10,18},{18,26},{... | collective-permute-start | bytes 196616 | tf_op jit(solution)/shard_map/while/body/eval_jaxpr/ppermute | solution.py:13
  773.9 25.5 %all_gather.9 = f32[2048,64]{0,1:T(8,128)S(1)} all-gather(f32[256,64]{0,1:T(8,128)S(1)} %dynamic-slice_select_fusion.2), channel_id=1, replica_groups=mesh['site'=4,'bond'=8] {'bond'}, dimensions={0}, use_global_device_ids=true | all-gather | bytes 589824 | tf_op jit(solution)/shard_map/while/body/eval_jaxpr/all_gather | solution.py:47
  806.7 10.4 %collective-permute-start = (f32[256,64]{0,1:T(8,128)S(1)}, f32[256,64]{0,1:T(8,128)S(1)}, u32[]{:S(2)}, u32[]{:S(2)}) collective-permute-start(f32[256,64]{0,1:T(8,128)S(1)} %get-tuple-element.252), channel_id=1, source_target_pairs={{0,8},{8,16},{16,24},{1,9},{9,17},{17,25},{2,10},{10,18},{18,26},{... | collective-permute-start | bytes 196616 | tf_op jit(solution)/shard_map/while/body/eval_jaxpr/ppermute | solution.py:13
  819.1 25.9 %all_gather.9 = f32[2048,64]{0,1:T(8,128)S(1)} all-gather(f32[256,64]{0,1:T(8,128)S(1)} %dynamic-slice_select_fusion.2), channel_id=1, replica_groups=mesh['site'=4,'bond'=8] {'bond'}, dimensions={0}, use_global_device_ids=true | all-gather | bytes 589824 | tf_op jit(solution)/shard_map/while/body/eval_jaxpr/all_gather | solution.py:47
  864.9 29.3 %reduce-scatter.2.cloned.1.call-done = f32[256,256]{1,0:T(8,128)} async-done(((f32[256,1024]{1,0:T(8,128)}), f32[256,256]{1,0:T(8,128)}) %reduce-scatter.2.cloned.1.call-update) | async-done | bytes 262160 | tf_op jit(solution)/shard_map/reduce_scatter | solution.py:60
  (109 shorter events, 259.5 us)
Async XLA Ops:
  6.5 887.6 %reduce-scatter.2.cloned.1.call-start = ((), (), s32[]{:S(2)}) async-start(), calls=%async_computation.1 | async-start | bytes 1310720 | tf_op jit(solution)/shard_map/reduce_scatter | solution.py:60
  39.3 10.5 %collective-permute-start = (f32[256,64]{0,1:T(8,128)S(1)}, f32[256,64]{0,1:T(8,128)S(1)}, u32[]{:S(2)}, u32[]{:S(2)}) collective-permute-start(f32[256,64]{0,1:T(8,128)S(1)} %get-tuple-element.252), channel_id=1, source_target_pairs={{0,8},{8,16},{16,24},{1,9},{9,17},{17,25},{2,10},{10,18},{18,26},{... | collective-permute-start | bytes 196616 | tf_op jit(solution)/shard_map/while/body/eval_jaxpr/ppermute | solution.py:13
  83.5 11.5 %collective-permute-start = (f32[256,64]{0,1:T(8,128)S(1)}, f32[256,64]{0,1:T(8,128)S(1)}, u32[]{:S(2)}, u32[]{:S(2)}) collective-permute-start(f32[256,64]{0,1:T(8,128)S(1)} %get-tuple-element.252), channel_id=1, source_target_pairs={{0,8},{8,16},{16,24},{1,9},{9,17},{17,25},{2,10},{10,18},{18,26},{... | collective-permute-start | bytes 196616 | tf_op jit(solution)/shard_map/while/body/eval_jaxpr/ppermute | solution.py:13
  128.4 11.8 %collective-permute-start = (f32[256,64]{0,1:T(8,128)S(1)}, f32[256,64]{0,1:T(8,128)S(1)}, u32[]{:S(2)}, u32[]{:S(2)}) collective-permute-start(f32[256,64]{0,1:T(8,128)S(1)} %get-tuple-element.252), channel_id=1, source_target_pairs={{0,8},{8,16},{16,24},{1,9},{9,17},{17,25},{2,10},{10,18},{18,26},{... | collective-permute-start | bytes 196616 | tf_op jit(solution)/shard_map/while/body/eval_jaxpr/ppermute | solution.py:13
  174.3 11.2 %collective-permute-start = (f32[256,64]{0,1:T(8,128)S(1)}, f32[256,64]{0,1:T(8,128)S(1)}, u32[]{:S(2)}, u32[]{:S(2)}) collective-permute-start(f32[256,64]{0,1:T(8,128)S(1)} %get-tuple-element.252), channel_id=1, source_target_pairs={{0,8},{8,16},{16,24},{1,9},{9,17},{17,25},{2,10},{10,18},{18,26},{... | collective-permute-start | bytes 196616 | tf_op jit(solution)/shard_map/while/body/eval_jaxpr/ppermute | solution.py:13
  219.2 11.5 %collective-permute-start = (f32[256,64]{0,1:T(8,128)S(1)}, f32[256,64]{0,1:T(8,128)S(1)}, u32[]{:S(2)}, u32[]{:S(2)}) collective-permute-start(f32[256,64]{0,1:T(8,128)S(1)} %get-tuple-element.252), channel_id=1, source_target_pairs={{0,8},{8,16},{16,24},{1,9},{9,17},{17,25},{2,10},{10,18},{18,26},{... | collective-permute-start | bytes 196616 | tf_op jit(solution)/shard_map/while/body/eval_jaxpr/ppermute | solution.py:13
  264.1 11.7 %collective-permute-start = (f32[256,64]{0,1:T(8,128)S(1)}, f32[256,64]{0,1:T(8,128)S(1)}, u32[]{:S(2)}, u32[]{:S(2)}) collective-permute-start(f32[256,64]{0,1:T(8,128)S(1)} %get-tuple-element.252), channel_id=1, source_target_pairs={{0,8},{8,16},{16,24},{1,9},{9,17},{17,25},{2,10},{10,18},{18,26},{... | collective-permute-start | bytes 196616 | tf_op jit(solution)/shard_map/while/body/eval_jaxpr/ppermute | solution.py:13
  309.7 11.3 %collective-permute-start = (f32[256,64]{0,1:T(8,128)S(1)}, f32[256,64]{0,1:T(8,128)S(1)}, u32[]{:S(2)}, u32[]{:S(2)}) collective-permute-start(f32[256,64]{0,1:T(8,128)S(1)} %get-tuple-element.252), channel_id=1, source_target_pairs={{0,8},{8,16},{16,24},{1,9},{9,17},{17,25},{2,10},{10,18},{18,26},{... | collective-permute-start | bytes 196616 | tf_op jit(solution)/shard_map/while/body/eval_jaxpr/ppermute | solution.py:13
  354.6 11.7 %collective-permute-start = (f32[256,64]{0,1:T(8,128)S(1)}, f32[256,64]{0,1:T(8,128)S(1)}, u32[]{:S(2)}, u32[]{:S(2)}) collective-permute-start(f32[256,64]{0,1:T(8,128)S(1)} %get-tuple-element.252), channel_id=1, source_target_pairs={{0,8},{8,16},{16,24},{1,9},{9,17},{17,25},{2,10},{10,18},{18,26},{... | collective-permute-start | bytes 196616 | tf_op jit(solution)/shard_map/while/body/eval_jaxpr/ppermute | solution.py:13
  400.1 11.4 %collective-permute-start = (f32[256,64]{0,1:T(8,128)S(1)}, f32[256,64]{0,1:T(8,128)S(1)}, u32[]{:S(2)}, u32[]{:S(2)}) collective-permute-start(f32[256,64]{0,1:T(8,128)S(1)} %get-tuple-element.252), channel_id=1, source_target_pairs={{0,8},{8,16},{16,24},{1,9},{9,17},{17,25},{2,10},{10,18},{18,26},{... | collective-permute-start | bytes 196616 | tf_op jit(solution)/shard_map/while/body/eval_jaxpr/ppermute | solution.py:13
  445.0 11.7 %collective-permute-start = (f32[256,64]{0,1:T(8,128)S(1)}, f32[256,64]{0,1:T(8,128)S(1)}, u32[]{:S(2)}, u32[]{:S(2)}) collective-permute-start(f32[256,64]{0,1:T(8,128)S(1)} %get-tuple-element.252), channel_id=1, source_target_pairs={{0,8},{8,16},{16,24},{1,9},{9,17},{17,25},{2,10},{10,18},{18,26},{... | collective-permute-start | bytes 196616 | tf_op jit(solution)/shard_map/while/body/eval_jaxpr/ppermute | solution.py:13
  490.5 11.4 %collective-permute-start = (f32[256,64]{0,1:T(8,128)S(1)}, f32[256,64]{0,1:T(8,128)S(1)}, u32[]{:S(2)}, u32[]{:S(2)}) collective-permute-start(f32[256,64]{0,1:T(8,128)S(1)} %get-tuple-element.252), channel_id=1, source_target_pairs={{0,8},{8,16},{16,24},{1,9},{9,17},{17,25},{2,10},{10,18},{18,26},{... | collective-permute-start | bytes 196616 | tf_op jit(solution)/shard_map/while/body/eval_jaxpr/ppermute | solution.py:13
  535.4 11.7 %collective-permute-start = (f32[256,64]{0,1:T(8,128)S(1)}, f32[256,64]{0,1:T(8,128)S(1)}, u32[]{:S(2)}, u32[]{:S(2)}) collective-permute-start(f32[256,64]{0,1:T(8,128)S(1)} %get-tuple-element.252), channel_id=1, source_target_pairs={{0,8},{8,16},{16,24},{1,9},{9,17},{17,25},{2,10},{10,18},{18,26},{... | collective-permute-start | bytes 196616 | tf_op jit(solution)/shard_map/while/body/eval_jaxpr/ppermute | solution.py:13
  580.9 11.4 %collective-permute-start = (f32[256,64]{0,1:T(8,128)S(1)}, f32[256,64]{0,1:T(8,128)S(1)}, u32[]{:S(2)}, u32[]{:S(2)}) collective-permute-start(f32[256,64]{0,1:T(8,128)S(1)} %get-tuple-element.252), channel_id=1, source_target_pairs={{0,8},{8,16},{16,24},{1,9},{9,17},{17,25},{2,10},{10,18},{18,26},{... | collective-permute-start | bytes 196616 | tf_op jit(solution)/shard_map/while/body/eval_jaxpr/ppermute | solution.py:13
  626.2 11.3 %collective-permute-start = (f32[256,64]{0,1:T(8,128)S(1)}, f32[256,64]{0,1:T(8,128)S(1)}, u32[]{:S(2)}, u32[]{:S(2)}) collective-permute-start(f32[256,64]{0,1:T(8,128)S(1)} %get-tuple-element.252), channel_id=1, source_target_pairs={{0,8},{8,16},{16,24},{1,9},{9,17},{17,25},{2,10},{10,18},{18,26},{... | collective-permute-start | bytes 196616 | tf_op jit(solution)/shard_map/while/body/eval_jaxpr/ppermute | solution.py:13
  671.2 11.6 %collective-permute-start = (f32[256,64]{0,1:T(8,128)S(1)}, f32[256,64]{0,1:T(8,128)S(1)}, u32[]{:S(2)}, u32[]{:S(2)}) collective-permute-start(f32[256,64]{0,1:T(8,128)S(1)} %get-tuple-element.252), channel_id=1, source_target_pairs={{0,8},{8,16},{16,24},{1,9},{9,17},{17,25},{2,10},{10,18},{18,26},{... | collective-permute-start | bytes 196616 | tf_op jit(solution)/shard_map/while/body/eval_jaxpr/ppermute | solution.py:13
  716.2 11.8 %collective-permute-start = (f32[256,64]{0,1:T(8,128)S(1)}, f32[256,64]{0,1:T(8,128)S(1)}, u32[]{:S(2)}, u32[]{:S(2)}) collective-permute-start(f32[256,64]{0,1:T(8,128)S(1)} %get-tuple-element.252), channel_id=1, source_target_pairs={{0,8},{8,16},{16,24},{1,9},{9,17},{17,25},{2,10},{10,18},{18,26},{... | collective-permute-start | bytes 196616 | tf_op jit(solution)/shard_map/while/body/eval_jaxpr/ppermute | solution.py:13
  761.7 11.4 %collective-permute-start = (f32[256,64]{0,1:T(8,128)S(1)}, f32[256,64]{0,1:T(8,128)S(1)}, u32[]{:S(2)}, u32[]{:S(2)}) collective-permute-start(f32[256,64]{0,1:T(8,128)S(1)} %get-tuple-element.252), channel_id=1, source_target_pairs={{0,8},{8,16},{16,24},{1,9},{9,17},{17,25},{2,10},{10,18},{18,26},{... | collective-permute-start | bytes 196616 | tf_op jit(solution)/shard_map/while/body/eval_jaxpr/ppermute | solution.py:13
  806.7 11.7 %collective-permute-start = (f32[256,64]{0,1:T(8,128)S(1)}, f32[256,64]{0,1:T(8,128)S(1)}, u32[]{:S(2)}, u32[]{:S(2)}) collective-permute-start(f32[256,64]{0,1:T(8,128)S(1)} %get-tuple-element.252), channel_id=1, source_target_pairs={{0,8},{8,16},{16,24},{1,9},{9,17},{17,25},{2,10},{10,18},{18,26},{... | collective-permute-start | bytes 196616 | tf_op jit(solution)/shard_map/while/body/eval_jaxpr/ppermute | solution.py:13
  852.3 11.2 %collective-permute-start = (f32[256,64]{0,1:T(8,128)S(1)}, f32[256,64]{0,1:T(8,128)S(1)}, u32[]{:S(2)}, u32[]{:S(2)}) collective-permute-start(f32[256,64]{0,1:T(8,128)S(1)} %get-tuple-element.252), channel_id=1, source_target_pairs={{0,8},{8,16},{16,24},{1,9},{9,17},{17,25},{2,10},{10,18},{18,26},{... | collective-permute-start | bytes 196616 | tf_op jit(solution)/shard_map/while/body/eval_jaxpr/ppermute | solution.py:13
Sparse Core Ops, SparseCore 0:
  865.0 29.1 reduce-scatter.1
where the time goes:
time: 905 us; the launch traced here: 901 us
  blocking collectives  485 us (54%)
  starting transfers between devices  193 us (21%)
  matrix products  138 us (15%)
  waiting for transfers between devices  54.1 us (6%)
  other arithmetic  14.7 us (2%)
  between operations  13.4 us (1%)
    all_gather x19, blocking collectives, tick(): whole = lax.all_gather(own_cols, 'bond', axis=0, tiled=True)  485 us
    ppermute x19, starting transfers between devices, from_behind(): return lax.ppermute(x, axis, pairs)  193 us
    dot_general x19, matrix products, contract(): jnp.dot(matrix_pair[1], states, precision=lax.Precision.HIGHEST, preferre...  69 us
    dot_general x19, matrix products, contract(): jnp.dot(matrix_pair[0], states, precision=lax.Precision.HIGHEST, preferre...  68.9 us
    reduce_scatter x1, waiting for transfers between devices, local(): return lax.psum_scatter(finals, 'site', scatter_dimension=1, tiled=True)  29.3 us
    ppermute x19, waiting for transfers between devices, from_behind(): return lax.ppermute(x, axis, pairs)  24.8 us
  transfers between devices with their start and end apart: 20, of which 20 were waited for; matrix products, arithmetic and copies ran while one was open for 0% of the time, Pallas kernels for 0%

commit v1 on v0

v1 whole, which is shorter than its diff:
```python
import functools

import jax
import jax.numpy as jnp
from jax import lax
from jax.experimental import pallas as pl
from jax.experimental.pallas import tpu as pltpu
from jax.sharding import PartitionSpec as P


class Grid:
    def __init__(self, sites, bonds):
        self.sites, self.bonds = sites, bonds
        self.cores = 2 if sites % 2 == 0 else 1
        self.ny = sites // self.cores
        self.nx = max(q for q in range(1, bonds + 1) if bonds % q == 0 and q * q <= bonds)
        self.nz = bonds // self.nx

    def here(self):
        site, bond = lax.axis_index("site"), lax.axis_index("bond")
        return bond // self.nx, bond % self.nx, site // self.cores, site % self.cores

    def index(self, z, x, y, core):
        site = (y % self.ny) * self.cores + core % self.cores
        return site * self.bonds + (z % self.nz) * self.nx + x % self.nx

    def send(self, value, dz=0, dx=0, dy=0, dcore=0, cores=None, rows=None):
        pairs = []
        for z in range(self.nz):
            for x in range(self.nx):
                for y in range(self.ny) if rows is None else rows:
                    for core in range(self.cores) if cores is None else cores:
                        pairs.append((self.index(z, x, y, core), self.index(z + dz, x + dx, y + dy, core + dcore)))
        return lax.ppermute(value, ("site", "bond"), pairs)


def halves(value):
    high = value.astype(jnp.bfloat16)
    low = (value - high.astype(jnp.float32)).astype(jnp.bfloat16)
    return high, low


def dot3(a, b):
    dot = functools.partial(jnp.dot, preferred_element_type=jnp.float32)
    return dot(a[0], b[0]) + (dot(a[0], b[1]) + dot(a[1], b[0]))


def pack(grid, mats, rows, strip):
    z, x, y, _ = grid.here()
    outcomes = mats.shape[0]
    width = grid.nz * strip
    parts = []
    for dx in range(grid.nx):
        for dy in range(grid.ny):
            strips = []
            for d in range(grid.nz):
                start = ((z - d) % grid.nz) * grid.nx * rows + ((x + dx) % grid.nx) * rows + ((y + dy) % grid.ny) * strip
                strips.append(lax.dynamic_slice_in_dim(mats, start, strip, 2))
            parts.append(jnp.concatenate(strips, axis=2))
    return parts


def site_kernel(grid, site, last, strip, clicks_ref, *refs):
    nx, ny, nz = grid.nx, grid.ny, grid.nz
    mine, other, states = refs[:nx], refs[nx : 2 * nx], refs[2 * nx : 2 * nx + nz]
    outs = refs[2 * nx + nz : 2 * nx + nz + nx * ny]
    mat_ref, high_ref, low_ref, sems = refs[2 * nx + nz + nx * ny :]
    _, _, y, core = grid.here()
    owner = core == site % grid.cores
    for dx in range(nx):

        @pl.when(owner)
        def _():
            pltpu.make_async_copy(mine[dx], mat_ref.at[dx], sems.at[dx]).start()

        @pl.when(jnp.logical_not(owner))
        def _():
            pltpu.make_async_copy(other[dx], mat_ref.at[dx], sems.at[dx]).start()

    for d in range(nz):
        high, low = halves(states[d][...])
        high_ref[pl.ds(d * strip, strip), :] = high
        low_ref[pl.ds(d * strip, strip), :] = low
    chosen = clicks_ref[...] == 1
    rows = mat_ref.shape[2]
    cols = high_ref.shape[1] // ny
    for ex in range(nx):
        dx = (nx - ex) % nx
        pltpu.make_async_copy(mine[dx], mat_ref.at[dx], sems.at[dx]).wait()
        for ey in range(ny):
            to = lax.rem(y + ey, ny)
            out_ref = outs[ex * ny + ey]
            if last:
                picked = pl.ds(pl.multiple_of(to * cols, cols), cols)
                b = (high_ref[:, picked], low_ref[:, picked])
                for part in range(rows // strip):
                    at = pl.ds(part * strip, strip)
                    both = [dot3(halves(mat_ref[dx, o, at, :]), b) for o in range(2)]
                    out_ref[at, :] = jnp.where(clicks_ref[:, picked] == 1, both[1], both[0])
            else:
                at = pl.ds(pl.multiple_of(to * strip, strip), strip)
                b = (high_ref[...], low_ref[...])
                both = [dot3(halves(mat_ref[dx, o, at, :]), b) for o in range(2)]
                out_ref[...] = jnp.where(chosen, both[1], both[0])


def site_product(grid, site, last, clicks, mine, other, states):
    nx, ny, nz = grid.nx, grid.ny, grid.nz
    outcomes, rows, width = mine[0].shape
    strip, cols = states[0].shape
    shape = (rows, cols // ny) if last else (strip, cols)
    if strip % 128 == 0 and (cols // ny) % 128 == 0:
        vmem, hbm = pl.BlockSpec(memory_space=pltpu.VMEM), pl.BlockSpec(memory_space=pl.ANY)
        flops = 2 * 3 * outcomes * nx * rows * width * cols
        moved = 4 * (nx * outcomes * rows * width + width * cols + nx * rows * cols)
        return pl.pallas_call(
            functools.partial(site_kernel, grid, site, last, strip),
            out_shape=[jax.ShapeDtypeStruct(shape, jnp.float32)] * (nx * ny),
            in_specs=[vmem] + [hbm] * (2 * nx) + [vmem] * nz,
            out_specs=[vmem] * (nx * ny),
            scratch_shapes=[
                pltpu.VMEM((nx, outcomes, rows, width), jnp.float32),
                pltpu.VMEM((width, cols), jnp.bfloat16),
                pltpu.VMEM((width, cols), jnp.bfloat16),
                pltpu.SemaphoreType.DMA((nx,)),
            ],
            compiler_params=pltpu.CompilerParams(vmem_limit_bytes=32 * 1024 * 1024),
            cost_estimate=pl.CostEstimate(flops=flops, bytes_accessed=moved, transcendentals=0),
        )(clicks, *mine, *other, *states)
    _, _, y, core = grid.here()
    b = jnp.concatenate(states, axis=0)
    outs = []
    for ex in range(nx):
        dx = (nx - ex) % nx
        mat = jnp.where(core == site % grid.cores, mine[dx], other[dx])
        both = [jnp.dot(mat[o], b, precision=lax.Precision.HIGH, preferred_element_type=jnp.float32) for o in range(2)]
        picked = jnp.where(clicks == 1, both[1], both[0])
        for ey in range(ny):
            to = (y + ey) % ny
            if last:
                outs.append(lax.dynamic_slice_in_dim(picked, to * shape[1], shape[1], 1))
            else:
                outs.append(lax.dynamic_slice_in_dim(picked, to * shape[0], shape[0], 0))
    return outs


def local(left_start, site_mats, clicks):
    sites, bonds = lax.axis_size("site"), lax.axis_size("bond")
    grid = Grid(sites, bonds)
    nx, ny, nz, cores = grid.nx, grid.ny, grid.nz, grid.cores
    z, x, y, core = grid.here()
    rows = site_mats.shape[2]
    strip = rows // ny
    samples = left_start.shape[1]
    share = samples // sites

    def own_samples(value):
        blocks = [lax.dynamic_slice_in_dim(value, (yy * cores + core) * share, share, 1) for yy in range(ny)]
        return jnp.concatenate(blocks, axis=1)

    pieces = pack(grid, site_mats[0], rows, strip)

    def spread(which):
        got = {}
        for dx in range(nx):
            for dy in range(ny):
                piece = pieces[dx * ny + dy]
                got[dx, dy] = piece if dx == dy == 0 else grid.send(piece, dx=dx, dy=dy, cores=[which])
        return got

    def of_site(got, ys):
        mine = []
        for dx in range(nx):
            value = got[dx, 0]
            for dy in range(1, ny):
                value = jnp.where((y - ys) % ny == dy, got[dx, dy], value)
            mine.append(value)
        return mine

    state = own_samples(lax.dynamic_slice_in_dim(left_start, y * strip, strip, 0))
    gathered = [state] + [grid.send(state, dz=d) for d in range(1, nz)]
    own_clicks = {(0, 0): clicks}
    for dy in range(ny):
        for dcore in range(cores):
            if dy or dcore:
                own_clicks[dy, dcore] = grid.send(clicks, dy=dy, dcore=dcore)

    def clicks_of(site):
        value = own_clicks[0, 0]
        for (dy, dcore), got in own_clicks.items():
            hit = ((y - site // cores) % ny == dy) & ((core - site % cores) % cores == dcore)
            value = jnp.where(hit, got, value)
        return own_samples(value)

    spreads = [spread(which) for which in range(cores)]
    for site in range(sites):
        last = site == sites - 1
        which = site % cores
        mine = of_site(spreads[which], site // cores)
        other = [grid.send(value, dcore=1, cores=[which]) for value in mine]
        outs = site_product(grid, site, last, clicks_of(site), mine, other, gathered)
        state = outs[0]
        for ex in range(nx):
            for ey in range(ny):
                if ex or ey:
                    state = state + grid.send(outs[ex * ny + ey], dx=ex, dy=ey)
        if not last:
            gathered = [state] + [grid.send(state, dz=d) for d in range(1, nz)]
    return state


def solution(mesh):
    return jax.shard_map(
        local,
        mesh=mesh,
        in_specs=(P("bond", None), P("site", None, "bond", None), P("site", None)),
        out_specs=P("bond", "site"),
        check_vma=False,
    )
```

time: 905 us -> 229 us (0.25)
  the two profiles are of different devices: /device:TPU:25 before, /device:TPU:12 now
where the time goes in v1:
time: 229 us; the launch traced here: 228 us
  waiting for transfers between devices  153 us (67%)
  starting transfers between devices  53.6 us (23%)
  Pallas kernels  9.28 us (4%)
  other arithmetic  8.18 us (4%)
  local copies, waits for them, and re-layouts  3.67 us (2%)
    ppermute x41, waiting for transfers between devices, send(): return lax.ppermute(value, ('site', 'bond'), pairs)  153 us
    ppermute x41, starting transfers between devices, send(): return lax.ppermute(value, ('site', 'bond'), pairs)  53.6 us
    pallas_call x4, Pallas kernels, site_product(): pl.pallas_call(functools.partial(site_kernel, grid, site, last, strip), o...  9.28 us
  transfers between devices with their start and end apart: 41, of which 26 were waited for; matrix products, arithmetic and copies ran while one was open for 3% of the time, Pallas kernels for 3%

profile of v1, /device:TPU:12, one launch (start us, length us, event | category | flops | bytes accessed | tf_op | source)
XLA Modules:
  0.0 228.4 jit_solution(4162203653444341413)
XLA Ops:
  0.0 2.5 %dynamic-slice_bitcast_fusion.3 = (f32[2,256,128]{2,1,0:T(8,128)S(1)}, f32[2,256,128]{2,1,0:T(8,128)S(1)}, f32[2,256,128]{2,1,0:T(8,128)S(1)}, f32[2,256,128]{2,...) fusion(f32[1,2,256,2048]{3,2,1,0:T(8,128)} %param.4, ...), kind=kLoop, calls=%fused_computation.20 | loop fusion | bytes 8388672 | tf_op jit(solution)/shard_map/dynamic_slice | solution.py:58
  3.6 2.4 %collective-permute-start.8 = (f32[2,256,512]{2,1,0:T(8,128)}, f32[2,256,512]{2,1,0:T(8,128)}, u32[]{:S(2)}, u32[]{:S(2)}) collective-permute-start(f32[2,256,512]{2,1,0:T(8,128)} %pad_maximum_fusion), channel_id=1, source_target_pairs={{0,16},{16,0},{1,17},{17,1},{2,18},{18,2},{3,19},{19,3},{4,20},{20... | collective-permute-start | bytes 3145736 | tf_op jit(solution)/shard_map/ppermute | solution.py:34
  7.0 3.5 %collective-permute-start.10 = (f32[2,256,512]{2,1,0:T(8,128)}, f32[2,256,512]{2,1,0:T(8,128)}, u32[]{:S(2)}, u32[]{:S(2)}) collective-permute-start(f32[2,256,512]{2,1,0:T(8,128)} %pad_maximum_fusion.3), channel_id=1, source_target_pairs={{0,1},{16,17},{1,0},{17,16},{2,3},{18,19},{3,2},{19,18},{4,5},{20,... | collective-permute-start | bytes 3145736 | tf_op jit(solution)/shard_map/ppermute | solution.py:34
  11.6 3.4 %collective-permute-start.9 = (f32[2,256,512]{2,1,0:T(8,128)}, f32[2,256,512]{2,1,0:T(8,128)}, u32[]{:S(2)}, u32[]{:S(2)}) collective-permute-start(f32[2,256,512]{2,1,0:T(8,128)} %pad_maximum_fusion.2), channel_id=1, source_target_pairs={{0,17},{16,1},{1,16},{17,0},{2,19},{18,3},{3,18},{19,2},{4,21},{20... | collective-permute-start | bytes 3145736 | tf_op jit(solution)/shard_map/ppermute | solution.py:34
  17.7 2.8 %collective-permute-done.8 = f32[2,256,512]{2,1,0:T(8,128)} collective-permute-done((f32[2,256,512]{2,1,0:T(8,128)}, f32[2,256,512]{2,1,0:T(8,128)}, u32[]{:S(2)}, u32[]{:S(2)}) %collective-permute-start.8) | collective-permute-done | bytes 1048608 | tf_op jit(solution)/shard_map/ppermute | solution.py:34
  22.8 10.0 %collective-permute-done.10 = f32[2,256,512]{2,1,0:T(8,128)} collective-permute-done((f32[2,256,512]{2,1,0:T(8,128)}, f32[2,256,512]{2,1,0:T(8,128)}, u32[]{:S(2)}, u32[]{:S(2)}) %collective-permute-start.10) | collective-permute-done | bytes 1048608 | tf_op jit(solution)/shard_map/ppermute | solution.py:34
  32.9 24.5 %collective-permute-done.9 = f32[2,256,512]{2,1,0:T(8,128)} collective-permute-done((f32[2,256,512]{2,1,0:T(8,128)}, f32[2,256,512]{2,1,0:T(8,128)}, u32[]{:S(2)}, u32[]{:S(2)}) %collective-permute-start.9) | collective-permute-done | bytes 1048608 | tf_op jit(solution)/shard_map/ppermute | solution.py:34
  68.1 13.5 %collective-permute-done.17.refs_5_ = f32[128,512]{1,0:T(8,128)S(1)} collective-permute-done((f32[128,512]{1,0:T(8,128)S(1)}, f32[128,512]{1,0:T(8,128)S(1)}, u32[]{:S(2)}, u32[]{:S(2)}) %collective-permute-start.17) | collective-permute-done | bytes 262176 | tf_op jit(solution)/shard_map/ppermute | solution.py:34
  86.3 2.3 %shard_map.37 = (f32[128,512]{1,0:T(8,128)S(1)}, f32[128,512]{1,0:T(8,128)S(1)}, f32[128,512]{1,0:T(8,128)S(1)}, f32[128,512]{1,0:T(8,128)S(1)}) custom-call(s32[1,512]{1,0:T(1,128)S(1)} %pad_add_fusion.3.clicks_ref, f32[2,256,512]{2,1,0:T(8,128)S(1)} %get-tuple-element.55.refs_0_, f32[2,256,512]{2,1,0:T(8,128)S(1)} %get-tuple-element.53.refs_1_, ...), custom_call_target="tpu_custom_call" | custom-call | flops 1610612736 | bytes 4194304 | tf_op jit(solution)/shard_map/pallas_call | solution.py:116
  92.1 5.5 %collective-permute-done.20 = f32[128,512]{1,0:T(8,128)S(1)} collective-permute-done((f32[128,512]{1,0:T(8,128)S(1)}, f32[128,512]{1,0:T(8,128)S(1)}, u32[]{:S(2)}, u32[]{:S(2)}) %collective-permute-start.20) | collective-permute-done | bytes 262176 | tf_op jit(solution)/shard_map/ppermute | solution.py:34
  100.9 3.5 %collective-permute-done.22 = f32[128,512]{1,0:T(8,128)S(1)} collective-permute-done((f32[128,512]{1,0:T(8,128)S(1)}, f32[128,512]{1,0:T(8,128)S(1)}, u32[]{:S(2)}, u32[]{:S(2)}) %collective-permute-start.22) | collective-permute-done | bytes 262176 | tf_op jit(solution)/shard_map/ppermute | solution.py:34
  105.6 2.4 %collective-permute-start.24 = (f32[128,512]{1,0:T(8,128)S(1)}, f32[128,512]{1,0:T(8,128)S(1)}, u32[]{:S(2)}, u32[]{:S(2)}) collective-permute-start(f32[128,512]{1,0:T(8,128)S(1)} %add_add_fusion.3.refs_4_), channel_id=1, source_target_pairs={{0,4},{8,12},{16,20},{24,28},{1,5},{9,13},{17,21},{25,29},{2,6},{1... | collective-permute-start | bytes 786440 | tf_op jit(solution)/shard_map/ppermute | solution.py:34
  108.1 1.9 collective-permute-start.25
  110.0 13.4 %collective-permute-done.23.refs_5_ = f32[128,512]{1,0:T(8,128)S(1)} collective-permute-done((f32[128,512]{1,0:T(8,128)S(1)}, f32[128,512]{1,0:T(8,128)S(1)}, u32[]{:S(2)}, u32[]{:S(2)}) %collective-permute-start.23) | collective-permute-done | bytes 262176 | tf_op jit(solution)/shard_map/ppermute | solution.py:34
  123.4 4.9 %collective-permute-done.24.refs_6_ = f32[128,512]{1,0:T(8,128)S(1)} collective-permute-done((f32[128,512]{1,0:T(8,128)S(1)}, f32[128,512]{1,0:T(8,128)S(1)}, u32[]{:S(2)}, u32[]{:S(2)}) %collective-permute-start.24) | collective-permute-done | bytes 262176 | tf_op jit(solution)/shard_map/ppermute | solution.py:34
  128.3 3.1 %collective-permute-done.25.refs_7_ = f32[128,512]{1,0:T(8,128)S(1)} collective-permute-done((f32[128,512]{1,0:T(8,128)S(1)}, f32[128,512]{1,0:T(8,128)S(1)}, u32[]{:S(2)}, u32[]{:S(2)}) %collective-permute-start.25) | collective-permute-done | bytes 262176 | tf_op jit(solution)/shard_map/ppermute | solution.py:34
  131.4 2.3 %shard_map.38 = (f32[128,512]{1,0:T(8,128)S(1)}, f32[128,512]{1,0:T(8,128)S(1)}, f32[128,512]{1,0:T(8,128)S(1)}, f32[128,512]{1,0:T(8,128)S(1)}) custom-call(s32[1,512]{1,0:T(1,128)S(1)} %pad_add_fusion.2.clicks_ref, f32[2,256,512]{2,1,0:T(8,128)S(1)} %get-tuple-element.59.refs_0_, f32[2,256,512]{2,1,0:T(8,128)S(1)} %get-tuple-element.57.refs_1_, ...), custom_call_target="tpu_custom_call" | custom-call | flops 1610612736 | bytes 4194304 | tf_op jit(solution)/shard_map/pallas_call | solution.py:116
  137.3 4.8 %collective-permute-done.26 = f32[128,512]{1,0:T(8,128)S(1)} collective-permute-done((f32[128,512]{1,0:T(8,128)S(1)}, f32[128,512]{1,0:T(8,128)S(1)}, u32[]{:S(2)}, u32[]{:S(2)}) %collective-permute-start.26) | collective-permute-done | bytes 262176 | tf_op jit(solution)/shard_map/ppermute | solution.py:34
  143.4 5.4 %collective-permute-done.28 = f32[128,512]{1,0:T(8,128)S(1)} collective-permute-done((f32[128,512]{1,0:T(8,128)S(1)}, f32[128,512]{1,0:T(8,128)S(1)}, u32[]{:S(2)}, u32[]{:S(2)}) %collective-permute-start.28) | collective-permute-done | bytes 262176 | tf_op jit(solution)/shard_map/ppermute | solution.py:34
  149.0 1.9 collective-permute-start.31
  153.6 13.2 %collective-permute-done.29.refs_5_ = f32[128,512]{1,0:T(8,128)S(1)} collective-permute-done((f32[128,512]{1,0:T(8,128)S(1)}, f32[128,512]{1,0:T(8,128)S(1)}, u32[]{:S(2)}, u32[]{:S(2)}) %collective-permute-start.29) | collective-permute-done | bytes 262176 | tf_op jit(solution)/shard_map/ppermute | solution.py:34
  166.8 3.9 %collective-permute-done.30.refs_6_ = f32[128,512]{1,0:T(8,128)S(1)} collective-permute-done((f32[128,512]{1,0:T(8,128)S(1)}, f32[128,512]{1,0:T(8,128)S(1)}, u32[]{:S(2)}, u32[]{:S(2)}) %collective-permute-start.30) | collective-permute-done | bytes 262176 | tf_op jit(solution)/shard_map/ppermute | solution.py:34
  170.7 2.3 %shard_map.39 = (f32[128,512]{1,0:T(8,128)S(1)}, f32[128,512]{1,0:T(8,128)S(1)}, f32[128,512]{1,0:T(8,128)S(1)}, f32[128,512]{1,0:T(8,128)S(1)}) custom-call(s32[1,512]{1,0:T(1,128)S(1)} %pad_add_fusion.1.clicks_ref, f32[2,256,512]{2,1,0:T(8,128)S(1)} %get-tuple-element.56.refs_0_, f32[2,256,512]{2,1,0:T(8,128)S(1)} %get-tuple-element.54.refs_1_, ...), custom_call_target="tpu_custom_call" | custom-call | flops 1610612736 | bytes 4194304 | tf_op jit(solution)/shard_map/pallas_call | solution.py:116
  176.6 4.8 %collective-permute-done.32 = f32[128,512]{1,0:T(8,128)S(1)} collective-permute-done((f32[128,512]{1,0:T(8,128)S(1)}, f32[128,512]{1,0:T(8,128)S(1)}, u32[]{:S(2)}, u32[]{:S(2)}) %collective-permute-start.32) | collective-permute-done | bytes 262176 | tf_op jit(solution)/shard_map/ppermute | solution.py:34
  182.8 4.6 %collective-permute-done.34 = f32[128,512]{1,0:T(8,128)S(1)} collective-permute-done((f32[128,512]{1,0:T(8,128)S(1)}, f32[128,512]{1,0:T(8,128)S(1)}, u32[]{:S(2)}, u32[]{:S(2)}) %collective-permute-start.34) | collective-permute-done | bytes 262176 | tf_op jit(solution)/shard_map/ppermute | solution.py:34
  187.7 2.4 %collective-permute-start.36 = (f32[128,512]{1,0:T(8,128)S(1)}, f32[128,512]{1,0:T(8,128)S(1)}, u32[]{:S(2)}, u32[]{:S(2)}) collective-permute-start(f32[128,512]{1,0:T(8,128)S(1)} %add_add_fusion.1.refs_4_), channel_id=1, source_target_pairs={{0,4},{8,12},{16,20},{24,28},{1,5},{9,13},{17,21},{25,29},{2,6},{1... | collective-permute-start | bytes 786440 | tf_op jit(solution)/shard_map/ppermute | solution.py:34
  190.1 1.9 collective-permute-start.37
  192.1 13.6 %collective-permute-done.35.refs_5_ = f32[128,512]{1,0:T(8,128)S(1)} collective-permute-done((f32[128,512]{1,0:T(8,128)S(1)}, f32[128,512]{1,0:T(8,128)S(1)}, u32[]{:S(2)}, u32[]{:S(2)}) %collective-permute-start.35) | collective-permute-done | bytes 262176 | tf_op jit(solution)/shard_map/ppermute | solution.py:34
  205.7 3.0 %collective-permute-done.36.refs_6_ = f32[128,512]{1,0:T(8,128)S(1)} collective-permute-done((f32[128,512]{1,0:T(8,128)S(1)}, f32[128,512]{1,0:T(8,128)S(1)}, u32[]{:S(2)}, u32[]{:S(2)}) %collective-permute-start.36) | collective-permute-done | bytes 262176 | tf_op jit(solution)/shard_map/ppermute | solution.py:34
  210.1 2.4 %shard_map.40 = (f32[256,256]{1,0:T(8,128)S(1)}, f32[256,256]{1,0:T(8,128)S(1)}, f32[256,256]{1,0:T(8,128)S(1)}, f32[256,256]{1,0:T(8,128)S(1)}) custom-call(s32[1,512]{1,0:T(1,128)S(1)} %pad_add_fusion.clicks_ref, f32[2,256,512]{2,1,0:T(8,128)S(1)} %get-tuple-element.60.refs_0_, f32[2,256,512]{2,1,0:T(8,128)S(1)} %get-tuple-element.58.refs_1_, ...), custom_call_target="tpu_custom_call" | custom-call | flops 1610612736 | bytes 4194304 | tf_op jit(solution)/shard_map/pallas_call | solution.py:116
  216.0 4.8 %collective-permute-done.38 = f32[256,256]{1,0:T(8,128)S(1)} collective-permute-done((f32[256,256]{1,0:T(8,128)S(1)}, f32[256,256]{1,0:T(8,128)S(1)}, u32[]{:S(2)}, u32[]{:S(2)}) %collective-permute-start.38) | collective-permute-done | bytes 262176 | tf_op jit(solution)/shard_map/ppermute | solution.py:34
  222.2 5.4 %collective-permute-done.40 = f32[256,256]{1,0:T(8,128)S(1)} collective-permute-done((f32[256,256]{1,0:T(8,128)S(1)}, f32[256,256]{1,0:T(8,128)S(1)}, u32[]{:S(2)}, u32[]{:S(2)}) %collective-permute-start.40) | collective-permute-done | bytes 262176 | tf_op jit(solution)/shard_map/ppermute | solution.py:34
  (77 shorter events, 51.4 us)
Async XLA Ops:
  3.6 17.0 %collective-permute-start.8 = (f32[2,256,512]{2,1,0:T(8,128)}, f32[2,256,512]{2,1,0:T(8,128)}, u32[]{:S(2)}, u32[]{:S(2)}) collective-permute-start(f32[2,256,512]{2,1,0:T(8,128)} %pad_maximum_fusion), channel_id=1, source_target_pairs={{0,16},{16,0},{1,17},{17,1},{2,18},{18,2},{3,19},{19,3},{4,20},{20... | collective-permute-start | bytes 3145736 | tf_op jit(solution)/shard_map/ppermute | solution.py:34
  7.0 25.9 %collective-permute-start.10 = (f32[2,256,512]{2,1,0:T(8,128)}, f32[2,256,512]{2,1,0:T(8,128)}, u32[]{:S(2)}, u32[]{:S(2)}) collective-permute-start(f32[2,256,512]{2,1,0:T(8,128)} %pad_maximum_fusion.3), channel_id=1, source_target_pairs={{0,1},{16,17},{1,0},{17,16},{2,3},{18,19},{3,2},{19,18},{4,5},{20,... | collective-permute-start | bytes 3145736 | tf_op jit(solution)/shard_map/ppermute | solution.py:34
  11.6 45.8 %collective-permute-start.9 = (f32[2,256,512]{2,1,0:T(8,128)}, f32[2,256,512]{2,1,0:T(8,128)}, u32[]{:S(2)}, u32[]{:S(2)}) collective-permute-start(f32[2,256,512]{2,1,0:T(8,128)} %pad_maximum_fusion.2), channel_id=1, source_target_pairs={{0,17},{16,1},{1,16},{17,0},{2,19},{18,3},{3,18},{19,2},{4,21},{20... | collective-permute-start | bytes 3145736 | tf_op jit(solution)/shard_map/ppermute | solution.py:34
  15.0 44.2 %collective-permute-start.5 = (f32[2,256,512]{2,1,0:T(8,128)}, f32[2,256,512]{2,1,0:T(8,128)S(1)}, u32[]{:S(2)}, u32[]{:S(2)}) collective-permute-start(f32[2,256,512]{2,1,0:T(8,128)} %pad_maximum_fusion.3), channel_id=1, source_target_pairs={{8,9},{24,25},{9,8},{25,24},{10,11},{26,27},{11,10},{27,26},{12,13... | collective-permute-start | bytes 3145736 | tf_op jit(solution)/shard_map/ppermute | solution.py:34
  15.7 44.8 %collective-permute-start.4 = (f32[2,256,512]{2,1,0:T(8,128)}, f32[2,256,512]{2,1,0:T(8,128)S(1)}, u32[]{:S(2)}, u32[]{:S(2)}) collective-permute-start(f32[2,256,512]{2,1,0:T(8,128)} %pad_maximum_fusion.2), channel_id=1, source_target_pairs={{8,25},{24,9},{9,24},{25,8},{10,27},{26,11},{11,26},{27,10},{12,29... | collective-permute-start | bytes 3145736 | tf_op jit(solution)/shard_map/ppermute | solution.py:34
  20.5 44.9 %collective-permute-start.3 = (f32[2,256,512]{2,1,0:T(8,128)}, f32[2,256,512]{2,1,0:T(8,128)S(1)}, u32[]{:S(2)}, u32[]{:S(2)}) collective-permute-start(f32[2,256,512]{2,1,0:T(8,128)} %pad_maximum_fusion), channel_id=1, source_target_pairs={{8,24},{24,8},{9,25},{25,9},{10,26},{26,10},{11,27},{27,11},{12,28... | collective-permute-start | bytes 3145736 | tf_op jit(solution)/shard_map/ppermute | solution.py:34
  32.9 29.4 %collective-permute-start = (s32[1,1024]{1,0:T(1,128)S(1)}, s32[1,1024]{1,0:T(1,128)S(1)}, u32[]{:S(2)}, u32[]{:S(2)}) collective-permute-start(s32[1,1024]{1,0:T(1,128)S(1)} %copy-done), channel_id=1, source_target_pairs={{0,24},{8,16},{16,8},{24,0},{1,25},{9,17},{17,9},{25,1},{2,26},{10... | collective-permute-start | bytes 12296 | tf_op jit(solution)/shard_map/ppermute | solution.py:34
  59.2 27.1 %collective-permute-start.16 = (f32[2,256,512]{2,1,0:T(8,128)S(1)}, f32[2,256,512]{2,1,0:T(8,128)S(1)}, u32[]{:S(2)}, u32[]{:S(2)}) collective-permute-start(f32[2,256,512]{2,1,0:T(8,128)S(1)} %get-tuple-element.53.refs_1_), channel_id=1, source_target_pairs={{0,8},{16,24},{1,9},{17,25},{2,10},{18,26},{3,11},{19,27},{4,12},{... | collective-permute-start | bytes 3145736 | tf_op jit(solution)/shard_map/ppermute | solution.py:34
  60.5 25.7 %collective-permute-start.15 = (f32[2,256,512]{2,1,0:T(8,128)S(1)}, f32[2,256,512]{2,1,0:T(8,128)S(1)}, u32[]{:S(2)}, u32[]{:S(2)}) collective-permute-start(f32[2,256,512]{2,1,0:T(8,128)S(1)} %get-tuple-element.55.refs_0_), channel_id=1, source_target_pairs={{0,8},{16,24},{1,9},{17,25},{2,10},{18,26},{3,11},{19,27},{4,12},{... | collective-permute-start | bytes 3145736 | tf_op jit(solution)/shard_map/ppermute | solution.py:34
  62.3 19.4 %collective-permute-start.17 = (f32[128,512]{1,0:T(8,128)S(1)}, f32[128,512]{1,0:T(8,128)S(1)}, u32[]{:S(2)}, u32[]{:S(2)}) collective-permute-start(f32[128,512]{1,0:T(8,128)S(1)} %pad_maximum_fusion.4.refs_4_), channel_id=1, source_target_pairs={{0,2},{8,10},{16,18},{24,26},{1,3},{9,11},{17,19},{25,27},{2,4},{1... | collective-permute-start | bytes 786440 | tf_op jit(solution)/shard_map/ppermute | solution.py:34
  63.9 20.5 %collective-permute-start.18 = (f32[128,512]{1,0:T(8,128)S(1)}, f32[128,512]{1,0:T(8,128)S(1)}, u32[]{:S(2)}, u32[]{:S(2)}) collective-permute-start(f32[128,512]{1,0:T(8,128)S(1)} %pad_maximum_fusion.4.refs_4_), channel_id=1, source_target_pairs={{0,4},{8,12},{16,20},{24,28},{1,5},{9,13},{17,21},{25,29},{2,6},{1... | collective-permute-start | bytes 786440 | tf_op jit(solution)/shard_map/ppermute | solution.py:34
  66.6 19.6 %collective-permute-start.19 = (f32[128,512]{1,0:T(8,128)S(1)}, f32[128,512]{1,0:T(8,128)S(1)}, u32[]{:S(2)}, u32[]{:S(2)}) collective-permute-start(f32[128,512]{1,0:T(8,128)S(1)} %pad_maximum_fusion.4.refs_4_), channel_id=1, source_target_pairs={{0,6},{8,14},{16,22},{24,30},{1,7},{9,15},{17,23},{25,31},{2,0},{1... | collective-permute-start | bytes 786440 | tf_op jit(solution)/shard_map/ppermute | solution.py:34
  81.7 24.0 %collective-permute-start.14 = (f32[2,256,512]{2,1,0:T(8,128)S(1)}, f32[2,256,512]{2,1,0:T(8,128)S(1)}, u32[]{:S(2)}, u32[]{:S(2)}) collective-permute-start(f32[2,256,512]{2,1,0:T(8,128)S(1)} %get-tuple-element.57.refs_1_), channel_id=1, source_target_pairs={{8,0},{24,16},{9,1},{25,17},{10,2},{26,18},{11,3},{27,19},{12,4},{... | collective-permute-start | bytes 3145736 | tf_op jit(solution)/shard_map/ppermute | solution.py:34
  84.5 23.6 %collective-permute-start.13 = (f32[2,256,512]{2,1,0:T(8,128)S(1)}, f32[2,256,512]{2,1,0:T(8,128)S(1)}, u32[]{:S(2)}, u32[]{:S(2)}) collective-permute-start(f32[2,256,512]{2,1,0:T(8,128)S(1)} %get-tuple-element.59.refs_0_), channel_id=1, source_target_pairs={{8,0},{24,16},{9,1},{25,17},{10,2},{26,18},{11,3},{27,19},{12,4},{... | collective-permute-start | bytes 3145736 | tf_op jit(solution)/shard_map/ppermute | solution.py:34
  89.1 10.4 %collective-permute-start.21 = (f32[128,512]{1,0:T(8,128)S(1)}, f32[128,512]{1,0:T(8,128)S(1)}, u32[]{:S(2)}, u32[]{:S(2)}) collective-permute-start(f32[128,512]{1,0:T(8,128)S(1)} %get-tuple-element.23), channel_id=1, source_target_pairs={{0,1},{8,9},{16,17},{24,25},{1,0},{9,8},{17,16},{25,24},{2,3},{10,... | collective-permute-start | bytes 786440 | tf_op jit(solution)/shard_map/ppermute | solution.py:34
  90.6 13.8 %collective-permute-start.22 = (f32[128,512]{1,0:T(8,128)S(1)}, f32[128,512]{1,0:T(8,128)S(1)}, u32[]{:S(2)}, u32[]{:S(2)}) collective-permute-start(f32[128,512]{1,0:T(8,128)S(1)} %get-tuple-element.24), channel_id=1, source_target_pairs={{0,17},{8,25},{16,1},{24,9},{1,16},{9,24},{17,0},{25,8},{2,19},{10... | collective-permute-start | bytes 786440 | tf_op jit(solution)/shard_map/ppermute | solution.py:34
  97.6 53.3 %collective-permute-start.12 = (f32[2,256,512]{2,1,0:T(8,128)S(1)}, f32[2,256,512]{2,1,0:T(8,128)S(1)}, u32[]{:S(2)}, u32[]{:S(2)}) collective-permute-start(f32[2,256,512]{2,1,0:T(8,128)S(1)} %get-tuple-element.54.refs_1_), channel_id=1, source_target_pairs={{0,8},{16,24},{1,9},{17,25},{2,10},{18,26},{3,11},{19,27},{4,12},{... | collective-permute-start | bytes 3145736 | tf_op jit(solution)/shard_map/ppermute | solution.py:34
  99.6 52.7 %collective-permute-start.11 = (f32[2,256,512]{2,1,0:T(8,128)S(1)}, f32[2,256,512]{2,1,0:T(8,128)S(1)}, u32[]{:S(2)}, u32[]{:S(2)}) collective-permute-start(f32[2,256,512]{2,1,0:T(8,128)S(1)} %get-tuple-element.56.refs_0_), channel_id=1, source_target_pairs={{0,8},{16,24},{1,9},{17,25},{2,10},{18,26},{3,11},{19,27},{4,12},{... | collective-permute-start | bytes 3145736 | tf_op jit(solution)/shard_map/ppermute | solution.py:34
  104.5 18.9 %collective-permute-start.23 = (f32[128,512]{1,0:T(8,128)S(1)}, f32[128,512]{1,0:T(8,128)S(1)}, u32[]{:S(2)}, u32[]{:S(2)}) collective-permute-start(f32[128,512]{1,0:T(8,128)S(1)} %add_add_fusion.3.refs_4_), channel_id=1, source_target_pairs={{0,2},{8,10},{16,18},{24,26},{1,3},{9,11},{17,19},{25,27},{2,4},{1... | collective-permute-start | bytes 786440 | tf_op jit(solution)/shard_map/ppermute | solution.py:34
  105.6 22.7 %collective-permute-start.24 = (f32[128,512]{1,0:T(8,128)S(1)}, f32[128,512]{1,0:T(8,128)S(1)}, u32[]{:S(2)}, u32[]{:S(2)}) collective-permute-start(f32[128,512]{1,0:T(8,128)S(1)} %add_add_fusion.3.refs_4_), channel_id=1, source_target_pairs={{0,4},{8,12},{16,20},{24,28},{1,5},{9,13},{17,21},{25,29},{2,6},{1... | collective-permute-start | bytes 786440 | tf_op jit(solution)/shard_map/ppermute | solution.py:34
  108.1 23.3 %collective-permute-start.25 = (f32[128,512]{1,0:T(8,128)S(1)}, f32[128,512]{1,0:T(8,128)S(1)}, u32[]{:S(2)}, u32[]{:S(2)}) collective-permute-start(f32[128,512]{1,0:T(8,128)S(1)} %add_add_fusion.3.refs_4_), channel_id=1, source_target_pairs={{0,6},{8,14},{16,22},{24,30},{1,7},{9,15},{17,23},{25,31},{2,0},{1... | collective-permute-start | bytes 786440 | tf_op jit(solution)/shard_map/ppermute | solution.py:34
  135.7 13.1 %collective-permute-start.28 = (f32[128,512]{1,0:T(8,128)S(1)}, f32[128,512]{1,0:T(8,128)S(1)}, u32[]{:S(2)}, u32[]{:S(2)}) collective-permute-start(f32[128,512]{1,0:T(8,128)S(1)} %get-tuple-element.28), channel_id=1, source_target_pairs={{0,17},{8,25},{16,1},{24,9},{1,16},{9,24},{17,0},{25,8},{2,19},{10... | collective-permute-start | bytes 786440 | tf_op jit(solution)/shard_map/ppermute | solution.py:34
  148.9 17.9 %collective-permute-start.29 = (f32[128,512]{1,0:T(8,128)S(1)}, f32[128,512]{1,0:T(8,128)S(1)}, u32[]{:S(2)}, u32[]{:S(2)}) collective-permute-start(f32[128,512]{1,0:T(8,128)S(1)} %add_add_fusion.2.refs_4_), channel_id=1, source_target_pairs={{0,2},{8,10},{16,18},{24,26},{1,3},{9,11},{17,19},{25,27},{2,4},{1... | collective-permute-start | bytes 786440 | tf_op jit(solution)/shard_map/ppermute | solution.py:34
  149.0 21.7 %collective-permute-start.30 = (f32[128,512]{1,0:T(8,128)S(1)}, f32[128,512]{1,0:T(8,128)S(1)}, u32[]{:S(2)}, u32[]{:S(2)}) collective-permute-start(f32[128,512]{1,0:T(8,128)S(1)} %add_add_fusion.2.refs_4_), channel_id=1, source_target_pairs={{0,4},{8,12},{16,20},{24,28},{1,5},{9,13},{17,21},{25,29},{2,6},{1... | collective-permute-start | bytes 786440 | tf_op jit(solution)/shard_map/ppermute | solution.py:34
  149.0 21.7 %collective-permute-start.31 = (f32[128,512]{1,0:T(8,128)S(1)}, f32[128,512]{1,0:T(8,128)S(1)}, u32[]{:S(2)}, u32[]{:S(2)}) collective-permute-start(f32[128,512]{1,0:T(8,128)S(1)} %add_add_fusion.2.refs_4_), channel_id=1, source_target_pairs={{0,6},{8,14},{16,22},{24,30},{1,7},{9,15},{17,23},{25,31},{2,0},{1... | collective-permute-start | bytes 786440 | tf_op jit(solution)/shard_map/ppermute | solution.py:34
  151.0 41.1 %collective-permute-start.7 = (f32[2,256,512]{2,1,0:T(8,128)S(1)}, f32[2,256,512]{2,1,0:T(8,128)S(1)}, u32[]{:S(2)}, u32[]{:S(2)}) collective-permute-start(f32[2,256,512]{2,1,0:T(8,128)S(1)} %get-tuple-element.58.refs_1_), channel_id=1, source_target_pairs={{8,0},{24,16},{9,1},{25,17},{10,2},{26,18},{11,3},{27,19},{12,4},{... | collective-permute-start | bytes 3145736 | tf_op jit(solution)/shard_map/ppermute | solution.py:34
  152.3 39.8 %collective-permute-start.6 = (f32[2,256,512]{2,1,0:T(8,128)S(1)}, f32[2,256,512]{2,1,0:T(8,128)S(1)}, u32[]{:S(2)}, u32[]{:S(2)}) collective-permute-start(f32[2,256,512]{2,1,0:T(8,128)S(1)} %get-tuple-element.60.refs_0_), channel_id=1, source_target_pairs={{8,0},{24,16},{9,1},{25,17},{10,2},{26,18},{11,3},{27,19},{12,4},{... | collective-permute-start | bytes 3145736 | tf_op jit(solution)/shard_map/ppermute | solution.py:34
  175.0 12.3 %collective-permute-start.34 = (f32[128,512]{1,0:T(8,128)S(1)}, f32[128,512]{1,0:T(8,128)S(1)}, u32[]{:S(2)}, u32[]{:S(2)}) collective-permute-start(f32[128,512]{1,0:T(8,128)S(1)} %get-tuple-element.32), channel_id=1, source_target_pairs={{0,17},{8,25},{16,1},{24,9},{1,16},{9,24},{17,0},{25,8},{2,19},{10... | collective-permute-start | bytes 786440 | tf_op jit(solution)/shard_map/ppermute | solution.py:34
  187.4 18.2 %collective-permute-start.35 = (f32[128,512]{1,0:T(8,128)S(1)}, f32[128,512]{1,0:T(8,128)S(1)}, u32[]{:S(2)}, u32[]{:S(2)}) collective-permute-start(f32[128,512]{1,0:T(8,128)S(1)} %add_add_fusion.1.refs_4_), channel_id=1, source_target_pairs={{0,2},{8,10},{16,18},{24,26},{1,3},{9,11},{17,19},{25,27},{2,4},{1... | collective-permute-start | bytes 786440 | tf_op jit(solution)/shard_map/ppermute | solution.py:34
  187.7 21.0 %collective-permute-start.36 = (f32[128,512]{1,0:T(8,128)S(1)}, f32[128,512]{1,0:T(8,128)S(1)}, u32[]{:S(2)}, u32[]{:S(2)}) collective-permute-start(f32[128,512]{1,0:T(8,128)S(1)} %add_add_fusion.1.refs_4_), channel_id=1, source_target_pairs={{0,4},{8,12},{16,20},{24,28},{1,5},{9,13},{17,21},{25,29},{2,6},{1... | collective-permute-start | bytes 786440 | tf_op jit(solution)/shard_map/ppermute | solution.py:34
  190.1 20.0 %collective-permute-start.37 = (f32[128,512]{1,0:T(8,128)S(1)}, f32[128,512]{1,0:T(8,128)S(1)}, u32[]{:S(2)}, u32[]{:S(2)}) collective-permute-start(f32[128,512]{1,0:T(8,128)S(1)} %add_add_fusion.1.refs_4_), channel_id=1, source_target_pairs={{0,6},{8,14},{16,22},{24,30},{1,7},{9,15},{17,23},{25,31},{2,0},{1... | collective-permute-start | bytes 786440 | tf_op jit(solution)/shard_map/ppermute | solution.py:34
  214.5 13.1 %collective-permute-start.40 = (f32[256,256]{1,0:T(8,128)S(1)}, f32[256,256]{1,0:T(8,128)S(1)}, u32[]{:S(2)}, u32[]{:S(2)}) collective-permute-start(f32[256,256]{1,0:T(8,128)S(1)} %get-tuple-element.36), channel_id=1, source_target_pairs={{0,17},{8,25},{16,1},{24,9},{1,16},{9,24},{17,0},{25,8},{2,19},{10... | collective-permute-start | bytes 786440 | tf_op jit(solution)/shard_map/ppermute | solution.py:34
  (10 other events, 95.4 us)

commit v2 on v0

v2 whole, which is shorter than its diff:
```python
import functools

import jax
import jax.numpy as jnp
from jax import lax
from jax.experimental import pallas as pl
from jax.experimental.pallas import tpu as pltpu
from jax.sharding import PartitionSpec as P


CLICK_ROWS = 8


class Grid:
    def __init__(self, sites, bonds, rows, samples):
        self.sites, self.bonds = sites, bonds
        self.cores = 2 if sites % 2 == 0 else 1
        self.ny = sites // self.cores
        self.nx = max(q for q in range(1, bonds + 1) if bonds % q == 0 and q * q <= bonds)
        self.nz = bonds // self.nx
        self.rows = rows
        self.strip = rows // self.ny
        self.width = self.strip * self.nz
        self.share = samples // sites
        self.cols = self.share * self.ny
        aligned = self.strip % 128 == 0 and self.share % 128 == 0
        self.kernels = aligned and self.cols == self.width and self.cores <= CLICK_ROWS

    def here(self):
        site, bond = lax.axis_index("site"), lax.axis_index("bond")
        return bond // self.nx, bond % self.nx, site // self.cores, site % self.cores

    def index(self, z, x, y, core):
        site = (y % self.ny) * self.cores + core % self.cores
        return site * self.bonds + (z % self.nz) * self.nx + x % self.nx

    def send(self, value, dz=0, dx=0, dy=0, dcore=0, across=0, cores=None):
        pairs = []
        for z in range(self.nz):
            for x in range(self.nx):
                for y in range(self.ny):
                    for core in range(self.cores) if cores is None else cores:
                        to = self.index((z ^ across) + dz, x + dx, y + dy, core + dcore)
                        pairs.append((self.index(z, x, y, core), to))
        return lax.ppermute(value, ("site", "bond"), pairs)

    def gather(self, state, relay=False):
        if self.nz & (self.nz - 1):
            return [state] + [self.send(state, dz=self.nz - d) for d in range(1, self.nz)]
        got = [state]
        for d in range(1, self.nz):
            got.append(self.send(got[d ^ 1], across=1) if relay and d & 1 else self.send(state, across=d))
        return got

    def gathered_from(self, z):
        if self.nz & (self.nz - 1):
            return [lax.rem(z + d, self.nz) for d in range(self.nz)]
        return [z ^ d for d in range(self.nz)]


def halves(value):
    high = value.astype(jnp.bfloat16)
    low = (value - high.astype(jnp.float32)).astype(jnp.bfloat16)
    return high, low


def dot3(a, b):
    dot = functools.partial(jnp.dot, preferred_element_type=jnp.float32)
    return dot(a[0], b[0]) + (dot(a[0], b[1]) + dot(a[1], b[0]))


def pack_kernel(grid, clicks_ref, mats_ref, left_ref, *refs):
    nx, ny, nz, cores, rows, strip, share = grid.nx, grid.ny, grid.nz, grid.cores, grid.rows, grid.strip, grid.share
    piece_refs, state_ref = refs[: nx * ny], refs[nx * ny]
    clicks_held_ref, held_ref, left_held_ref, clicks_sem, in_sems, out_sems, left_sems, state_sem = refs[nx * ny + 1 :]
    _, x, y, core = grid.here()
    clicks_copy = pltpu.make_async_copy(clicks_ref, clicks_held_ref, clicks_sem)
    clicks_copy.start()
    order = [(dx, dy) for dx in reversed(range(nx)) for dy in reversed(range(ny))]
    into = {}
    for dx, dy in order:
        e = dx * ny + dy
        into[e] = []
        for zz in range(nz):
            start = zz * nx * rows + lax.rem(x + dx, nx) * rows + lax.rem(y + dy, ny) * strip
            columns = pl.ds(pl.multiple_of(start, strip), strip)
            for o in range(2):
                target = held_ref.at[e, pl.ds(o * rows, rows), pl.ds(zz * strip, strip)]
                into[e].append(pltpu.make_async_copy(mats_ref.at[o, :, columns], target, in_sems.at[e, zz, o]))
        for copy in into[e]:
            copy.start()
    states = []
    for yy in range(ny):
        start = pl.multiple_of((yy * cores + core) * share, share)
        source = left_ref.at[pl.ds(pl.multiple_of(y * strip, strip), strip), pl.ds(start, share)]
        states.append(pltpu.make_async_copy(source, left_held_ref.at[:, pl.ds(yy * share, share)], left_sems.at[yy]))
    for copy in states:
        copy.start()
    clicks_copy.wait()
    for e in range(nx * ny):
        held_ref[e, 2 * rows :, :] = jnp.zeros((CLICK_ROWS, grid.width), jnp.float32)
        for c in range(cores):
            for yy in range(ny):
                start = (yy * cores + c) * share
                value = clicks_held_ref[:, start : start + share].astype(jnp.float32)
                held_ref[e, 2 * rows + c : 2 * rows + c + 1, yy * share : (yy + 1) * share] = value
    outward = []
    for dx, dy in order:
        e = dx * ny + dy
        for copy in into[e]:
            copy.wait()
        outward.append(pltpu.make_async_copy(held_ref.at[e], piece_refs[e], out_sems.at[e]))
        outward[-1].start()
    for copy in states:
        copy.wait()
    outward.append(pltpu.make_async_copy(left_held_ref, state_ref, state_sem))
    outward[-1].start()
    for copy in outward:
        copy.wait()


def own_samples(grid, value):
    core = grid.here()[3]
    starts = [(yy * grid.cores + core) * grid.share for yy in range(grid.ny)]
    return jnp.concatenate([lax.dynamic_slice_in_dim(value, start, grid.share, 1) for start in starts], axis=1)


def pack(grid, clicks, mats, left):
    nx, ny, nz, rows, strip = grid.nx, grid.ny, grid.nz, grid.rows, grid.strip
    if grid.kernels:
        hbm = pl.BlockSpec(memory_space=pltpu.HBM)
        tall = 2 * rows + CLICK_ROWS
        out = pl.pallas_call(
            functools.partial(pack_kernel, grid),
            out_shape=[jax.ShapeDtypeStruct((tall, grid.width), jnp.float32)] * (nx * ny)
            + [jax.ShapeDtypeStruct((strip, grid.cols), jnp.float32)],
            in_specs=[hbm] * 3,
            out_specs=[hbm] * (nx * ny + 1),
            scratch_shapes=[
                pltpu.VMEM(clicks.shape, jnp.int32),
                pltpu.VMEM((nx * ny, tall, grid.width), jnp.float32),
                pltpu.VMEM((strip, grid.cols), jnp.float32),
                pltpu.SemaphoreType.DMA,
                pltpu.SemaphoreType.DMA((nx * ny, nz, 2)),
                pltpu.SemaphoreType.DMA((nx * ny,)),
                pltpu.SemaphoreType.DMA((ny,)),
                pltpu.SemaphoreType.DMA,
            ],
            compiler_params=pltpu.CompilerParams(vmem_limit_bytes=57 * 1024 * 1024),
            cost_estimate=pl.CostEstimate(flops=0, bytes_accessed=2 * mats.size * 4, transcendentals=0),
        )(clicks, mats, left)
        return out[: nx * ny], out[nx * ny]
    _, x, y, _ = grid.here()
    pieces = []
    for dx in range(nx):
        for dy in range(ny):
            strips = []
            for zz in range(nz):
                start = zz * nx * rows + ((x + dx) % nx) * rows + ((y + dy) % ny) * strip
                strips.append(lax.dynamic_slice_in_dim(mats, start, strip, 2))
            pieces.append(jnp.concatenate(strips, axis=2).reshape(2 * rows, grid.width))
    return pieces, own_samples(grid, lax.dynamic_slice_in_dim(left, y * strip, strip, 0))


def collect_kernel(grid, site, keys, *refs):
    n = len(keys)
    pieces, (out_ref, held_ref, in_sems, out_sems) = dict(zip(keys, refs[:n])), refs[-4:]
    y = grid.here()[2]
    behind = lax.rem(y + grid.ny - site // grid.cores, grid.ny)
    for dx, dy in keys:

        @pl.when(behind == dy)
        def _():
            pltpu.make_async_copy(pieces[dx, dy], held_ref.at[dx], in_sems.at[dx]).start()

    outward = []
    for dx in range(grid.nx):
        pltpu.make_async_copy(pieces[dx, 0], held_ref.at[dx], in_sems.at[dx]).wait()
        outward.append(pltpu.make_async_copy(held_ref.at[dx], out_ref.at[dx], out_sems.at[dx]))
        outward[-1].start()
    for copy in outward:
        copy.wait()


def collect(grid, site, pieces, token):
    nx = grid.nx
    tall, width = pieces[0, 0].shape
    if grid.kernels:
        hbm, fixed = pl.BlockSpec(memory_space=pl.ANY), pl.BlockSpec(memory_space=pltpu.HBM)
        return pl.pallas_call(
            functools.partial(collect_kernel, grid, site, tuple(pieces)),
            out_shape=jax.ShapeDtypeStruct((nx, tall, width), jnp.float32),
            in_specs=[fixed if key == (0, 0) else hbm for key in pieces] + [hbm] * len(token),
            out_specs=hbm,
            scratch_shapes=[
                pltpu.VMEM((nx, tall, width), jnp.float32),
                pltpu.SemaphoreType.DMA((nx,)),
                pltpu.SemaphoreType.DMA((nx,)),
            ],
            compiler_params=pltpu.CompilerParams(vmem_limit_bytes=32 * 1024 * 1024),
            cost_estimate=pl.CostEstimate(flops=0, bytes_accessed=8 * nx * tall * width, transcendentals=0),
        )(*pieces.values(), *token)
    behind = (grid.here()[2] - site // grid.cores) % grid.ny
    rows = []
    for dx in range(nx):
        value = pieces[dx, 0]
        for dy in range(1, grid.ny):
            value = jnp.where(behind == dy, pieces[dx, dy], value)
        rows.append(value)
    return jnp.stack(rows)


def site_kernel(grid, site, last, tokens, mine_ref, other_ref, *refs):
    nx, ny, nz, rows, strip, share = grid.nx, grid.ny, grid.nz, grid.rows, grid.strip, grid.share
    states, refs = refs[:nz], refs[nz + tokens :]
    outs = refs[: nx * ny]
    mat_ref, state_ref, high_ref, low_ref, sems, state_sems = refs[nx * ny :]
    z, _, y, core = grid.here()
    owner = core == site % grid.cores
    inward = []
    for n, source in enumerate(grid.gathered_from(z)):
        at = pl.ds(pl.multiple_of(source * strip, strip), strip)
        inward.append(pltpu.make_async_copy(states[n], state_ref.at[at], state_sems.at[n]))
        inward[-1].start()

    @pl.when(owner)
    def _():
        for dx in range(nx):
            pltpu.make_async_copy(mine_ref.at[dx], mat_ref.at[dx], sems.at[dx]).start()

    @pl.when(jnp.logical_not(owner))
    def _():
        for dx in range(nx):
            pltpu.make_async_copy(other_ref.at[dx], mat_ref.at[dx], sems.at[dx]).start()

    for copy in inward:
        copy.wait()
    high_ref[...], low_ref[...] = halves(state_ref[...])
    for ex in range(nx):
        dx = (nx - ex) % nx
        pltpu.make_async_copy(mine_ref.at[dx], mat_ref.at[dx], sems.at[dx]).wait()
        if ex == 0:
            clicks = mat_ref[0, 2 * rows : 2 * rows + CLICK_ROWS, :]
            row = lax.broadcasted_iota(jnp.int32, clicks.shape, 0)
            clicks = jnp.sum(jnp.where(row == core, clicks, 0.0), axis=0, keepdims=True)
        for ey in range(ny):
            to = lax.rem(y + ey, ny)
            out_ref = outs[ex * ny + ey]
            if last:
                columns = pl.ds(pl.multiple_of(to * share, share), share)
                b = (high_ref[:, columns], low_ref[:, columns])
                picked = jnp.zeros((1, share), jnp.float32)
                for yy in range(ny):
                    picked = jnp.where(to == yy, clicks[:, yy * share : (yy + 1) * share], picked)
                both = [dot3(halves(mat_ref[dx, o * rows : (o + 1) * rows, :]), b) for o in range(2)]
                out_ref[...] = jnp.where(picked == 1, both[1], both[0])
            else:
                at = pl.multiple_of(to * strip, strip)
                b = (high_ref[...], low_ref[...])
                both = [dot3(halves(mat_ref[dx, pl.ds(o * rows + at, strip), :]), b) for o in range(2)]
                out_ref[...] = jnp.where(clicks == 1, both[1], both[0])


def site_product(grid, site, clicks, mine, other, states, token=()):
    nx, ny, nz, rows, width, cols = grid.nx, grid.ny, grid.nz, grid.rows, grid.width, grid.cols
    last = site == grid.sites - 1
    shape = (rows, grid.share) if last else (grid.strip, cols)
    if grid.kernels:
        vmem, hbm = pl.BlockSpec(memory_space=pltpu.VMEM), pl.BlockSpec(memory_space=pl.ANY)
        fixed = pl.BlockSpec(memory_space=pltpu.HBM)
        tall = mine.shape[1]
        flops = 2 * 3 * 2 * nx * rows * width * cols
        moved = 4 * (nx * tall * width + width * cols + nx * rows * cols)
        return pl.pallas_call(
            functools.partial(site_kernel, grid, site, last, len(token)),
            out_shape=[jax.ShapeDtypeStruct(shape, jnp.float32)] * (nx * ny),
            in_specs=[hbm] * 2 + [fixed if site == 0 else hbm] + [hbm] * (nz - 1 + len(token)),
            out_specs=[vmem] * (nx * ny),
            scratch_shapes=[
                pltpu.VMEM((nx, tall, width), jnp.float32),
                pltpu.VMEM((width, cols), jnp.float32),
                pltpu.VMEM((width, cols), jnp.bfloat16),
                pltpu.VMEM((width, cols), jnp.bfloat16),
                pltpu.SemaphoreType.DMA((nx,)),
                pltpu.SemaphoreType.DMA((nz,)),
            ],
            compiler_params=pltpu.CompilerParams(vmem_limit_bytes=32 * 1024 * 1024),
            cost_estimate=pl.CostEstimate(flops=flops, bytes_accessed=moved, transcendentals=0),
        )(mine, other, *states, *token)
    z, _, y, core = grid.here()
    whole = jnp.zeros((width, cols), jnp.float32)
    for value, source in zip(states, grid.gathered_from(z)):
        whole = lax.dynamic_update_slice_in_dim(whole, value, source * grid.strip, 0)
    outs = []
    for ex in range(nx):
        dx = (nx - ex) % nx
        mat = jnp.where(core == site % grid.cores, mine[dx], other[dx])
        both = jnp.dot(mat, whole, precision=lax.Precision.HIGH, preferred_element_type=jnp.float32)
        picked = jnp.where(clicks == 1, both[rows:], both[:rows])
        for ey in range(ny):
            axis = 1 if last else 0
            outs.append(lax.dynamic_slice_in_dim(picked, ((y + ey) % ny) * shape[axis], shape[axis], axis))
    return outs


def local(left_start, site_mats, clicks):
    sites, bonds = lax.axis_size("site"), lax.axis_size("bond")
    grid = Grid(sites, bonds, site_mats.shape[2], left_start.shape[1])
    nx, ny, nz, cores = grid.nx, grid.ny, grid.nz, grid.cores
    _, _, y, core = grid.here()
    pieces, state = pack(grid, clicks, site_mats[0], left_start)
    shifts = [(dx, dy) for dx in range(nx) for dy in range(ny)]

    own_clicks = {}
    if not grid.kernels:
        for dy in range(ny):
            for dcore in range(cores):
                own_clicks[dy, dcore] = grid.send(clicks, dy=dy, dcore=dcore) if dy or dcore else clicks

    def clicks_of(site):
        value = clicks
        for (dy, dcore), got in own_clicks.items():
            hit = ((y - site // cores) % ny == dy) & ((core - site % cores) % cores == dcore)
            value = jnp.where(hit, got, value)
        return own_samples(grid, value)

    def spread(which, pieces, some):
        return {(dx, dy): grid.send(pieces[dx * ny + dy], dx=dx, dy=dy, cores=[which]) for dx, dy in some}

    straight = [(dx, dy) for dx, dy in shifts[1:] if not (dx and dy)]
    oblique = [(dx, dy) for dx, dy in shifts if dx and dy]
    spreads = [{(0, 0): pieces[0]} for _ in range(max(cores, 2))]
    spreads[0].update(spread(0, pieces, shifts[:0:-1]))
    sides = {}

    def sides_of(site, token):
        mine = collect(grid, site, spreads[site % cores], token)
        sides[site] = mine, grid.send(mine, dcore=1, cores=[site % cores])

    for site in range(sites):
        gathered = grid.gather(state, relay=True)
        if site < cores - 1:
            gathered[-1], later = lax.optimization_barrier((gathered[-1], pieces))
            spreads[site + 1].update(spread(site + 1, later, straight))
        token = gathered if site == 0 else gathered[1:3]
        if 0 < site < sites - 1:
            sides_of(site + 1, token)
            token = sides[site + 1][:1]
        if site not in sides:
            sides_of(site, token)
        mine, other = sides[site]
        token = list(spreads[1].values())[1:] if site == 0 else []
        outs = site_product(grid, site, clicks_of(site), mine, other, gathered, token)
        state = outs[0]
        for e, (ex, ey) in enumerate(shifts):
            if e:
                state = state + grid.send(outs[e], dx=ex, dy=ey)
        if site < cores - 1:
            state, later = lax.optimization_barrier((state, pieces))
            spreads[site + 1].update(spread(site + 1, later, oblique))
    return state


def solution(mesh):
    return jax.shard_map(
        local,
        mesh=mesh,
        in_specs=(P("bond", None), P("site", None, "bond", None), P("site", None)),
        out_specs=P("bond", "site"),
        check_vma=False,
    )
```

time: 905 us -> 187 us (0.21)
  blocking collectives: 485 us -> 0 us
  starting transfers between devices: 193 us -> 33.2 us
  matrix products: 138 us -> 0 us
  waiting for transfers between devices: 54.1 us -> 132 us
  Pallas kernels: 0 us -> 16.2 us
  other arithmetic: 14.7 us -> 1.02 us
  between operations: 13.4 us -> 0.25 us
    all_gather x19 -> x0, blocking collectives: 485 us -> none  [tick(): whole = lax.all_gather(own_cols, 'bond', axis=0, tiled=True)]
    ppermute x19 -> x34, starting transfers between devices: 193 us -> 33.2 us  [send(): return lax.ppermute(value, ('site', 'bond'), pairs)]
    dot_general x38 -> x0, matrix products: 138 us -> none  [the longest x19 69 us: contract(): jnp.dot(matrix_pair[1], states, precision=lax.Precision.HIGHEST, preferre...]
    ppermute x19 -> x34, waiting for transfers between devices: 24.8 us -> 132 us  [send(): return lax.ppermute(value, ('site', 'bond'), pairs)]
    reduce_scatter x1 -> x0, waiting for transfers between devices: 29.3 us -> none  [local(): return lax.psum_scatter(finals, 'site', scatter_dimension=1, tiled=True)]
    pallas_call x0 -> x9, Pallas kernels: none -> 16.2 us  [the longest x4 9.95 us: site_product(): pl.pallas_call(functools.partial(site_kernel, grid, site, last, len(token...]
    eq x19 -> x0, other arithmetic: 14.5 us -> none  [contract(): return jnp.where(chosen[None, :] == 1, second, first)]
  transfers between devices with their start and end apart: 20 -> 34, of which waited for: 20 -> 24; matrix products, arithmetic and copies ran while one was open for 0% -> 0% of each run, Pallas kernels for 0% -> 3%
where the time goes in v2:
time: 187 us; the launch traced here: 184 us
  waiting for transfers between devices  132 us (71%)
  starting transfers between devices  33.2 us (18%)
  Pallas kernels  16.2 us (9%)
  local copies, waits for them, and re-layouts  2.19 us (1%)
    ppermute x34, waiting for transfers between devices, send(): return lax.ppermute(value, ('site', 'bond'), pairs)  132 us
    ppermute x34, starting transfers between devices, send(): return lax.ppermute(value, ('site', 'bond'), pairs)  33.2 us
    pallas_call x4, Pallas kernels, site_product(): pl.pallas_call(functools.partial(site_kernel, grid, site, last, len(token...  9.95 us
    pallas_call x1, Pallas kernels, pack(): pl.pallas_call(functools.partial(pack_kernel, grid), out_shape=[jax.Shape...  4.57 us
  transfers between devices with their start and end apart: 34, of which 24 were waited for; matrix products, arithmetic and copies ran while one was open for 0% of the time, Pallas kernels for 3%

profile of v2, /device:TPU:25, one launch (start us, length us, event | category | flops | bytes accessed | tf_op | source)
XLA Modules:
  0.0 184.3 jit_solution(9433077982855156188)
XLA Ops:
  0.0 4.6 %shard_map.37 = (f32[520,512]{1,0:T(8,128)}, f32[520,512]{1,0:T(8,128)}, f32[520,512]{1,0:T(8,128)}, f32[520,512]{1,0:T(8,128)}, f32[128,512]{1,0:T(8,128)}) custom-call(s32[1,1024]{1,0:T(1,128)} %clicks_ref.1, f32[2,256,2048]{2,1,0:T(8,128)} %bitcast.1, f32[256,1024]{1,0:T(8,128)} %left_ref.1), custom_call_target="tpu_custom_call" | custom-call | bytes 8388608 | tf_op jit(solution)/shard_map/pallas_call | solution.py:133
  6.9 9.0 %collective-permute-done.refs_6_.refs_2_ = f32[128,512]{1,0:T(8,128)S(1)} collective-permute-done((f32[128,512]{1,0:T(8,128)}, f32[128,512]{1,0:T(8,128)S(1)}, u32[]{:S(2)}, u32[]{:S(2)}) %collective-permute-start) | collective-permute-done | bytes 262176 | tf_op jit(solution)/shard_map/ppermute | solution.py:45
  15.9 1.5 collective-permute-start.7
  17.4 6.6 %collective-permute-done.1.refs_7_.refs_3_ = f32[128,512]{1,0:T(8,128)S(1)} collective-permute-done((f32[128,512]{1,0:T(8,128)S(1)}, f32[128,512]{1,0:T(8,128)S(1)}, u32[]{:S(2)}, u32[]{:S(2)}) %collective-permute-start.1) | collective-permute-done | bytes 262176 | tf_op jit(solution)/shard_map/ppermute | solution.py:45
  24.0 3.1 %collective-permute-done.7.refs_5_.refs_1_ = f32[128,512]{1,0:T(8,128)S(1)} collective-permute-done((f32[128,512]{1,0:T(8,128)}, f32[128,512]{1,0:T(8,128)S(1)}, u32[]{:S(2)}, u32[]{:S(2)}) %collective-permute-start.7) | collective-permute-done | bytes 262176 | tf_op jit(solution)/shard_map/ppermute | solution.py:45
  31.1 3.1 %collective-permute-start.2 = (f32[520,512]{1,0:T(8,128)S(1)}, f32[520,512]{1,0:T(8,128)S(1)}, u32[]{:S(2)}, u32[]{:S(2)}) collective-permute-start(f32[520,512]{1,0:T(8,128)S(1)} %copy-done.6), channel_id=1, source_target_pairs={{8,24},{24,8},{9,25},{25,9},{10,26},{26,10},{11,27},{27,11},{12,28... | collective-permute-start | bytes 3194888 | tf_op jit(solution)/shard_map/ppermute | solution.py:45
  34.2 3.1 %collective-permute-start.3 = (f32[520,512]{1,0:T(8,128)S(1)}, f32[520,512]{1,0:T(8,128)S(1)}, u32[]{:S(2)}, u32[]{:S(2)}) collective-permute-start(f32[520,512]{1,0:T(8,128)S(1)} %copy-done.5), channel_id=1, source_target_pairs={{8,9},{24,25},{9,8},{25,24},{10,11},{26,27},{11,10},{27,26},{12,13... | collective-permute-start | bytes 3194888 | tf_op jit(solution)/shard_map/ppermute | solution.py:45
  37.4 10.5 %collective-permute-done.2.refs_4_.refs_1_ = f32[520,512]{1,0:T(8,128)S(1)} collective-permute-done((f32[520,512]{1,0:T(8,128)S(1)}, f32[520,512]{1,0:T(8,128)S(1)}, u32[]{:S(2)}, u32[]{:S(2)}) %collective-permute-start.2) | collective-permute-done | bytes 1064992 | tf_op jit(solution)/shard_map/ppermute | solution.py:45
  47.8 2.1 %collective-permute-done.3.refs_5_.refs_2_ = f32[520,512]{1,0:T(8,128)S(1)} collective-permute-done((f32[520,512]{1,0:T(8,128)S(1)}, f32[520,512]{1,0:T(8,128)S(1)}, u32[]{:S(2)}, u32[]{:S(2)}) %collective-permute-start.3) | collective-permute-done | bytes 1064992 | tf_op jit(solution)/shard_map/ppermute | solution.py:45
  50.0 2.5 %shard_map.39 = (f32[128,512]{1,0:T(8,128)S(1)}, f32[128,512]{1,0:T(8,128)S(1)}, f32[128,512]{1,0:T(8,128)S(1)}, f32[128,512]{1,0:T(8,128)S(1)}) custom-call(f32[2,520,512]{2,1,0:T(8,128)S(1)} %shard_map.38.mine_ref, f32[2,520,512]{2,1,0:T(8,128)S(1)} %collective-permute-done.8.other_ref, f32[128,512]{1,0:T(8,128)S(1)} %copy-done.3, ...), custom_call_target="tpu_custom_call" | custom-call | flops 1610612736 | bytes 4227072 | tf_op jit(solution)/shard_map/pallas_call | solution.py:274
  55.2 5.2 %collective-permute-done.9 = f32[128,512]{1,0:T(8,128)S(1)} collective-permute-done((f32[128,512]{1,0:T(8,128)S(1)}, f32[128,512]{1,0:T(8,128)S(1)}, u32[]{:S(2)}, u32[]{:S(2)}) %collective-permute-start.9) | collective-permute-done | bytes 262176 | tf_op jit(solution)/shard_map/ppermute | solution.py:45
  60.5 2.7 %collective-permute-done.11 = f32[128,512]{1,0:T(8,128)S(1)} collective-permute-done((f32[128,512]{1,0:T(8,128)S(1)}, f32[128,512]{1,0:T(8,128)S(1)}, u32[]{:S(2)}, u32[]{:S(2)}) %collective-permute-start.11) | collective-permute-done | bytes 262176 | tf_op jit(solution)/shard_map/ppermute | solution.py:45
  63.3 4.1 %collective-permute-start.12 = (f32[520,512]{1,0:T(8,128)S(1)}, f32[520,512]{1,0:T(8,128)S(1)}, u32[]{:S(2)}, u32[]{:S(2)}) collective-permute-start(f32[520,512]{1,0:T(8,128)S(1)} %copy-done.4), channel_id=1, source_target_pairs={{8,25},{24,9},{9,24},{25,8},{10,27},{26,11},{11,26},{27,10},{12,29... | collective-permute-start | bytes 3194888 | tf_op jit(solution)/shard_map/ppermute | solution.py:45
  67.7 8.7 %collective-permute-done.14.refs_5_.refs_2_ = f32[128,512]{1,0:T(8,128)S(1)} collective-permute-done((f32[128,512]{1,0:T(8,128)S(1)}, f32[128,512]{1,0:T(8,128)S(1)}, u32[]{:S(2)}, u32[]{:S(2)}) %collective-permute-start.14) | collective-permute-done | bytes 262176 | tf_op jit(solution)/shard_map/ppermute | solution.py:45
  76.8 3.1 %collective-permute-done.12.refs_3_ = f32[520,512]{1,0:T(8,128)S(1)} collective-permute-done((f32[520,512]{1,0:T(8,128)S(1)}, f32[520,512]{1,0:T(8,128)S(1)}, u32[]{:S(2)}, u32[]{:S(2)}) %collective-permute-start.12) | collective-permute-done | bytes 1064992 | tf_op jit(solution)/shard_map/ppermute | solution.py:45
  80.3 1.4 collective-permute-start.15
  83.3 3.8 %collective-permute-done.16.refs_3_ = f32[128,512]{1,0:T(8,128)S(1)} collective-permute-done((f32[128,512]{1,0:T(8,128)S(1)}, f32[128,512]{1,0:T(8,128)S(1)}, u32[]{:S(2)}, u32[]{:S(2)}) %collective-permute-start.16) | collective-permute-done | bytes 262176 | tf_op jit(solution)/shard_map/ppermute | solution.py:45
  87.1 2.5 %shard_map.42 = (f32[128,512]{1,0:T(8,128)S(1)}, f32[128,512]{1,0:T(8,128)S(1)}, f32[128,512]{1,0:T(8,128)S(1)}, f32[128,512]{1,0:T(8,128)S(1)}) custom-call(f32[2,520,512]{2,1,0:T(8,128)S(1)} %shard_map.41.mine_ref, f32[2,520,512]{2,1,0:T(8,128)S(1)} %collective-permute-done.15.other_ref, f32[128,512]{1,0:T(8,128)S(1)} %add_add_fusion.3.refs_0_, ...), custom_call_target="tpu_custom_call" | custom-call | flops 1610612736 | bytes 4227072 | tf_op jit(solution)/shard_map/pallas_call | solution.py:274
  92.3 4.9 %collective-permute-done.17 = f32[128,512]{1,0:T(8,128)S(1)} collective-permute-done((f32[128,512]{1,0:T(8,128)S(1)}, f32[128,512]{1,0:T(8,128)S(1)}, u32[]{:S(2)}, u32[]{:S(2)}) %collective-permute-start.17) | collective-permute-done | bytes 262176 | tf_op jit(solution)/shard_map/ppermute | solution.py:45
  97.2 1.9 %collective-permute-done.18 = f32[128,512]{1,0:T(8,128)S(1)} collective-permute-done((f32[128,512]{1,0:T(8,128)S(1)}, f32[128,512]{1,0:T(8,128)S(1)}, u32[]{:S(2)}, u32[]{:S(2)}) %collective-permute-start.18) | collective-permute-done | bytes 262176 | tf_op jit(solution)/shard_map/ppermute | solution.py:45
  99.1 4.8 %collective-permute-done.19 = f32[128,512]{1,0:T(8,128)S(1)} collective-permute-done((f32[128,512]{1,0:T(8,128)S(1)}, f32[128,512]{1,0:T(8,128)S(1)}, u32[]{:S(2)}, u32[]{:S(2)}) %collective-permute-start.19) | collective-permute-done | bytes 262176 | tf_op jit(solution)/shard_map/ppermute | solution.py:45
  104.4 14.4 %collective-permute-done.21.refs_5_.refs_2_ = f32[128,512]{1,0:T(8,128)S(1)} collective-permute-done((f32[128,512]{1,0:T(8,128)S(1)}, f32[128,512]{1,0:T(8,128)S(1)}, u32[]{:S(2)}, u32[]{:S(2)}) %collective-permute-start.21) | collective-permute-done | bytes 262176 | tf_op jit(solution)/shard_map/ppermute | solution.py:45
  119.2 2.5 %collective-permute-start.22 = (f32[2,520,512]{2,1,0:T(8,128)S(1)}, f32[2,520,512]{2,1,0:T(8,128)S(1)}, u32[]{:S(2)}, u32[]{:S(2)}) collective-permute-start(f32[2,520,512]{2,1,0:T(8,128)S(1)} %shard_map.43.mine_ref), channel_id=1, source_target_pairs={{8,0},{24,16},{9,1},{25,17},{10,2},{26,18},{11,3},{27,19},{12,4},{... | collective-permute-start | bytes 6389768 | tf_op jit(solution)/shard_map/ppermute | solution.py:45
  121.8 7.7 %collective-permute-done.24.refs_3_ = f32[128,512]{1,0:T(8,128)S(1)} collective-permute-done((f32[128,512]{1,0:T(8,128)S(1)}, f32[128,512]{1,0:T(8,128)S(1)}, u32[]{:S(2)}, u32[]{:S(2)}) %collective-permute-start.24) | collective-permute-done | bytes 262176 | tf_op jit(solution)/shard_map/ppermute | solution.py:45
  129.5 2.5 %shard_map.44 = (f32[128,512]{1,0:T(8,128)S(1)}, f32[128,512]{1,0:T(8,128)S(1)}, f32[128,512]{1,0:T(8,128)S(1)}, f32[128,512]{1,0:T(8,128)S(1)}) custom-call(f32[2,520,512]{2,1,0:T(8,128)S(1)} %shard_map.40.refs_4_.mine_ref, f32[2,520,512]{2,1,0:T(8,128)S(1)} %collective-permute-done.23.other_ref, f32[128,512]{1,0:T(8,128)S(1)} %add_add_fusion.2.refs_0_, ...), custom_call_target="tpu_custom_call" | custom-call | flops 1610612736 | bytes 4227072 | tf_op jit(solution)/shard_map/pallas_call | solution.py:274
  134.7 4.8 %collective-permute-done.25 = f32[128,512]{1,0:T(8,128)S(1)} collective-permute-done((f32[128,512]{1,0:T(8,128)S(1)}, f32[128,512]{1,0:T(8,128)S(1)}, u32[]{:S(2)}, u32[]{:S(2)}) %collective-permute-start.25) | collective-permute-done | bytes 262176 | tf_op jit(solution)/shard_map/ppermute | solution.py:45
  140.5 5.6 %collective-permute-done.27 = f32[128,512]{1,0:T(8,128)S(1)} collective-permute-done((f32[128,512]{1,0:T(8,128)S(1)}, f32[128,512]{1,0:T(8,128)S(1)}, u32[]{:S(2)}, u32[]{:S(2)}) %collective-permute-start.27) | collective-permute-done | bytes 262176 | tf_op jit(solution)/shard_map/ppermute | solution.py:45
  146.7 13.9 %collective-permute-done.29.refs_2_ = f32[128,512]{1,0:T(8,128)S(1)} collective-permute-done((f32[128,512]{1,0:T(8,128)S(1)}, f32[128,512]{1,0:T(8,128)S(1)}, u32[]{:S(2)}, u32[]{:S(2)}) %collective-permute-start.29) | collective-permute-done | bytes 262176 | tf_op jit(solution)/shard_map/ppermute | solution.py:45
  160.6 7.4 %collective-permute-done.30.refs_3_ = f32[128,512]{1,0:T(8,128)S(1)} collective-permute-done((f32[128,512]{1,0:T(8,128)S(1)}, f32[128,512]{1,0:T(8,128)S(1)}, u32[]{:S(2)}, u32[]{:S(2)}) %collective-permute-start.30) | collective-permute-done | bytes 262176 | tf_op jit(solution)/shard_map/ppermute | solution.py:45
  168.0 2.5 %shard_map.45 = (f32[256,256]{1,0:T(8,128)S(1)}, f32[256,256]{1,0:T(8,128)S(1)}, f32[256,256]{1,0:T(8,128)S(1)}, f32[256,256]{1,0:T(8,128)S(1)}) custom-call(f32[2,520,512]{2,1,0:T(8,128)S(1)} %shard_map.43.mine_ref, f32[2,520,512]{2,1,0:T(8,128)S(1)} %collective-permute-done.22.other_ref, f32[128,512]{1,0:T(8,128)S(1)} %add_add_fusion.1.refs_0_, ...), custom_call_target="tpu_custom_call" | custom-call | flops 1610612736 | bytes 4227072 | tf_op jit(solution)/shard_map/pallas_call | solution.py:274
  173.2 3.8 %collective-permute-done.31 = f32[256,256]{1,0:T(8,128)S(1)} collective-permute-done((f32[256,256]{1,0:T(8,128)S(1)}, f32[256,256]{1,0:T(8,128)S(1)}, u32[]{:S(2)}, u32[]{:S(2)}) %collective-permute-start.31) | collective-permute-done | bytes 262176 | tf_op jit(solution)/shard_map/ppermute | solution.py:45
  178.0 5.6 %collective-permute-done.33 = f32[256,256]{1,0:T(8,128)S(1)} collective-permute-done((f32[256,256]{1,0:T(8,128)S(1)}, f32[256,256]{1,0:T(8,128)S(1)}, u32[]{:S(2)}, u32[]{:S(2)}) %collective-permute-start.33) | collective-permute-done | bytes 262176 | tf_op jit(solution)/shard_map/ppermute | solution.py:45
  (63 shorter events, 24.3 us)
Async XLA Ops:
  4.6 22.4 %collective-permute-start.6 = (f32[520,512]{1,0:T(8,128)}, f32[520,512]{1,0:T(8,128)S(1)}, u32[]{:S(2)}, u32[]{:S(2)}) collective-permute-start(f32[520,512]{1,0:T(8,128)} %get-tuple-element.36), channel_id=1, source_target_pairs={{0,16},{16,0},{1,17},{17,1},{2,18},{18,2},{3,19},{19,3},{4,20},{20... | collective-permute-start | bytes 3194888 | tf_op jit(solution)/shard_map/ppermute | solution.py:45
  5.3 21.7 %collective-permute-start.5 = (f32[520,512]{1,0:T(8,128)}, f32[520,512]{1,0:T(8,128)S(1)}, u32[]{:S(2)}, u32[]{:S(2)}) collective-permute-start(f32[520,512]{1,0:T(8,128)} %get-tuple-element.37), channel_id=1, source_target_pairs={{0,1},{16,17},{1,0},{17,16},{2,3},{18,19},{3,2},{19,18},{4,5},{20,... | collective-permute-start | bytes 3194888 | tf_op jit(solution)/shard_map/ppermute | solution.py:45
  6.1 21.0 %collective-permute-start.4 = (f32[520,512]{1,0:T(8,128)}, f32[520,512]{1,0:T(8,128)S(1)}, u32[]{:S(2)}, u32[]{:S(2)}) collective-permute-start(f32[520,512]{1,0:T(8,128)} %get-tuple-element.43), channel_id=1, source_target_pairs={{0,17},{16,1},{1,16},{17,0},{2,19},{18,3},{3,18},{19,2},{4,21},{20... | collective-permute-start | bytes 3194888 | tf_op jit(solution)/shard_map/ppermute | solution.py:45
  6.8 9.1 %collective-permute-start = (f32[128,512]{1,0:T(8,128)}, f32[128,512]{1,0:T(8,128)S(1)}, u32[]{:S(2)}, u32[]{:S(2)}) collective-permute-start(f32[128,512]{1,0:T(8,128)} %get-tuple-element.32.refs_4_.refs_0_), channel_id=1, source_target_pairs={{0,4},{8,12},{16,20},{24,28},{1,5},{9,13},{17,21},{25,29},{2,6},{1... | collective-permute-start | bytes 786440 | tf_op jit(solution)/shard_map/ppermute | solution.py:45
  15.9 8.1 %collective-permute-start.1 = (f32[128,512]{1,0:T(8,128)S(1)}, f32[128,512]{1,0:T(8,128)S(1)}, u32[]{:S(2)}, u32[]{:S(2)}) collective-permute-start(f32[128,512]{1,0:T(8,128)S(1)} %collective-permute-done.refs_6_.refs_2_), channel_id=1, source_target_pairs={{0,2},{8,10},{16,18},{24,26},{1,3},{9,11},{17,19},{25,27},{2,0},{1... | collective-permute-start | bytes 786440 | tf_op jit(solution)/shard_map/ppermute | solution.py:45
  15.9 11.1 %collective-permute-start.7 = (f32[128,512]{1,0:T(8,128)}, f32[128,512]{1,0:T(8,128)S(1)}, u32[]{:S(2)}, u32[]{:S(2)}) collective-permute-start(f32[128,512]{1,0:T(8,128)} %get-tuple-element.32.refs_4_.refs_0_), channel_id=1, source_target_pairs={{0,2},{8,10},{16,18},{24,26},{1,3},{9,11},{17,19},{25,27},{2,0},{1... | collective-permute-start | bytes 786440 | tf_op jit(solution)/shard_map/ppermute | solution.py:45
  29.6 20.3 %collective-permute-start.8 = (f32[2,520,512]{2,1,0:T(8,128)S(1)}, f32[2,520,512]{2,1,0:T(8,128)S(1)}, u32[]{:S(2)}, u32[]{:S(2)}) collective-permute-start(f32[2,520,512]{2,1,0:T(8,128)S(1)} %shard_map.38.mine_ref), channel_id=1, source_target_pairs={{0,8},{16,24},{1,9},{17,25},{2,10},{18,26},{3,11},{19,27},{4,12},{... | collective-permute-start | bytes 6389768 | tf_op jit(solution)/shard_map/ppermute | solution.py:45
  31.1 16.8 %collective-permute-start.2 = (f32[520,512]{1,0:T(8,128)S(1)}, f32[520,512]{1,0:T(8,128)S(1)}, u32[]{:S(2)}, u32[]{:S(2)}) collective-permute-start(f32[520,512]{1,0:T(8,128)S(1)} %copy-done.6), channel_id=1, source_target_pairs={{8,24},{24,8},{9,25},{25,9},{10,26},{26,10},{11,27},{27,11},{12,28... | collective-permute-start | bytes 3194888 | tf_op jit(solution)/shard_map/ppermute | solution.py:45
  34.2 15.7 %collective-permute-start.3 = (f32[520,512]{1,0:T(8,128)S(1)}, f32[520,512]{1,0:T(8,128)S(1)}, u32[]{:S(2)}, u32[]{:S(2)}) collective-permute-start(f32[520,512]{1,0:T(8,128)S(1)} %copy-done.5), channel_id=1, source_target_pairs={{8,9},{24,25},{9,8},{25,24},{10,11},{26,27},{11,10},{27,26},{12,13... | collective-permute-start | bytes 3194888 | tf_op jit(solution)/shard_map/ppermute | solution.py:45
  52.5 7.9 %collective-permute-start.9 = (f32[128,512]{1,0:T(8,128)S(1)}, f32[128,512]{1,0:T(8,128)S(1)}, u32[]{:S(2)}, u32[]{:S(2)}) collective-permute-start(f32[128,512]{1,0:T(8,128)S(1)} %get-tuple-element.40), channel_id=1, source_target_pairs={{0,16},{8,24},{16,0},{24,8},{1,17},{9,25},{17,1},{25,9},{2,18},{10... | collective-permute-start | bytes 786440 | tf_op jit(solution)/shard_map/ppermute | solution.py:45
  52.8 7.7 %collective-permute-start.10 = (f32[128,512]{1,0:T(8,128)S(1)}, f32[128,512]{1,0:T(8,128)S(1)}, u32[]{:S(2)}, u32[]{:S(2)}) collective-permute-start(f32[128,512]{1,0:T(8,128)S(1)} %get-tuple-element.41), channel_id=1, source_target_pairs={{0,1},{8,9},{16,17},{24,25},{1,0},{9,8},{17,16},{25,24},{2,3},{10,... | collective-permute-start | bytes 786440 | tf_op jit(solution)/shard_map/ppermute | solution.py:45
  54.0 9.2 %collective-permute-start.11 = (f32[128,512]{1,0:T(8,128)S(1)}, f32[128,512]{1,0:T(8,128)S(1)}, u32[]{:S(2)}, u32[]{:S(2)}) collective-permute-start(f32[128,512]{1,0:T(8,128)S(1)} %get-tuple-element.42), channel_id=1, source_target_pairs={{0,17},{8,25},{16,1},{24,9},{1,16},{9,24},{17,0},{25,8},{2,19},{10... | collective-permute-start | bytes 786440 | tf_op jit(solution)/shard_map/ppermute | solution.py:45
  63.3 16.6 %collective-permute-start.12 = (f32[520,512]{1,0:T(8,128)S(1)}, f32[520,512]{1,0:T(8,128)S(1)}, u32[]{:S(2)}, u32[]{:S(2)}) collective-permute-start(f32[520,512]{1,0:T(8,128)S(1)} %copy-done.4), channel_id=1, source_target_pairs={{8,25},{24,9},{9,24},{25,8},{10,27},{26,11},{11,26},{27,10},{12,29... | collective-permute-start | bytes 3194888 | tf_op jit(solution)/shard_map/ppermute | solution.py:45
  67.4 9.0 %collective-permute-start.14 = (f32[128,512]{1,0:T(8,128)S(1)}, f32[128,512]{1,0:T(8,128)S(1)}, u32[]{:S(2)}, u32[]{:S(2)}) collective-permute-start(f32[128,512]{1,0:T(8,128)S(1)} %add_add_fusion.3.refs_0_), channel_id=1, source_target_pairs={{0,4},{8,12},{16,20},{24,28},{1,5},{9,13},{17,21},{25,29},{2,6},{1... | collective-permute-start | bytes 786440 | tf_op jit(solution)/shard_map/ppermute | solution.py:45
  67.5 8.9 %collective-permute-start.13 = (f32[128,512]{1,0:T(8,128)S(1)}, f32[128,512]{1,0:T(8,128)S(1)}, u32[]{:S(2)}, u32[]{:S(2)}) collective-permute-start(f32[128,512]{1,0:T(8,128)S(1)} %add_add_fusion.3.refs_0_), channel_id=1, source_target_pairs={{0,2},{8,10},{16,18},{24,26},{1,3},{9,11},{17,19},{25,27},{2,0},{1... | collective-permute-start | bytes 786440 | tf_op jit(solution)/shard_map/ppermute | solution.py:45
  80.3 6.7 %collective-permute-start.15 = (f32[2,520,512]{2,1,0:T(8,128)S(1)}, f32[2,520,512]{2,1,0:T(8,128)S(1)}, u32[]{:S(2)}, u32[]{:S(2)}) collective-permute-start(f32[2,520,512]{2,1,0:T(8,128)S(1)} %shard_map.41.mine_ref), channel_id=1, source_target_pairs={{8,0},{24,16},{9,1},{25,17},{10,2},{26,18},{11,3},{27,19},{12,4},{... | collective-permute-start | bytes 6389768 | tf_op jit(solution)/shard_map/ppermute | solution.py:45
  82.0 39.8 %collective-permute-start.23 = (f32[2,520,512]{2,1,0:T(8,128)S(1)}, f32[2,520,512]{2,1,0:T(8,128)S(1)}, u32[]{:S(2)}, u32[]{:S(2)}) collective-permute-start(f32[2,520,512]{2,1,0:T(8,128)S(1)} %shard_map.40.refs_4_.mine_ref), channel_id=1, source_target_pairs={{0,8},{16,24},{1,9},{17,25},{2,10},{18,26},{3,11},{19,27},{4,12},{... | collective-permute-start | bytes 6389768 | tf_op jit(solution)/shard_map/ppermute | solution.py:45
  89.6 7.6 %collective-permute-start.17 = (f32[128,512]{1,0:T(8,128)S(1)}, f32[128,512]{1,0:T(8,128)S(1)}, u32[]{:S(2)}, u32[]{:S(2)}) collective-permute-start(f32[128,512]{1,0:T(8,128)S(1)} %get-tuple-element.46), channel_id=1, source_target_pairs={{0,16},{8,24},{16,0},{24,8},{1,17},{9,25},{17,1},{25,9},{2,18},{10... | collective-permute-start | bytes 786440 | tf_op jit(solution)/shard_map/ppermute | solution.py:45
  90.9 8.3 %collective-permute-start.18 = (f32[128,512]{1,0:T(8,128)S(1)}, f32[128,512]{1,0:T(8,128)S(1)}, u32[]{:S(2)}, u32[]{:S(2)}) collective-permute-start(f32[128,512]{1,0:T(8,128)S(1)} %get-tuple-element.47), channel_id=1, source_target_pairs={{0,1},{8,9},{16,17},{24,25},{1,0},{9,8},{17,16},{25,24},{2,3},{10,... | collective-permute-start | bytes 786440 | tf_op jit(solution)/shard_map/ppermute | solution.py:45
  92.2 11.8 %collective-permute-start.19 = (f32[128,512]{1,0:T(8,128)S(1)}, f32[128,512]{1,0:T(8,128)S(1)}, u32[]{:S(2)}, u32[]{:S(2)}) collective-permute-start(f32[128,512]{1,0:T(8,128)S(1)} %get-tuple-element.48), channel_id=1, source_target_pairs={{0,17},{8,25},{16,1},{24,9},{1,16},{9,24},{17,0},{25,8},{2,19},{10... | collective-permute-start | bytes 786440 | tf_op jit(solution)/shard_map/ppermute | solution.py:45
  104.0 14.7 %collective-permute-start.21 = (f32[128,512]{1,0:T(8,128)S(1)}, f32[128,512]{1,0:T(8,128)S(1)}, u32[]{:S(2)}, u32[]{:S(2)}) collective-permute-start(f32[128,512]{1,0:T(8,128)S(1)} %add_add_fusion.2.refs_0_), channel_id=1, source_target_pairs={{0,4},{8,12},{16,20},{24,28},{1,5},{9,13},{17,21},{25,29},{2,6},{1... | collective-permute-start | bytes 786440 | tf_op jit(solution)/shard_map/ppermute | solution.py:45
  104.2 14.6 %collective-permute-start.20 = (f32[128,512]{1,0:T(8,128)S(1)}, f32[128,512]{1,0:T(8,128)S(1)}, u32[]{:S(2)}, u32[]{:S(2)}) collective-permute-start(f32[128,512]{1,0:T(8,128)S(1)} %add_add_fusion.2.refs_0_), channel_id=1, source_target_pairs={{0,2},{8,10},{16,18},{24,26},{1,3},{9,11},{17,19},{25,27},{2,0},{1... | collective-permute-start | bytes 786440 | tf_op jit(solution)/shard_map/ppermute | solution.py:45
  119.2 48.8 %collective-permute-start.22 = (f32[2,520,512]{2,1,0:T(8,128)S(1)}, f32[2,520,512]{2,1,0:T(8,128)S(1)}, u32[]{:S(2)}, u32[]{:S(2)}) collective-permute-start(f32[2,520,512]{2,1,0:T(8,128)S(1)} %shard_map.43.mine_ref), channel_id=1, source_target_pairs={{8,0},{24,16},{9,1},{25,17},{10,2},{26,18},{11,3},{27,19},{12,4},{... | collective-permute-start | bytes 6389768 | tf_op jit(solution)/shard_map/ppermute | solution.py:45
  121.7 7.8 %collective-permute-start.24 = (f32[128,512]{1,0:T(8,128)S(1)}, f32[128,512]{1,0:T(8,128)S(1)}, u32[]{:S(2)}, u32[]{:S(2)}) collective-permute-start(f32[128,512]{1,0:T(8,128)S(1)} %collective-permute-done.21.refs_5_.refs_2_), channel_id=1, source_target_pairs={{0,2},{8,10},{16,18},{24,26},{1,3},{9,11},{17,19},{25,27},{2,0},{1... | collective-permute-start | bytes 786440 | tf_op jit(solution)/shard_map/ppermute | solution.py:45
  132.0 7.6 %collective-permute-start.25 = (f32[128,512]{1,0:T(8,128)S(1)}, f32[128,512]{1,0:T(8,128)S(1)}, u32[]{:S(2)}, u32[]{:S(2)}) collective-permute-start(f32[128,512]{1,0:T(8,128)S(1)} %get-tuple-element.50), channel_id=1, source_target_pairs={{0,16},{8,24},{16,0},{24,8},{1,17},{9,25},{17,1},{25,9},{2,18},{10... | collective-permute-start | bytes 786440 | tf_op jit(solution)/shard_map/ppermute | solution.py:45
  133.3 7.2 %collective-permute-start.26 = (f32[128,512]{1,0:T(8,128)S(1)}, f32[128,512]{1,0:T(8,128)S(1)}, u32[]{:S(2)}, u32[]{:S(2)}) collective-permute-start(f32[128,512]{1,0:T(8,128)S(1)} %get-tuple-element.51), channel_id=1, source_target_pairs={{0,1},{8,9},{16,17},{24,25},{1,0},{9,8},{17,16},{25,24},{2,3},{10,... | collective-permute-start | bytes 786440 | tf_op jit(solution)/shard_map/ppermute | solution.py:45
  134.5 11.5 %collective-permute-start.27 = (f32[128,512]{1,0:T(8,128)S(1)}, f32[128,512]{1,0:T(8,128)S(1)}, u32[]{:S(2)}, u32[]{:S(2)}) collective-permute-start(f32[128,512]{1,0:T(8,128)S(1)} %get-tuple-element.52), channel_id=1, source_target_pairs={{0,17},{8,25},{16,1},{24,9},{1,16},{9,24},{17,0},{25,8},{2,19},{10... | collective-permute-start | bytes 786440 | tf_op jit(solution)/shard_map/ppermute | solution.py:45
  146.1 14.5 %collective-permute-start.29 = (f32[128,512]{1,0:T(8,128)S(1)}, f32[128,512]{1,0:T(8,128)S(1)}, u32[]{:S(2)}, u32[]{:S(2)}) collective-permute-start(f32[128,512]{1,0:T(8,128)S(1)} %add_add_fusion.1.refs_0_), channel_id=1, source_target_pairs={{0,4},{8,12},{16,20},{24,28},{1,5},{9,13},{17,21},{25,29},{2,6},{1... | collective-permute-start | bytes 786440 | tf_op jit(solution)/shard_map/ppermute | solution.py:45
  146.5 14.1 %collective-permute-start.28 = (f32[128,512]{1,0:T(8,128)S(1)}, f32[128,512]{1,0:T(8,128)S(1)}, u32[]{:S(2)}, u32[]{:S(2)}) collective-permute-start(f32[128,512]{1,0:T(8,128)S(1)} %add_add_fusion.1.refs_0_), channel_id=1, source_target_pairs={{0,2},{8,10},{16,18},{24,26},{1,3},{9,11},{17,19},{25,27},{2,0},{1... | collective-permute-start | bytes 786440 | tf_op jit(solution)/shard_map/ppermute | solution.py:45
  160.6 7.4 %collective-permute-start.30 = (f32[128,512]{1,0:T(8,128)S(1)}, f32[128,512]{1,0:T(8,128)S(1)}, u32[]{:S(2)}, u32[]{:S(2)}) collective-permute-start(f32[128,512]{1,0:T(8,128)S(1)} %collective-permute-done.29.refs_2_), channel_id=1, source_target_pairs={{0,2},{8,10},{16,18},{24,26},{1,3},{9,11},{17,19},{25,27},{2,0},{1... | collective-permute-start | bytes 786440 | tf_op jit(solution)/shard_map/ppermute | solution.py:45
  170.5 6.5 %collective-permute-start.31 = (f32[256,256]{1,0:T(8,128)S(1)}, f32[256,256]{1,0:T(8,128)S(1)}, u32[]{:S(2)}, u32[]{:S(2)}) collective-permute-start(f32[256,256]{1,0:T(8,128)S(1)} %get-tuple-element.54), channel_id=1, source_target_pairs={{0,16},{8,24},{16,0},{24,8},{1,17},{9,25},{17,1},{25,9},{2,18},{10... | collective-permute-start | bytes 786440 | tf_op jit(solution)/shard_map/ppermute | solution.py:45
  173.0 10.5 %collective-permute-start.33 = (f32[256,256]{1,0:T(8,128)S(1)}, f32[256,256]{1,0:T(8,128)S(1)}, u32[]{:S(2)}, u32[]{:S(2)}) collective-permute-start(f32[256,256]{1,0:T(8,128)S(1)} %get-tuple-element.56), channel_id=1, source_target_pairs={{0,17},{8,25},{16,1},{24,9},{1,16},{9,24},{17,0},{25,8},{2,19},{10... | collective-permute-start | bytes 786440 | tf_op jit(solution)/shard_map/ppermute | solution.py:45
  (9 other events, 78.5 us)

commit v3 on v2

v3 whole, which is shorter than its diff:
```python
import functools

import jax
import jax.numpy as jnp
from jax import lax
from jax.experimental import pallas as pl
from jax.experimental.pallas import tpu as pltpu
from jax.sharding import PartitionSpec as P


CLICK_ROWS = 8
PACK_VMEM = 48 * 1024 * 1024
RELAY = (True, True, True)


class Grid:
    def __init__(self, sites, bonds, rows, samples):
        self.sites, self.bonds = sites, bonds
        self.cores = 2 if sites % 2 == 0 else 1
        self.ny = sites // self.cores
        self.nx = max(q for q in range(1, bonds + 1) if bonds % q == 0 and q * q <= bonds)
        self.nz = bonds // self.nx
        self.rows = rows
        self.strip = rows // self.ny
        self.width = self.strip * self.nz
        self.share = samples // sites
        self.cols = self.share * self.ny
        aligned = self.strip % 128 == 0 and self.share % 128 == 0
        self.kernels = aligned and self.cols == self.width and self.cores <= CLICK_ROWS

    def here(self):
        site, bond = lax.axis_index("site"), lax.axis_index("bond")
        return bond // self.nx, bond % self.nx, site // self.cores, site % self.cores

    def index(self, z, x, y, core):
        site = (y % self.ny) * self.cores + core % self.cores
        return site * self.bonds + (z % self.nz) * self.nx + x % self.nx

    def send(self, value, dz=0, dx=0, dy=0, dcore=0, across=0, cores=None):
        pairs = []
        for z in range(self.nz):
            for x in range(self.nx):
                for y in range(self.ny):
                    for core in range(self.cores) if cores is None else cores:
                        to = self.index((z ^ across) + dz, x + dx, y + dy, core + dcore)
                        pairs.append((self.index(z, x, y, core), to))
        return lax.ppermute(value, ("site", "bond"), pairs)

    def gather(self, state, relay=False):
        if self.nz & (self.nz - 1):
            return [state] + [self.send(state, dz=self.nz - d) for d in range(1, self.nz)]
        got = [state]
        for d in range(1, self.nz):
            got.append(self.send(got[d ^ 1], across=1) if relay and d & 1 else self.send(state, across=d))
        return got

    def gathered_from(self, z):
        if self.nz & (self.nz - 1):
            return [lax.rem(z + d, self.nz) for d in range(self.nz)]
        return [z ^ d for d in range(self.nz)]


def halves(value):
    high = value.astype(jnp.bfloat16)
    low = (value - high.astype(jnp.float32)).astype(jnp.bfloat16)
    return high, low


def dot3(a, b):
    dot = functools.partial(jnp.dot, preferred_element_type=jnp.float32)
    return dot(a[0], b[0]) + (dot(a[0], b[1]) + dot(a[1], b[0]))


def pack_kernel(grid, clicks_ref, mats_ref, left_ref, *refs):
    nx, ny, nz, cores, rows, strip, share = grid.nx, grid.ny, grid.nz, grid.cores, grid.rows, grid.strip, grid.share
    piece_refs, state_ref = refs[: nx * ny], refs[nx * ny]
    clicks_held_ref, clicks_sem, in_sems, left_sems = refs[nx * ny + 1 :]
    _, x, y, core = grid.here()
    clicks_copy = pltpu.make_async_copy(clicks_ref, clicks_held_ref, clicks_sem)
    clicks_copy.start()
    order = [(dx, dy) for dx in reversed(range(nx)) for dy in reversed(range(ny))]
    into = {}
    for dx, dy in order:
        e = dx * ny + dy
        into[e] = []
        for zz in range(nz):
            start = zz * nx * rows + lax.rem(x + dx, nx) * rows + lax.rem(y + dy, ny) * strip
            columns = pl.ds(pl.multiple_of(start, strip), strip)
            for o in range(2):
                target = piece_refs[e].at[pl.ds(o * rows, rows), pl.ds(zz * strip, strip)]
                into[e].append(pltpu.make_async_copy(mats_ref.at[o, :, columns], target, in_sems.at[e, zz, o]))
        for copy in into[e]:
            copy.start()
    states = []
    for yy in range(ny):
        start = pl.multiple_of((yy * cores + core) * share, share)
        source = left_ref.at[pl.ds(pl.multiple_of(y * strip, strip), strip), pl.ds(start, share)]
        states.append(pltpu.make_async_copy(source, state_ref.at[:, pl.ds(yy * share, share)], left_sems.at[yy]))
    for copy in states:
        copy.start()
    clicks_copy.wait()
    for piece_ref in piece_refs:
        piece_ref[2 * rows :, :] = jnp.zeros((CLICK_ROWS, grid.width), jnp.float32)
        for c in range(cores):
            for yy in range(ny):
                start = (yy * cores + c) * share
                value = clicks_held_ref[:, start : start + share].astype(jnp.float32)
                piece_ref[2 * rows + c : 2 * rows + c + 1, yy * share : (yy + 1) * share] = value
    for copy in sum(into.values(), states):
        copy.wait()


def own_samples(grid, value):
    core = grid.here()[3]
    starts = [(yy * grid.cores + core) * grid.share for yy in range(grid.ny)]
    return jnp.concatenate([lax.dynamic_slice_in_dim(value, start, grid.share, 1) for start in starts], axis=1)


def pack(grid, clicks, mats, left):
    nx, ny, nz, rows, strip = grid.nx, grid.ny, grid.nz, grid.rows, grid.strip
    if grid.kernels:
        vmem, hbm = pl.BlockSpec(memory_space=pltpu.VMEM), pl.BlockSpec(memory_space=pltpu.HBM)
        tall = 2 * rows + CLICK_ROWS
        out = pl.pallas_call(
            functools.partial(pack_kernel, grid),
            out_shape=[jax.ShapeDtypeStruct((tall, grid.width), jnp.float32)] * (nx * ny)
            + [jax.ShapeDtypeStruct((strip, grid.cols), jnp.float32)],
            in_specs=[hbm] * 3,
            out_specs=[vmem] * (nx * ny + 1),
            scratch_shapes=[
                pltpu.VMEM(clicks.shape, jnp.int32),
                pltpu.SemaphoreType.DMA,
                pltpu.SemaphoreType.DMA((nx * ny, nz, 2)),
                pltpu.SemaphoreType.DMA((ny,)),
            ],
            compiler_params=pltpu.CompilerParams(vmem_limit_bytes=PACK_VMEM),
            cost_estimate=pl.CostEstimate(flops=0, bytes_accessed=2 * mats.size * 4, transcendentals=0),
        )(clicks, mats, left)
        return out[: nx * ny], out[nx * ny]
    _, x, y, _ = grid.here()
    pieces = []
    for dx in range(nx):
        for dy in range(ny):
            strips = []
            for zz in range(nz):
                start = zz * nx * rows + ((x + dx) % nx) * rows + ((y + dy) % ny) * strip
                strips.append(lax.dynamic_slice_in_dim(mats, start, strip, 2))
            pieces.append(jnp.concatenate(strips, axis=2).reshape(2 * rows, grid.width))
    return pieces, own_samples(grid, lax.dynamic_slice_in_dim(left, y * strip, strip, 0))


def collect_kernel(grid, sites, keys, *refs):
    pieces, (out_ref, held_ref, in_sems, out_sems) = dict(zip(keys, refs)), refs[-4:]
    _, _, y, core = grid.here()

    @pl.when(core == sites[0] % grid.cores)
    def _():
        for k, site in enumerate(sites):
            behind = lax.rem(y + grid.ny - site // grid.cores, grid.ny)
            for dx, dy in keys:

                @pl.when(behind == dy)
                def _():
                    pltpu.make_async_copy(pieces[dx, dy], held_ref.at[k, dx], in_sems.at[k, dx]).start()

        outward = []
        for k in range(len(sites)):
            for dx in range(grid.nx):
                pltpu.make_async_copy(refs[0], held_ref.at[k, dx], in_sems.at[k, dx]).wait()
                outward.append(pltpu.make_async_copy(held_ref.at[k, dx], out_ref.at[k, dx], out_sems.at[k, dx]))
                outward[-1].start()
        for copy in outward:
            copy.wait()


def collect(grid, sites, pieces, token=()):
    nx = grid.nx
    keys = tuple(pieces)
    tall, width = pieces[0, 0].shape
    if grid.kernels:
        hbm = pl.BlockSpec(memory_space=pl.ANY)
        shape = (len(sites), nx, tall, width)
        operands = list(pieces.values()) + list(token)
        return pl.pallas_call(
            functools.partial(collect_kernel, grid, tuple(sites), keys),
            out_shape=jax.ShapeDtypeStruct(shape, jnp.float32),
            in_specs=[hbm] * len(operands),
            out_specs=hbm,
            scratch_shapes=[
                pltpu.VMEM(shape, jnp.float32),
                pltpu.SemaphoreType.DMA(shape[:2]),
                pltpu.SemaphoreType.DMA(shape[:2]),
            ],
            compiler_params=pltpu.CompilerParams(vmem_limit_bytes=32 * 1024 * 1024),
            cost_estimate=pl.CostEstimate(flops=0, bytes_accessed=8 * len(sites) * nx * tall * width, transcendentals=0),
        )(*operands)
    mats = []
    for site in sites:
        behind = (grid.here()[2] - site // grid.cores) % grid.ny
        for dx in range(nx):
            value = pieces[dx, 0]
            for dy in range(1, grid.ny):
                value = jnp.where(behind == dy, pieces[dx, dy], value)
            mats.append(value)
    return jnp.stack(mats).reshape(len(sites), nx, tall, width)


def site_kernel(grid, site, last, tokens, *refs):
    nx, ny, nz, rows, strip, share = grid.nx, grid.ny, grid.nz, grid.rows, grid.strip, grid.share
    mats, refs = refs[: grid.cores], refs[grid.cores :]
    states, refs = refs[:nz], refs[nz + tokens :]
    outs = refs[: nx * ny]
    mat_ref, state_ref, high_ref, low_ref, sems, state_sems = refs[nx * ny :]
    z, _, y, core = grid.here()
    place = site // grid.cores
    inward = []
    for n, source in enumerate(grid.gathered_from(z)):
        at = pl.ds(pl.multiple_of(source * strip, strip), strip)
        inward.append(pltpu.make_async_copy(states[n], state_ref.at[at], state_sems.at[n]))
        inward[-1].start()

    for role, ref in enumerate(mats):

        @pl.when(core == role)
        def _():
            for dx in range(nx):
                pltpu.make_async_copy(ref.at[place, dx], mat_ref.at[dx], sems.at[dx]).start()

    for copy in inward:
        copy.wait()
    high_ref[...], low_ref[...] = halves(state_ref[...])
    for ex in range(nx):
        dx = (nx - ex) % nx
        pltpu.make_async_copy(mats[0].at[place, dx], mat_ref.at[dx], sems.at[dx]).wait()
        if ex == 0:
            clicks = mat_ref[0, 2 * rows : 2 * rows + CLICK_ROWS, :]
            row = lax.broadcasted_iota(jnp.int32, clicks.shape, 0)
            clicks = jnp.sum(jnp.where(row == core, clicks, 0.0), axis=0, keepdims=True)
        for ey in range(ny):
            to = lax.rem(y + ey, ny)
            out_ref = outs[ex * ny + ey]
            if last:
                columns = pl.ds(pl.multiple_of(to * share, share), share)
                b = (high_ref[:, columns], low_ref[:, columns])
                picked = jnp.zeros((1, share), jnp.float32)
                for yy in range(ny):
                    picked = jnp.where(to == yy, clicks[:, yy * share : (yy + 1) * share], picked)
                both = [dot3(halves(mat_ref[dx, o * rows : (o + 1) * rows, :]), b) for o in range(2)]
                out_ref[...] = jnp.where(picked == 1, both[1], both[0])
            else:
                at = pl.multiple_of(to * strip, strip)
                b = (high_ref[...], low_ref[...])
                both = [dot3(halves(mat_ref[dx, pl.ds(o * rows + at, strip), :]), b) for o in range(2)]
                out_ref[...] = jnp.where(clicks == 1, both[1], both[0])


def site_product(grid, site, clicks, mats, states, token=()):
    nx, ny, nz, rows, width, cols = grid.nx, grid.ny, grid.nz, grid.rows, grid.width, grid.cols
    last = site == grid.sites - 1
    shape = (rows, grid.share) if last else (grid.strip, cols)
    if grid.kernels:
        vmem, hbm = pl.BlockSpec(memory_space=pltpu.VMEM), pl.BlockSpec(memory_space=pl.ANY)
        tall = grid.rows * 2 + CLICK_ROWS
        flops = 2 * 3 * 2 * nx * rows * width * cols
        moved = 4 * (nx * tall * width + width * cols + nx * rows * cols)
        return pl.pallas_call(
            functools.partial(site_kernel, grid, site, last, len(token)),
            out_shape=[jax.ShapeDtypeStruct(shape, jnp.float32)] * (nx * ny),
            in_specs=[hbm] * (len(mats) + nz + len(token)),
            out_specs=[vmem] * (nx * ny),
            scratch_shapes=[
                pltpu.VMEM((nx, tall, width), jnp.float32),
                pltpu.VMEM((width, cols), jnp.float32),
                pltpu.VMEM((width, cols), jnp.bfloat16),
                pltpu.VMEM((width, cols), jnp.bfloat16),
                pltpu.SemaphoreType.DMA((nx,)),
                pltpu.SemaphoreType.DMA((nz,)),
            ],
            compiler_params=pltpu.CompilerParams(vmem_limit_bytes=32 * 1024 * 1024),
            cost_estimate=pl.CostEstimate(flops=flops, bytes_accessed=moved, transcendentals=0),
        )(*mats, *states, *token)
    z, _, y, core = grid.here()
    whole = jnp.zeros((width, cols), jnp.float32)
    for value, source in zip(states, grid.gathered_from(z)):
        whole = lax.dynamic_update_slice_in_dim(whole, value, source * grid.strip, 0)
    outs = []
    for ex in range(nx):
        dx = (nx - ex) % nx
        mat = 0
        for role, value in enumerate(mats):
            mat = jnp.where(core == role, value[site // grid.cores, dx], mat)
        both = jnp.dot(mat, whole, precision=lax.Precision.HIGH, preferred_element_type=jnp.float32)
        picked = jnp.where(clicks == 1, both[rows:], both[:rows])
        for ey in range(ny):
            axis = 1 if last else 0
            outs.append(lax.dynamic_slice_in_dim(picked, ((y + ey) % ny) * shape[axis], shape[axis], axis))
    return outs


def local(left_start, site_mats, clicks):
    sites, bonds = lax.axis_size("site"), lax.axis_size("bond")
    grid = Grid(sites, bonds, site_mats.shape[2], left_start.shape[1])
    nx, ny, nz, cores = grid.nx, grid.ny, grid.nz, grid.cores
    _, _, y, core = grid.here()
    pieces, state = pack(grid, clicks, site_mats[0], left_start)
    shifts = [(dx, dy) for dx in range(nx) for dy in range(ny)]

    own_clicks = {}
    if not grid.kernels:
        for dy in range(ny):
            for dcore in range(cores):
                own_clicks[dy, dcore] = grid.send(clicks, dy=dy, dcore=dcore) if dy or dcore else clicks

    def clicks_of(site):
        value = clicks
        for (dy, dcore), got in own_clicks.items():
            hit = ((y - site // cores) % ny == dy) & ((core - site % cores) % cores == dcore)
            value = jnp.where(hit, got, value)
        return own_samples(grid, value)

    def spread(which, pieces):
        got = {(dx, dy): grid.send(pieces[dx * ny + dy], dx=dx, dy=dy, cores=[which]) for dx, dy in shifts[:0:-1]}
        return {(0, 0): pieces[0], **got}

    mats = []
    for site in range(sites):
        gathered = grid.gather(state, relay=RELAY[min(site, 2)])
        token = []
        if site == 0:
            for which in range(cores):
                if which:
                    gathered[-1], later = lax.optimization_barrier((gathered[-1], pieces))
                mine = collect(grid, range(which, sites, cores), spread(which, later if which else pieces), gathered)
                others = [grid.send(mine, dcore=d, cores=[which]) for d in range(1, cores)]
                mats.append([([mine] + others)[(role - which) % cores] for role in range(cores)])
                token += [mine] if which else []
        outs = site_product(grid, site, clicks_of(site), mats[site % cores], gathered, token)
        state = outs[0]
        for ex, ey in shifts[:0:-1]:
            state = state + grid.send(outs[ex * ny + ey], dx=ex, dy=ey)
    return state


def solution(mesh):
    return jax.shard_map(
        local,
        mesh=mesh,
        in_specs=(P("bond", None), P("site", None, "bond", None), P("site", None)),
        out_specs=P("bond", "site"),
        check_vma=False,
    )
```

time: 187 us -> 175 us (0.936)
  starting transfers between devices: 33.2 us -> 26.1 us
  Pallas kernels: 16.2 us -> 13.5 us
  waiting for transfers between devices: 132 us -> 130 us
    ppermute x34 -> x32, starting transfers between devices: 33.2 us -> 26.1 us  [send(): return lax.ppermute(value, ('site', 'bond'), pairs)]
    pallas_call x1, Pallas kernels: 4.57 us -> 2.6 us  [pack(): pl.pallas_call(functools.partial(pack_kernel, grid), out_shape=[jax.Shape...]
    ppermute x34 -> x32, waiting for transfers between devices: 132 us -> 130 us  [send(): return lax.ppermute(value, ('site', 'bond'), pairs)]
  transfers between devices with their start and end apart: 34 -> 32, of which waited for: 24 -> 22; matrix products, arithmetic and copies ran while one was open for 0% -> 0% of each run, Pallas kernels for 3% -> 2%
where the time goes in v3:
time: 175 us; the launch traced here: 173 us
  waiting for transfers between devices  130 us (74%)
  starting transfers between devices  26.1 us (15%)
  Pallas kernels  13.5 us (8%)
  local copies, waits for them, and re-layouts  1.91 us (1%)
    ppermute x32, waiting for transfers between devices, send(): return lax.ppermute(value, ('site', 'bond'), pairs)  130 us
    ppermute x32, starting transfers between devices, send(): return lax.ppermute(value, ('site', 'bond'), pairs)  26.1 us
    pallas_call x4, Pallas kernels, site_product(): pl.pallas_call(functools.partial(site_kernel, grid, site, last, len(token...  9.94 us
  transfers between devices with their start and end apart: 32, of which 22 were waited for; matrix products, arithmetic and copies ran while one was open for 0% of the time, Pallas kernels for 2%

profile of v3, /device:TPU:25, one launch (start us, length us, event | category | flops | bytes accessed | tf_op | source)
XLA Modules:
  0.0 173.0 jit_solution(14943925378785913141)
XLA Ops:
  1.9 2.6 %shard_map.37 = (f32[520,512]{1,0:T(8,128)S(1)}, f32[520,512]{1,0:T(8,128)S(1)}, f32[520,512]{1,0:T(8,128)S(1)}, f32[520,512]{1,0:T(8,128)S(1)}, f32[128,512]{1,0:T(8,128)S(1)}) custom-call(s32[1,1024]{1,0:T(1,128)S(1)} %copy-done.1, f32[2,256,2048]{2,1,0:T(8,128)} %bitcast.1, f32[256,1024]{1,0:T(8,128)S(1)} %copy-done), custom_call_target="tpu_custom_call" | custom-call | bytes 8388608 | tf_op jit(solution)/shard_map/pallas_call | solution.py:124
  7.0 8.6 %collective-permute-done.refs_6_.refs_4_ = f32[128,512]{1,0:T(8,128)S(1)} collective-permute-done((f32[128,512]{1,0:T(8,128)S(1)}, f32[128,512]{1,0:T(8,128)S(1)}, u32[]{:S(2)}, u32[]{:S(2)}) %collective-permute-start) | collective-permute-done | bytes 262176 | tf_op jit(solution)/shard_map/ppermute | solution.py:47
  15.6 10.8 %collective-permute-done.1.refs_7_.refs_5_ = f32[128,512]{1,0:T(8,128)S(1)} collective-permute-done((f32[128,512]{1,0:T(8,128)S(1)}, f32[128,512]{1,0:T(8,128)S(1)}, u32[]{:S(2)}, u32[]{:S(2)}) %collective-permute-start.1) | collective-permute-done | bytes 262176 | tf_op jit(solution)/shard_map/ppermute | solution.py:47
  27.8 4.1 %collective-permute-start.2 = (f32[520,512]{1,0:T(8,128)S(1)}, f32[520,512]{1,0:T(8,128)S(1)}, u32[]{:S(2)}, u32[]{:S(2)}) collective-permute-start(f32[520,512]{1,0:T(8,128)S(1)} %get-tuple-element.37), channel_id=1, source_target_pairs={{8,25},{24,9},{9,24},{25,8},{10,27},{26,11},{11,26},{27,10},{12,29... | collective-permute-start | bytes 3194888 | tf_op jit(solution)/shard_map/ppermute | solution.py:47
  31.9 2.2 %collective-permute-start.3 = (f32[520,512]{1,0:T(8,128)S(1)}, f32[520,512]{1,0:T(8,128)S(1)}, u32[]{:S(2)}, u32[]{:S(2)}) collective-permute-start(f32[520,512]{1,0:T(8,128)S(1)} %get-tuple-element.38), channel_id=1, source_target_pairs={{8,9},{24,25},{9,8},{25,24},{10,11},{26,27},{11,10},{27,26},{12,13... | collective-permute-start | bytes 3194888 | tf_op jit(solution)/shard_map/ppermute | solution.py:47
  34.1 2.1 %collective-permute-start.4 = (f32[520,512]{1,0:T(8,128)S(1)}, f32[520,512]{1,0:T(8,128)S(1)}, u32[]{:S(2)}, u32[]{:S(2)}) collective-permute-start(f32[520,512]{1,0:T(8,128)S(1)} %get-tuple-element.39), channel_id=1, source_target_pairs={{8,24},{24,8},{9,25},{25,9},{10,26},{26,10},{11,27},{27,11},{12,28... | collective-permute-start | bytes 3194888 | tf_op jit(solution)/shard_map/ppermute | solution.py:47
  36.2 11.4 %collective-permute-done.2.refs_1_ = f32[520,512]{1,0:T(8,128)S(1)} collective-permute-done((f32[520,512]{1,0:T(8,128)S(1)}, f32[520,512]{1,0:T(8,128)S(1)}, u32[]{:S(2)}, u32[]{:S(2)}) %collective-permute-start.2) | collective-permute-done | bytes 1064992 | tf_op jit(solution)/shard_map/ppermute | solution.py:47
  47.7 15.3 %collective-permute-done.3.refs_2_ = f32[520,512]{1,0:T(8,128)S(1)} collective-permute-done((f32[520,512]{1,0:T(8,128)S(1)}, f32[520,512]{1,0:T(8,128)S(1)}, u32[]{:S(2)}, u32[]{:S(2)}) %collective-permute-start.3) | collective-permute-done | bytes 1064992 | tf_op jit(solution)/shard_map/ppermute | solution.py:47
  67.0 2.5 %shard_map.40 = (f32[128,512]{1,0:T(8,128)S(1)}, f32[128,512]{1,0:T(8,128)S(1)}, f32[128,512]{1,0:T(8,128)S(1)}, f32[128,512]{1,0:T(8,128)S(1)}) custom-call(f32[2,2,520,512]{3,2,1,0:T(8,128)S(1)} %shard_map.39.refs_0_, f32[2,2,520,512]{3,2,1,0:T(8,128)S(1)} %collective-permute-done.10.refs_1_, f32[128,512]{1,0:T(8,128)S(1)} %get-tuple-element.31.refs_4_.refs_2_, ...), custom_call_target="tpu_custom_call" | custom-call | flops 1610612736 | bytes 4227072 | tf_op jit(solution)/shard_map/pallas_call | solution.py:266
  69.6 2.3 %collective-permute-start.11 = (f32[128,512]{1,0:T(8,128)S(1)}, f32[128,512]{1,0:T(8,128)S(1)}, u32[]{:S(2)}, u32[]{:S(2)}) collective-permute-start(f32[128,512]{1,0:T(8,128)S(1)} %get-tuple-element.42), channel_id=1, source_target_pairs={{0,17},{8,25},{16,1},{24,9},{1,16},{9,24},{17,0},{25,8},{2,19},{10... | collective-permute-start | bytes 786440 | tf_op jit(solution)/shard_map/ppermute | solution.py:47
  72.3 3.6 %collective-permute-done.11 = f32[128,512]{1,0:T(8,128)S(1)} collective-permute-done((f32[128,512]{1,0:T(8,128)S(1)}, f32[128,512]{1,0:T(8,128)S(1)}, u32[]{:S(2)}, u32[]{:S(2)}) %collective-permute-start.11) | collective-permute-done | bytes 262176 | tf_op jit(solution)/shard_map/ppermute | solution.py:47
  75.8 3.2 %collective-permute-done.12 = f32[128,512]{1,0:T(8,128)S(1)} collective-permute-done((f32[128,512]{1,0:T(8,128)S(1)}, f32[128,512]{1,0:T(8,128)S(1)}, u32[]{:S(2)}, u32[]{:S(2)}) %collective-permute-start.12) | collective-permute-done | bytes 262176 | tf_op jit(solution)/shard_map/ppermute | solution.py:47
  79.4 8.1 %collective-permute-done.15.refs_4_ = f32[128,512]{1,0:T(8,128)S(1)} collective-permute-done((f32[128,512]{1,0:T(8,128)S(1)}, f32[128,512]{1,0:T(8,128)S(1)}, u32[]{:S(2)}, u32[]{:S(2)}) %collective-permute-start.15) | collective-permute-done | bytes 262176 | tf_op jit(solution)/shard_map/ppermute | solution.py:47
  87.5 5.5 %collective-permute-done.16.refs_5_ = f32[128,512]{1,0:T(8,128)S(1)} collective-permute-done((f32[128,512]{1,0:T(8,128)S(1)}, f32[128,512]{1,0:T(8,128)S(1)}, u32[]{:S(2)}, u32[]{:S(2)}) %collective-permute-start.16) | collective-permute-done | bytes 262176 | tf_op jit(solution)/shard_map/ppermute | solution.py:47
  93.0 2.5 %shard_map.41 = (f32[128,512]{1,0:T(8,128)S(1)}, f32[128,512]{1,0:T(8,128)S(1)}, f32[128,512]{1,0:T(8,128)S(1)}, f32[128,512]{1,0:T(8,128)S(1)}) custom-call(f32[2,2,520,512]{3,2,1,0:T(8,128)S(1)} %collective-permute-done.6.refs_0_, f32[2,2,520,512]{3,2,1,0:T(8,128)S(1)} %shard_map.38.refs_6_.refs_1_, f32[128,512]{1,0:T(8,128)S(1)} %add_add_fusion.3.refs_2_, ...), custom_call_target="tpu_custom_call" | custom-call | flops 1610612736 | bytes 4227072 | tf_op jit(solution)/shard_map/pallas_call | solution.py:266
  95.5 2.1 %collective-permute-start.17 = (f32[128,512]{1,0:T(8,128)S(1)}, f32[128,512]{1,0:T(8,128)S(1)}, u32[]{:S(2)}, u32[]{:S(2)}) collective-permute-start(f32[128,512]{1,0:T(8,128)S(1)} %get-tuple-element.46), channel_id=1, source_target_pairs={{0,17},{8,25},{16,1},{24,9},{1,16},{9,24},{17,0},{25,8},{2,19},{10... | collective-permute-start | bytes 786440 | tf_op jit(solution)/shard_map/ppermute | solution.py:47
  98.2 3.8 %collective-permute-done.17 = f32[128,512]{1,0:T(8,128)S(1)} collective-permute-done((f32[128,512]{1,0:T(8,128)S(1)}, f32[128,512]{1,0:T(8,128)S(1)}, u32[]{:S(2)}, u32[]{:S(2)}) %collective-permute-start.17) | collective-permute-done | bytes 262176 | tf_op jit(solution)/shard_map/ppermute | solution.py:47
  102.0 2.5 %collective-permute-done.18 = f32[128,512]{1,0:T(8,128)S(1)} collective-permute-done((f32[128,512]{1,0:T(8,128)S(1)}, f32[128,512]{1,0:T(8,128)S(1)}, u32[]{:S(2)}, u32[]{:S(2)}) %collective-permute-start.18) | collective-permute-done | bytes 262176 | tf_op jit(solution)/shard_map/ppermute | solution.py:47
  105.5 8.0 %collective-permute-done.21.refs_4_ = f32[128,512]{1,0:T(8,128)S(1)} collective-permute-done((f32[128,512]{1,0:T(8,128)S(1)}, f32[128,512]{1,0:T(8,128)S(1)}, u32[]{:S(2)}, u32[]{:S(2)}) %collective-permute-start.21) | collective-permute-done | bytes 262176 | tf_op jit(solution)/shard_map/ppermute | solution.py:47
  113.6 2.1 %collective-permute-done.20.refs_3_ = f32[128,512]{1,0:T(8,128)S(1)} collective-permute-done((f32[128,512]{1,0:T(8,128)S(1)}, f32[128,512]{1,0:T(8,128)S(1)}, u32[]{:S(2)}, u32[]{:S(2)}) %collective-permute-start.20) | collective-permute-done | bytes 262176 | tf_op jit(solution)/shard_map/ppermute | solution.py:47
  115.7 3.1 %collective-permute-done.22.refs_5_ = f32[128,512]{1,0:T(8,128)S(1)} collective-permute-done((f32[128,512]{1,0:T(8,128)S(1)}, f32[128,512]{1,0:T(8,128)S(1)}, u32[]{:S(2)}, u32[]{:S(2)}) %collective-permute-start.22) | collective-permute-done | bytes 262176 | tf_op jit(solution)/shard_map/ppermute | solution.py:47
  118.8 2.5 %shard_map.42 = (f32[128,512]{1,0:T(8,128)S(1)}, f32[128,512]{1,0:T(8,128)S(1)}, f32[128,512]{1,0:T(8,128)S(1)}, f32[128,512]{1,0:T(8,128)S(1)}) custom-call(f32[2,2,520,512]{3,2,1,0:T(8,128)S(1)} %shard_map.39.refs_0_, f32[2,2,520,512]{3,2,1,0:T(8,128)S(1)} %collective-permute-done.10.refs_1_, f32[128,512]{1,0:T(8,128)S(1)} %add_add_fusion.2.refs_2_, ...), custom_call_target="tpu_custom_call" | custom-call | flops 1610612736 | bytes 4227072 | tf_op jit(solution)/shard_map/pallas_call | solution.py:266
  121.3 2.1 %collective-permute-start.23 = (f32[128,512]{1,0:T(8,128)S(1)}, f32[128,512]{1,0:T(8,128)S(1)}, u32[]{:S(2)}, u32[]{:S(2)}) collective-permute-start(f32[128,512]{1,0:T(8,128)S(1)} %get-tuple-element.50), channel_id=1, source_target_pairs={{0,17},{8,25},{16,1},{24,9},{1,16},{9,24},{17,0},{25,8},{2,19},{10... | collective-permute-start | bytes 786440 | tf_op jit(solution)/shard_map/ppermute | solution.py:47
  124.0 6.3 %collective-permute-done.23 = f32[128,512]{1,0:T(8,128)S(1)} collective-permute-done((f32[128,512]{1,0:T(8,128)S(1)}, f32[128,512]{1,0:T(8,128)S(1)}, u32[]{:S(2)}, u32[]{:S(2)}) %collective-permute-start.23) | collective-permute-done | bytes 262176 | tf_op jit(solution)/shard_map/ppermute | solution.py:47
  130.4 3.3 %collective-permute-done.24 = f32[128,512]{1,0:T(8,128)S(1)} collective-permute-done((f32[128,512]{1,0:T(8,128)S(1)}, f32[128,512]{1,0:T(8,128)S(1)}, u32[]{:S(2)}, u32[]{:S(2)}) %collective-permute-start.24) | collective-permute-done | bytes 262176 | tf_op jit(solution)/shard_map/ppermute | solution.py:47
  134.1 13.5 %collective-permute-done.27.refs_4_ = f32[128,512]{1,0:T(8,128)S(1)} collective-permute-done((f32[128,512]{1,0:T(8,128)S(1)}, f32[128,512]{1,0:T(8,128)S(1)}, u32[]{:S(2)}, u32[]{:S(2)}) %collective-permute-start.27) | collective-permute-done | bytes 262176 | tf_op jit(solution)/shard_map/ppermute | solution.py:47
  147.6 7.3 %collective-permute-done.28.refs_5_ = f32[128,512]{1,0:T(8,128)S(1)} collective-permute-done((f32[128,512]{1,0:T(8,128)S(1)}, f32[128,512]{1,0:T(8,128)S(1)}, u32[]{:S(2)}, u32[]{:S(2)}) %collective-permute-start.28) | collective-permute-done | bytes 262176 | tf_op jit(solution)/shard_map/ppermute | solution.py:47
  154.9 2.5 %shard_map.43 = (f32[256,256]{1,0:T(8,128)S(1)}, f32[256,256]{1,0:T(8,128)S(1)}, f32[256,256]{1,0:T(8,128)S(1)}, f32[256,256]{1,0:T(8,128)S(1)}) custom-call(f32[2,2,520,512]{3,2,1,0:T(8,128)S(1)} %collective-permute-done.6.refs_0_, f32[2,2,520,512]{3,2,1,0:T(8,128)S(1)} %shard_map.38.refs_6_.refs_1_, f32[128,512]{1,0:T(8,128)S(1)} %add_add_fusion.1.refs_2_, ...), custom_call_target="tpu_custom_call" | custom-call | flops 1610612736 | bytes 4227072 | tf_op jit(solution)/shard_map/pallas_call | solution.py:266
  157.4 1.9 %collective-permute-start.29 = (f32[256,256]{1,0:T(8,128)S(1)}, f32[256,256]{1,0:T(8,128)S(1)}, u32[]{:S(2)}, u32[]{:S(2)}) collective-permute-start(f32[256,256]{1,0:T(8,128)S(1)} %get-tuple-element.54), channel_id=1, source_target_pairs={{0,17},{8,25},{16,1},{24,9},{1,16},{9,24},{17,0},{25,8},{2,19},{10... | collective-permute-start | bytes 786440 | tf_op jit(solution)/shard_map/ppermute | solution.py:47
  160.1 4.7 %collective-permute-done.29 = f32[256,256]{1,0:T(8,128)S(1)} collective-permute-done((f32[256,256]{1,0:T(8,128)S(1)}, f32[256,256]{1,0:T(8,128)S(1)}, u32[]{:S(2)}, u32[]{:S(2)}) %collective-permute-start.29) | collective-permute-done | bytes 262176 | tf_op jit(solution)/shard_map/ppermute | solution.py:47
  164.8 5.4 %collective-permute-done.30 = f32[256,256]{1,0:T(8,128)S(1)} collective-permute-done((f32[256,256]{1,0:T(8,128)S(1)}, f32[256,256]{1,0:T(8,128)S(1)}, u32[]{:S(2)}, u32[]{:S(2)}) %collective-permute-start.30) | collective-permute-done | bytes 262176 | tf_op jit(solution)/shard_map/ppermute | solution.py:47
  170.2 2.0 %collective-permute-done.31 = f32[256,256]{1,0:T(8,128)S(1)} collective-permute-done((f32[256,256]{1,0:T(8,128)S(1)}, f32[256,256]{1,0:T(8,128)S(1)}, u32[]{:S(2)}, u32[]{:S(2)}) %collective-permute-start.31) | collective-permute-done | bytes 262176 | tf_op jit(solution)/shard_map/ppermute | solution.py:47
  (47 shorter events, 14.8 us)
Async XLA Ops:
  4.5 21.9 %collective-permute-start.9 = (f32[520,512]{1,0:T(8,128)S(1)}, f32[520,512]{1,0:T(8,128)S(1)}, u32[]{:S(2)}, u32[]{:S(2)}) collective-permute-start(f32[520,512]{1,0:T(8,128)S(1)} %get-tuple-element.39), channel_id=1, source_target_pairs={{0,16},{16,0},{1,17},{17,1},{2,18},{18,2},{3,19},{19,3},{4,20},{20... | collective-permute-start | bytes 3194888 | tf_op jit(solution)/shard_map/ppermute | solution.py:47
  5.3 21.2 %collective-permute-start.8 = (f32[520,512]{1,0:T(8,128)S(1)}, f32[520,512]{1,0:T(8,128)S(1)}, u32[]{:S(2)}, u32[]{:S(2)}) collective-permute-start(f32[520,512]{1,0:T(8,128)S(1)} %get-tuple-element.38), channel_id=1, source_target_pairs={{0,1},{16,17},{1,0},{17,16},{2,3},{18,19},{3,2},{19,18},{4,5},{20,... | collective-permute-start | bytes 3194888 | tf_op jit(solution)/shard_map/ppermute | solution.py:47
  6.0 20.4 %collective-permute-start.7 = (f32[520,512]{1,0:T(8,128)S(1)}, f32[520,512]{1,0:T(8,128)S(1)}, u32[]{:S(2)}, u32[]{:S(2)}) collective-permute-start(f32[520,512]{1,0:T(8,128)S(1)} %get-tuple-element.37), channel_id=1, source_target_pairs={{0,17},{16,1},{1,16},{17,0},{2,19},{18,3},{3,18},{19,2},{4,21},{20... | collective-permute-start | bytes 3194888 | tf_op jit(solution)/shard_map/ppermute | solution.py:47
  6.7 8.9 %collective-permute-start = (f32[128,512]{1,0:T(8,128)S(1)}, f32[128,512]{1,0:T(8,128)S(1)}, u32[]{:S(2)}, u32[]{:S(2)}) collective-permute-start(f32[128,512]{1,0:T(8,128)S(1)} %get-tuple-element.31.refs_4_.refs_2_), channel_id=1, source_target_pairs={{0,4},{8,12},{16,20},{24,28},{1,5},{9,13},{17,21},{25,29},{2,6},{1... | collective-permute-start | bytes 786440 | tf_op jit(solution)/shard_map/ppermute | solution.py:47
  6.9 8.8 %collective-permute-start.5 = (f32[128,512]{1,0:T(8,128)S(1)}, f32[128,512]{1,0:T(8,128)S(1)}, u32[]{:S(2)}, u32[]{:S(2)}) collective-permute-start(f32[128,512]{1,0:T(8,128)S(1)} %get-tuple-element.31.refs_4_.refs_2_), channel_id=1, source_target_pairs={{0,2},{8,10},{16,18},{24,26},{1,3},{9,11},{17,19},{25,27},{2,0},{1... | collective-permute-start | bytes 786440 | tf_op jit(solution)/shard_map/ppermute | solution.py:47
  15.6 10.8 %collective-permute-start.1 = (f32[128,512]{1,0:T(8,128)S(1)}, f32[128,512]{1,0:T(8,128)S(1)}, u32[]{:S(2)}, u32[]{:S(2)}) collective-permute-start(f32[128,512]{1,0:T(8,128)S(1)} %collective-permute-done.refs_6_.refs_4_), channel_id=1, source_target_pairs={{0,2},{8,10},{16,18},{24,26},{1,3},{9,11},{17,19},{25,27},{2,0},{1... | collective-permute-start | bytes 786440 | tf_op jit(solution)/shard_map/ppermute | solution.py:47
  26.5 40.5 %collective-permute-start.10 = (f32[2,2,520,512]{3,2,1,0:T(8,128)S(1)}, f32[2,2,520,512]{3,2,1,0:T(8,128)S(1)}, u32[]{:S(2)}, u32[]{:S(2)}) collective-permute-start(f32[2,2,520,512]{3,2,1,0:T(8,128)S(1)} %shard_map.39.refs_0_), channel_id=1, source_target_pairs={{0,8},{16,24},{1,9},{17,25},{2,10},{18,26},{3,11},{19,27},{4,12},{... | collective-permute-start | bytes 12779528 | tf_op jit(solution)/shard_map/ppermute | solution.py:47
  27.8 19.8 %collective-permute-start.2 = (f32[520,512]{1,0:T(8,128)S(1)}, f32[520,512]{1,0:T(8,128)S(1)}, u32[]{:S(2)}, u32[]{:S(2)}) collective-permute-start(f32[520,512]{1,0:T(8,128)S(1)} %get-tuple-element.37), channel_id=1, source_target_pairs={{8,25},{24,9},{9,24},{25,8},{10,27},{26,11},{11,26},{27,10},{12,29... | collective-permute-start | bytes 3194888 | tf_op jit(solution)/shard_map/ppermute | solution.py:47
  31.9 31.1 %collective-permute-start.3 = (f32[520,512]{1,0:T(8,128)S(1)}, f32[520,512]{1,0:T(8,128)S(1)}, u32[]{:S(2)}, u32[]{:S(2)}) collective-permute-start(f32[520,512]{1,0:T(8,128)S(1)} %get-tuple-element.38), channel_id=1, source_target_pairs={{8,9},{24,25},{9,8},{25,24},{10,11},{26,27},{11,10},{27,26},{12,13... | collective-permute-start | bytes 3194888 | tf_op jit(solution)/shard_map/ppermute | solution.py:47
  34.1 30.5 %collective-permute-start.4 = (f32[520,512]{1,0:T(8,128)S(1)}, f32[520,512]{1,0:T(8,128)S(1)}, u32[]{:S(2)}, u32[]{:S(2)}) collective-permute-start(f32[520,512]{1,0:T(8,128)S(1)} %get-tuple-element.39), channel_id=1, source_target_pairs={{8,24},{24,8},{9,25},{25,9},{10,26},{26,10},{11,27},{27,11},{12,28... | collective-permute-start | bytes 3194888 | tf_op jit(solution)/shard_map/ppermute | solution.py:47
  65.5 22.1 %collective-permute-start.6 = (f32[2,2,520,512]{3,2,1,0:T(8,128)S(1)}, f32[2,2,520,512]{3,2,1,0:T(8,128)S(1)}, u32[]{:S(2)}, u32[]{:S(2)}) collective-permute-start(f32[2,2,520,512]{3,2,1,0:T(8,128)S(1)} %shard_map.38.refs_6_.refs_1_), channel_id=1, source_target_pairs={{8,0},{24,16},{9,1},{25,17},{10,2},{26,18},{11,3},{27,19},{12,4},{... | collective-permute-start | bytes 12779528 | tf_op jit(solution)/shard_map/ppermute | solution.py:47
  69.6 6.3 %collective-permute-start.11 = (f32[128,512]{1,0:T(8,128)S(1)}, f32[128,512]{1,0:T(8,128)S(1)}, u32[]{:S(2)}, u32[]{:S(2)}) collective-permute-start(f32[128,512]{1,0:T(8,128)S(1)} %get-tuple-element.42), channel_id=1, source_target_pairs={{0,17},{8,25},{16,1},{24,9},{1,16},{9,24},{17,0},{25,8},{2,19},{10... | collective-permute-start | bytes 786440 | tf_op jit(solution)/shard_map/ppermute | solution.py:47
  71.8 7.2 %collective-permute-start.12 = (f32[128,512]{1,0:T(8,128)S(1)}, f32[128,512]{1,0:T(8,128)S(1)}, u32[]{:S(2)}, u32[]{:S(2)}) collective-permute-start(f32[128,512]{1,0:T(8,128)S(1)} %get-tuple-element.43), channel_id=1, source_target_pairs={{0,1},{8,9},{16,17},{24,25},{1,0},{9,8},{17,16},{25,24},{2,3},{10,... | collective-permute-start | bytes 786440 | tf_op jit(solution)/shard_map/ppermute | solution.py:47
  72.1 6.9 %collective-permute-start.13 = (f32[128,512]{1,0:T(8,128)S(1)}, f32[128,512]{1,0:T(8,128)S(1)}, u32[]{:S(2)}, u32[]{:S(2)}) collective-permute-start(f32[128,512]{1,0:T(8,128)S(1)} %get-tuple-element.44), channel_id=1, source_target_pairs={{0,16},{8,24},{16,0},{24,8},{1,17},{9,25},{17,1},{25,9},{2,18},{10... | collective-permute-start | bytes 786440 | tf_op jit(solution)/shard_map/ppermute | solution.py:47
  79.1 8.4 %collective-permute-start.15 = (f32[128,512]{1,0:T(8,128)S(1)}, f32[128,512]{1,0:T(8,128)S(1)}, u32[]{:S(2)}, u32[]{:S(2)}) collective-permute-start(f32[128,512]{1,0:T(8,128)S(1)} %add_add_fusion.3.refs_2_), channel_id=1, source_target_pairs={{0,4},{8,12},{16,20},{24,28},{1,5},{9,13},{17,21},{25,29},{2,6},{1... | collective-permute-start | bytes 786440 | tf_op jit(solution)/shard_map/ppermute | solution.py:47
  79.2 8.3 %collective-permute-start.14 = (f32[128,512]{1,0:T(8,128)S(1)}, f32[128,512]{1,0:T(8,128)S(1)}, u32[]{:S(2)}, u32[]{:S(2)}) collective-permute-start(f32[128,512]{1,0:T(8,128)S(1)} %add_add_fusion.3.refs_2_), channel_id=1, source_target_pairs={{0,2},{8,10},{16,18},{24,26},{1,3},{9,11},{17,19},{25,27},{2,0},{1... | collective-permute-start | bytes 786440 | tf_op jit(solution)/shard_map/ppermute | solution.py:47
  87.5 5.5 %collective-permute-start.16 = (f32[128,512]{1,0:T(8,128)S(1)}, f32[128,512]{1,0:T(8,128)S(1)}, u32[]{:S(2)}, u32[]{:S(2)}) collective-permute-start(f32[128,512]{1,0:T(8,128)S(1)} %collective-permute-done.15.refs_4_), channel_id=1, source_target_pairs={{0,2},{8,10},{16,18},{24,26},{1,3},{9,11},{17,19},{25,27},{2,0},{1... | collective-permute-start | bytes 786440 | tf_op jit(solution)/shard_map/ppermute | solution.py:47
  95.5 6.5 %collective-permute-start.17 = (f32[128,512]{1,0:T(8,128)S(1)}, f32[128,512]{1,0:T(8,128)S(1)}, u32[]{:S(2)}, u32[]{:S(2)}) collective-permute-start(f32[128,512]{1,0:T(8,128)S(1)} %get-tuple-element.46), channel_id=1, source_target_pairs={{0,17},{8,25},{16,1},{24,9},{1,16},{9,24},{17,0},{25,8},{2,19},{10... | collective-permute-start | bytes 786440 | tf_op jit(solution)/shard_map/ppermute | solution.py:47
  97.6 6.9 %collective-permute-start.18 = (f32[128,512]{1,0:T(8,128)S(1)}, f32[128,512]{1,0:T(8,128)S(1)}, u32[]{:S(2)}, u32[]{:S(2)}) collective-permute-start(f32[128,512]{1,0:T(8,128)S(1)} %get-tuple-element.47), channel_id=1, source_target_pairs={{0,1},{8,9},{16,17},{24,25},{1,0},{9,8},{17,16},{25,24},{2,3},{10,... | collective-permute-start | bytes 786440 | tf_op jit(solution)/shard_map/ppermute | solution.py:47
  97.9 6.6 %collective-permute-start.19 = (f32[128,512]{1,0:T(8,128)S(1)}, f32[128,512]{1,0:T(8,128)S(1)}, u32[]{:S(2)}, u32[]{:S(2)}) collective-permute-start(f32[128,512]{1,0:T(8,128)S(1)} %get-tuple-element.48), channel_id=1, source_target_pairs={{0,16},{8,24},{16,0},{24,8},{1,17},{9,25},{17,1},{25,9},{2,18},{10... | collective-permute-start | bytes 786440 | tf_op jit(solution)/shard_map/ppermute | solution.py:47
  104.6 9.0 %collective-permute-start.21 = (f32[128,512]{1,0:T(8,128)S(1)}, f32[128,512]{1,0:T(8,128)S(1)}, u32[]{:S(2)}, u32[]{:S(2)}) collective-permute-start(f32[128,512]{1,0:T(8,128)S(1)} %add_add_fusion.2.refs_2_), channel_id=1, source_target_pairs={{0,4},{8,12},{16,20},{24,28},{1,5},{9,13},{17,21},{25,29},{2,6},{1... | collective-permute-start | bytes 786440 | tf_op jit(solution)/shard_map/ppermute | solution.py:47
  104.7 11.0 %collective-permute-start.20 = (f32[128,512]{1,0:T(8,128)S(1)}, f32[128,512]{1,0:T(8,128)S(1)}, u32[]{:S(2)}, u32[]{:S(2)}) collective-permute-start(f32[128,512]{1,0:T(8,128)S(1)} %add_add_fusion.2.refs_2_), channel_id=1, source_target_pairs={{0,2},{8,10},{16,18},{24,26},{1,3},{9,11},{17,19},{25,27},{2,0},{1... | collective-permute-start | bytes 786440 | tf_op jit(solution)/shard_map/ppermute | solution.py:47
  113.6 5.2 %collective-permute-start.22 = (f32[128,512]{1,0:T(8,128)S(1)}, f32[128,512]{1,0:T(8,128)S(1)}, u32[]{:S(2)}, u32[]{:S(2)}) collective-permute-start(f32[128,512]{1,0:T(8,128)S(1)} %collective-permute-done.21.refs_4_), channel_id=1, source_target_pairs={{0,2},{8,10},{16,18},{24,26},{1,3},{9,11},{17,19},{25,27},{2,0},{1... | collective-permute-start | bytes 786440 | tf_op jit(solution)/shard_map/ppermute | solution.py:47
  121.3 9.1 %collective-permute-start.23 = (f32[128,512]{1,0:T(8,128)S(1)}, f32[128,512]{1,0:T(8,128)S(1)}, u32[]{:S(2)}, u32[]{:S(2)}) collective-permute-start(f32[128,512]{1,0:T(8,128)S(1)} %get-tuple-element.50), channel_id=1, source_target_pairs={{0,17},{8,25},{16,1},{24,9},{1,16},{9,24},{17,0},{25,8},{2,19},{10... | collective-permute-start | bytes 786440 | tf_op jit(solution)/shard_map/ppermute | solution.py:47
  123.4 10.3 %collective-permute-start.24 = (f32[128,512]{1,0:T(8,128)S(1)}, f32[128,512]{1,0:T(8,128)S(1)}, u32[]{:S(2)}, u32[]{:S(2)}) collective-permute-start(f32[128,512]{1,0:T(8,128)S(1)} %get-tuple-element.51), channel_id=1, source_target_pairs={{0,1},{8,9},{16,17},{24,25},{1,0},{9,8},{17,16},{25,24},{2,3},{10,... | collective-permute-start | bytes 786440 | tf_op jit(solution)/shard_map/ppermute | solution.py:47
  123.7 10.1 %collective-permute-start.25 = (f32[128,512]{1,0:T(8,128)S(1)}, f32[128,512]{1,0:T(8,128)S(1)}, u32[]{:S(2)}, u32[]{:S(2)}) collective-permute-start(f32[128,512]{1,0:T(8,128)S(1)} %get-tuple-element.52), channel_id=1, source_target_pairs={{0,16},{8,24},{16,0},{24,8},{1,17},{9,25},{17,1},{25,9},{2,18},{10... | collective-permute-start | bytes 786440 | tf_op jit(solution)/shard_map/ppermute | solution.py:47
  133.8 13.8 %collective-permute-start.27 = (f32[128,512]{1,0:T(8,128)S(1)}, f32[128,512]{1,0:T(8,128)S(1)}, u32[]{:S(2)}, u32[]{:S(2)}) collective-permute-start(f32[128,512]{1,0:T(8,128)S(1)} %add_add_fusion.1.refs_2_), channel_id=1, source_target_pairs={{0,4},{8,12},{16,20},{24,28},{1,5},{9,13},{17,21},{25,29},{2,6},{1... | collective-permute-start | bytes 786440 | tf_op jit(solution)/shard_map/ppermute | solution.py:47
  133.9 13.7 %collective-permute-start.26 = (f32[128,512]{1,0:T(8,128)S(1)}, f32[128,512]{1,0:T(8,128)S(1)}, u32[]{:S(2)}, u32[]{:S(2)}) collective-permute-start(f32[128,512]{1,0:T(8,128)S(1)} %add_add_fusion.1.refs_2_), channel_id=1, source_target_pairs={{0,2},{8,10},{16,18},{24,26},{1,3},{9,11},{17,19},{25,27},{2,0},{1... | collective-permute-start | bytes 786440 | tf_op jit(solution)/shard_map/ppermute | solution.py:47
  147.6 7.3 %collective-permute-start.28 = (f32[128,512]{1,0:T(8,128)S(1)}, f32[128,512]{1,0:T(8,128)S(1)}, u32[]{:S(2)}, u32[]{:S(2)}) collective-permute-start(f32[128,512]{1,0:T(8,128)S(1)} %collective-permute-done.27.refs_4_), channel_id=1, source_target_pairs={{0,2},{8,10},{16,18},{24,26},{1,3},{9,11},{17,19},{25,27},{2,0},{1... | collective-permute-start | bytes 786440 | tf_op jit(solution)/shard_map/ppermute | solution.py:47
  157.4 7.4 %collective-permute-start.29 = (f32[256,256]{1,0:T(8,128)S(1)}, f32[256,256]{1,0:T(8,128)S(1)}, u32[]{:S(2)}, u32[]{:S(2)}) collective-permute-start(f32[256,256]{1,0:T(8,128)S(1)} %get-tuple-element.54), channel_id=1, source_target_pairs={{0,17},{8,25},{16,1},{24,9},{1,16},{9,24},{17,0},{25,8},{2,19},{10... | collective-permute-start | bytes 786440 | tf_op jit(solution)/shard_map/ppermute | solution.py:47
  159.3 10.9 %collective-permute-start.30 = (f32[256,256]{1,0:T(8,128)S(1)}, f32[256,256]{1,0:T(8,128)S(1)}, u32[]{:S(2)}, u32[]{:S(2)}) collective-permute-start(f32[256,256]{1,0:T(8,128)S(1)} %get-tuple-element.55), channel_id=1, source_target_pairs={{0,1},{8,9},{16,17},{24,25},{1,0},{9,8},{17,16},{25,24},{2,3},{10,... | collective-permute-start | bytes 786440 | tf_op jit(solution)/shard_map/ppermute | solution.py:47
  159.6 12.6 %collective-permute-start.31 = (f32[256,256]{1,0:T(8,128)S(1)}, f32[256,256]{1,0:T(8,128)S(1)}, u32[]{:S(2)}, u32[]{:S(2)}) collective-permute-start(f32[256,256]{1,0:T(8,128)S(1)} %get-tuple-element.56), channel_id=1, source_target_pairs={{0,16},{8,24},{16,0},{24,8},{1,17},{9,25},{17,1},{25,9},{2,18},{10... | collective-permute-start | bytes 786440 | tf_op jit(solution)/shard_map/ppermute | solution.py:47
  (2 other events, 1.9 us)

commit v4 on v3

--- a/solution.py
+++ b/solution.py
@@ -10,7 +10,7 @@
 
 CLICK_ROWS = 8
 PACK_VMEM = 48 * 1024 * 1024
-RELAY = (True, True, True)
+RELAY = (True, True, False, True)
 
 
 class Grid:
@@ -324,7 +324,7 @@
 
     mats = []
     for site in range(sites):
-        gathered = grid.gather(state, relay=RELAY[min(site, 2)])
+        gathered = grid.gather(state, relay=RELAY[min(site, 3)])
         token = []
         if site == 0:
             for which in range(cores):

time: 175 us -> 171 us (0.977)
  waiting for transfers between devices: 130 us -> 125 us
  starting transfers between devices: 26.1 us -> 28.6 us
    ppermute x32, waiting for transfers between devices: 130 us -> 125 us  [send(): return lax.ppermute(value, ('site', 'bond'), pairs)]
    ppermute x32, starting transfers between devices: 26.1 us -> 28.6 us  [send(): return lax.ppermute(value, ('site', 'bond'), pairs)]
where the time goes in v4:
time: 171 us
  waiting for transfers between devices  125 us (73%)
  starting transfers between devices  28.6 us (17%)
  Pallas kernels  13.5 us (8%)
  local copies, waits for them, and re-layouts  1.91 us (1%)
    ppermute x32, waiting for transfers between devices, send(): return lax.ppermute(value, ('site', 'bond'), pairs)  125 us
    ppermute x32, starting transfers between devices, send(): return lax.ppermute(value, ('site', 'bond'), pairs)  28.6 us
    pallas_call x4, Pallas kernels, site_product(): pl.pallas_call(functools.partial(site_kernel, grid, site, last, len(token...  9.94 us
  transfers between devices with their start and end apart: 32, of which 22 were waited for; matrix products, arithmetic and copies ran while one was open for 0% of the time, Pallas kernels for 2%

profile of v4, /device:TPU:25, one launch (start us, length us, event | category | flops | bytes accessed | tf_op | source)
XLA Modules:
  0.0 170.7 jit_solution(2262076456876513712)
XLA Ops:
  1.9 2.6 %shard_map.37 = (f32[520,512]{1,0:T(8,128)S(1)}, f32[520,512]{1,0:T(8,128)S(1)}, f32[520,512]{1,0:T(8,128)S(1)}, f32[520,512]{1,0:T(8,128)S(1)}, f32[128,512]{1,0:T(8,128)S(1)}) custom-call(s32[1,1024]{1,0:T(1,128)S(1)} %copy-done.1, f32[2,256,2048]{2,1,0:T(8,128)} %bitcast.1, f32[256,1024]{1,0:T(8,128)S(1)} %copy-done), custom_call_target="tpu_custom_call" | custom-call | bytes 8388608 | tf_op jit(solution)/shard_map/pallas_call | solution.py:124
  7.0 8.6 %collective-permute-done.refs_6_.refs_4_ = f32[128,512]{1,0:T(8,128)S(1)} collective-permute-done((f32[128,512]{1,0:T(8,128)S(1)}, f32[128,512]{1,0:T(8,128)S(1)}, u32[]{:S(2)}, u32[]{:S(2)}) %collective-permute-start) | collective-permute-done | bytes 262176 | tf_op jit(solution)/shard_map/ppermute | solution.py:47
  15.6 10.8 %collective-permute-done.1.refs_7_.refs_5_ = f32[128,512]{1,0:T(8,128)S(1)} collective-permute-done((f32[128,512]{1,0:T(8,128)S(1)}, f32[128,512]{1,0:T(8,128)S(1)}, u32[]{:S(2)}, u32[]{:S(2)}) %collective-permute-start.1) | collective-permute-done | bytes 262176 | tf_op jit(solution)/shard_map/ppermute | solution.py:47
  27.8 4.1 %collective-permute-start.2 = (f32[520,512]{1,0:T(8,128)S(1)}, f32[520,512]{1,0:T(8,128)S(1)}, u32[]{:S(2)}, u32[]{:S(2)}) collective-permute-start(f32[520,512]{1,0:T(8,128)S(1)} %get-tuple-element.37), channel_id=1, source_target_pairs={{8,25},{24,9},{9,24},{25,8},{10,27},{26,11},{11,26},{27,10},{12,29... | collective-permute-start | bytes 3194888 | tf_op jit(solution)/shard_map/ppermute | solution.py:47
  31.9 2.2 %collective-permute-start.3 = (f32[520,512]{1,0:T(8,128)S(1)}, f32[520,512]{1,0:T(8,128)S(1)}, u32[]{:S(2)}, u32[]{:S(2)}) collective-permute-start(f32[520,512]{1,0:T(8,128)S(1)} %get-tuple-element.38), channel_id=1, source_target_pairs={{8,9},{24,25},{9,8},{25,24},{10,11},{26,27},{11,10},{27,26},{12,13... | collective-permute-start | bytes 3194888 | tf_op jit(solution)/shard_map/ppermute | solution.py:47
  34.1 2.1 %collective-permute-start.4 = (f32[520,512]{1,0:T(8,128)S(1)}, f32[520,512]{1,0:T(8,128)S(1)}, u32[]{:S(2)}, u32[]{:S(2)}) collective-permute-start(f32[520,512]{1,0:T(8,128)S(1)} %get-tuple-element.39), channel_id=1, source_target_pairs={{8,24},{24,8},{9,25},{25,9},{10,26},{26,10},{11,27},{27,11},{12,28... | collective-permute-start | bytes 3194888 | tf_op jit(solution)/shard_map/ppermute | solution.py:47
  36.2 11.4 %collective-permute-done.2.refs_1_ = f32[520,512]{1,0:T(8,128)S(1)} collective-permute-done((f32[520,512]{1,0:T(8,128)S(1)}, f32[520,512]{1,0:T(8,128)S(1)}, u32[]{:S(2)}, u32[]{:S(2)}) %collective-permute-start.2) | collective-permute-done | bytes 1064992 | tf_op jit(solution)/shard_map/ppermute | solution.py:47
  47.7 15.3 %collective-permute-done.3.refs_2_ = f32[520,512]{1,0:T(8,128)S(1)} collective-permute-done((f32[520,512]{1,0:T(8,128)S(1)}, f32[520,512]{1,0:T(8,128)S(1)}, u32[]{:S(2)}, u32[]{:S(2)}) %collective-permute-start.3) | collective-permute-done | bytes 1064992 | tf_op jit(solution)/shard_map/ppermute | solution.py:47
  67.0 2.5 %shard_map.40 = (f32[128,512]{1,0:T(8,128)S(1)}, f32[128,512]{1,0:T(8,128)S(1)}, f32[128,512]{1,0:T(8,128)S(1)}, f32[128,512]{1,0:T(8,128)S(1)}) custom-call(f32[2,2,520,512]{3,2,1,0:T(8,128)S(1)} %shard_map.39.refs_0_, f32[2,2,520,512]{3,2,1,0:T(8,128)S(1)} %collective-permute-done.10.refs_1_, f32[128,512]{1,0:T(8,128)S(1)} %get-tuple-element.31.refs_4_.refs_2_, ...), custom_call_target="tpu_custom_call" | custom-call | flops 1610612736 | bytes 4227072 | tf_op jit(solution)/shard_map/pallas_call | solution.py:266
  69.6 2.3 %collective-permute-start.11 = (f32[128,512]{1,0:T(8,128)S(1)}, f32[128,512]{1,0:T(8,128)S(1)}, u32[]{:S(2)}, u32[]{:S(2)}) collective-permute-start(f32[128,512]{1,0:T(8,128)S(1)} %get-tuple-element.42), channel_id=1, source_target_pairs={{0,17},{8,25},{16,1},{24,9},{1,16},{9,24},{17,0},{25,8},{2,19},{10... | collective-permute-start | bytes 786440 | tf_op jit(solution)/shard_map/ppermute | solution.py:47
  72.3 3.6 %collective-permute-done.11 = f32[128,512]{1,0:T(8,128)S(1)} collective-permute-done((f32[128,512]{1,0:T(8,128)S(1)}, f32[128,512]{1,0:T(8,128)S(1)}, u32[]{:S(2)}, u32[]{:S(2)}) %collective-permute-start.11) | collective-permute-done | bytes 262176 | tf_op jit(solution)/shard_map/ppermute | solution.py:47
  75.8 3.2 %collective-permute-done.12 = f32[128,512]{1,0:T(8,128)S(1)} collective-permute-done((f32[128,512]{1,0:T(8,128)S(1)}, f32[128,512]{1,0:T(8,128)S(1)}, u32[]{:S(2)}, u32[]{:S(2)}) %collective-permute-start.12) | collective-permute-done | bytes 262176 | tf_op jit(solution)/shard_map/ppermute | solution.py:47
  79.4 8.1 %collective-permute-done.15.refs_4_ = f32[128,512]{1,0:T(8,128)S(1)} collective-permute-done((f32[128,512]{1,0:T(8,128)S(1)}, f32[128,512]{1,0:T(8,128)S(1)}, u32[]{:S(2)}, u32[]{:S(2)}) %collective-permute-start.15) | collective-permute-done | bytes 262176 | tf_op jit(solution)/shard_map/ppermute | solution.py:47
  87.5 5.5 %collective-permute-done.16.refs_5_ = f32[128,512]{1,0:T(8,128)S(1)} collective-permute-done((f32[128,512]{1,0:T(8,128)S(1)}, f32[128,512]{1,0:T(8,128)S(1)}, u32[]{:S(2)}, u32[]{:S(2)}) %collective-permute-start.16) | collective-permute-done | bytes 262176 | tf_op jit(solution)/shard_map/ppermute | solution.py:47
  93.0 2.5 %shard_map.41 = (f32[128,512]{1,0:T(8,128)S(1)}, f32[128,512]{1,0:T(8,128)S(1)}, f32[128,512]{1,0:T(8,128)S(1)}, f32[128,512]{1,0:T(8,128)S(1)}) custom-call(f32[2,2,520,512]{3,2,1,0:T(8,128)S(1)} %collective-permute-done.6.refs_0_, f32[2,2,520,512]{3,2,1,0:T(8,128)S(1)} %shard_map.38.refs_6_.refs_1_, f32[128,512]{1,0:T(8,128)S(1)} %add_add_fusion.3.refs_2_, ...), custom_call_target="tpu_custom_call" | custom-call | flops 1610612736 | bytes 4227072 | tf_op jit(solution)/shard_map/pallas_call | solution.py:266
  95.5 2.1 %collective-permute-start.17 = (f32[128,512]{1,0:T(8,128)S(1)}, f32[128,512]{1,0:T(8,128)S(1)}, u32[]{:S(2)}, u32[]{:S(2)}) collective-permute-start(f32[128,512]{1,0:T(8,128)S(1)} %get-tuple-element.46), channel_id=1, source_target_pairs={{0,17},{8,25},{16,1},{24,9},{1,16},{9,24},{17,0},{25,8},{2,19},{10... | collective-permute-start | bytes 786440 | tf_op jit(solution)/shard_map/ppermute | solution.py:47
  98.2 3.8 %collective-permute-done.17 = f32[128,512]{1,0:T(8,128)S(1)} collective-permute-done((f32[128,512]{1,0:T(8,128)S(1)}, f32[128,512]{1,0:T(8,128)S(1)}, u32[]{:S(2)}, u32[]{:S(2)}) %collective-permute-start.17) | collective-permute-done | bytes 262176 | tf_op jit(solution)/shard_map/ppermute | solution.py:47
  102.0 2.8 %collective-permute-done.18 = f32[128,512]{1,0:T(8,128)S(1)} collective-permute-done((f32[128,512]{1,0:T(8,128)S(1)}, f32[128,512]{1,0:T(8,128)S(1)}, u32[]{:S(2)}, u32[]{:S(2)}) %collective-permute-start.18) | collective-permute-done | bytes 262176 | tf_op jit(solution)/shard_map/ppermute | solution.py:47
  106.1 2.4 %collective-permute-start.20 = (f32[128,512]{1,0:T(8,128)S(1)}, f32[128,512]{1,0:T(8,128)S(1)}, u32[]{:S(2)}, u32[]{:S(2)}) collective-permute-start(f32[128,512]{1,0:T(8,128)S(1)} %add_add_fusion.2.refs_2_), channel_id=1, source_target_pairs={{0,2},{8,10},{16,18},{24,26},{1,3},{9,11},{17,19},{25,27},{2,0},{1... | collective-permute-start | bytes 786440 | tf_op jit(solution)/shard_map/ppermute | solution.py:47
  108.5 3.7 %collective-permute-done.22.refs_5_ = f32[128,512]{1,0:T(8,128)S(1)} collective-permute-done((f32[128,512]{1,0:T(8,128)S(1)}, f32[128,512]{1,0:T(8,128)S(1)}, u32[]{:S(2)}, u32[]{:S(2)}) %collective-permute-start.22) | collective-permute-done | bytes 262176 | tf_op jit(solution)/shard_map/ppermute | solution.py:47
  112.2 7.3 %collective-permute-done.21.refs_4_ = f32[128,512]{1,0:T(8,128)S(1)} collective-permute-done((f32[128,512]{1,0:T(8,128)S(1)}, f32[128,512]{1,0:T(8,128)S(1)}, u32[]{:S(2)}, u32[]{:S(2)}) %collective-permute-start.21) | collective-permute-done | bytes 262176 | tf_op jit(solution)/shard_map/ppermute | solution.py:47
  119.5 2.5 %shard_map.42 = (f32[128,512]{1,0:T(8,128)S(1)}, f32[128,512]{1,0:T(8,128)S(1)}, f32[128,512]{1,0:T(8,128)S(1)}, f32[128,512]{1,0:T(8,128)S(1)}) custom-call(f32[2,2,520,512]{3,2,1,0:T(8,128)S(1)} %shard_map.39.refs_0_, f32[2,2,520,512]{3,2,1,0:T(8,128)S(1)} %collective-permute-done.10.refs_1_, f32[128,512]{1,0:T(8,128)S(1)} %add_add_fusion.2.refs_2_, ...), custom_call_target="tpu_custom_call" | custom-call | flops 1610612736 | bytes 4227072 | tf_op jit(solution)/shard_map/pallas_call | solution.py:266
  124.7 5.8 %collective-permute-done.23 = f32[128,512]{1,0:T(8,128)S(1)} collective-permute-done((f32[128,512]{1,0:T(8,128)S(1)}, f32[128,512]{1,0:T(8,128)S(1)}, u32[]{:S(2)}, u32[]{:S(2)}) %collective-permute-start.23) | collective-permute-done | bytes 262176 | tf_op jit(solution)/shard_map/ppermute | solution.py:47
  131.1 2.1 %collective-permute-done.25 = f32[128,512]{1,0:T(8,128)S(1)} collective-permute-done((f32[128,512]{1,0:T(8,128)S(1)}, f32[128,512]{1,0:T(8,128)S(1)}, u32[]{:S(2)}, u32[]{:S(2)}) %collective-permute-start.25) | collective-permute-done | bytes 262176 | tf_op jit(solution)/shard_map/ppermute | solution.py:47
  133.4 8.8 %collective-permute-done.27.refs_4_ = f32[128,512]{1,0:T(8,128)S(1)} collective-permute-done((f32[128,512]{1,0:T(8,128)S(1)}, f32[128,512]{1,0:T(8,128)S(1)}, u32[]{:S(2)}, u32[]{:S(2)}) %collective-permute-start.27) | collective-permute-done | bytes 262176 | tf_op jit(solution)/shard_map/ppermute | solution.py:47
  142.2 5.1 %collective-permute-done.26.refs_3_ = f32[128,512]{1,0:T(8,128)S(1)} collective-permute-done((f32[128,512]{1,0:T(8,128)S(1)}, f32[128,512]{1,0:T(8,128)S(1)}, u32[]{:S(2)}, u32[]{:S(2)}) %collective-permute-start.26) | collective-permute-done | bytes 262176 | tf_op jit(solution)/shard_map/ppermute | solution.py:47
  147.3 5.2 %collective-permute-done.28.refs_5_ = f32[128,512]{1,0:T(8,128)S(1)} collective-permute-done((f32[128,512]{1,0:T(8,128)S(1)}, f32[128,512]{1,0:T(8,128)S(1)}, u32[]{:S(2)}, u32[]{:S(2)}) %collective-permute-start.28) | collective-permute-done | bytes 262176 | tf_op jit(solution)/shard_map/ppermute | solution.py:47
  152.6 2.5 %shard_map.43 = (f32[256,256]{1,0:T(8,128)S(1)}, f32[256,256]{1,0:T(8,128)S(1)}, f32[256,256]{1,0:T(8,128)S(1)}, f32[256,256]{1,0:T(8,128)S(1)}) custom-call(f32[2,2,520,512]{3,2,1,0:T(8,128)S(1)} %collective-permute-done.6.refs_0_, f32[2,2,520,512]{3,2,1,0:T(8,128)S(1)} %shard_map.38.refs_6_.refs_1_, f32[128,512]{1,0:T(8,128)S(1)} %add_add_fusion.1.refs_2_, ...), custom_call_target="tpu_custom_call" | custom-call | flops 1610612736 | bytes 4227072 | tf_op jit(solution)/shard_map/pallas_call | solution.py:266
  155.5 2.3 %collective-permute-start.31 = (f32[256,256]{1,0:T(8,128)S(1)}, f32[256,256]{1,0:T(8,128)S(1)}, u32[]{:S(2)}, u32[]{:S(2)}) collective-permute-start(f32[256,256]{1,0:T(8,128)S(1)} %get-tuple-element.56), channel_id=1, source_target_pairs={{0,16},{8,24},{16,0},{24,8},{1,17},{9,25},{17,1},{25,9},{2,18},{10... | collective-permute-start | bytes 786440 | tf_op jit(solution)/shard_map/ppermute | solution.py:47
  157.8 5.8 %collective-permute-done.29 = f32[256,256]{1,0:T(8,128)S(1)} collective-permute-done((f32[256,256]{1,0:T(8,128)S(1)}, f32[256,256]{1,0:T(8,128)S(1)}, u32[]{:S(2)}, u32[]{:S(2)}) %collective-permute-start.29) | collective-permute-done | bytes 262176 | tf_op jit(solution)/shard_map/ppermute | solution.py:47
  163.6 4.0 %collective-permute-done.30 = f32[256,256]{1,0:T(8,128)S(1)} collective-permute-done((f32[256,256]{1,0:T(8,128)S(1)}, f32[256,256]{1,0:T(8,128)S(1)}, u32[]{:S(2)}, u32[]{:S(2)}) %collective-permute-start.30) | collective-permute-done | bytes 262176 | tf_op jit(solution)/shard_map/ppermute | solution.py:47
  167.6 2.3 %collective-permute-done.31 = f32[256,256]{1,0:T(8,128)S(1)} collective-permute-done((f32[256,256]{1,0:T(8,128)S(1)}, f32[256,256]{1,0:T(8,128)S(1)}, u32[]{:S(2)}, u32[]{:S(2)}) %collective-permute-start.31) | collective-permute-done | bytes 262176 | tf_op jit(solution)/shard_map/ppermute | solution.py:47
  (47 shorter events, 17.2 us)
Async XLA Ops:
  4.5 21.9 %collective-permute-start.9 = (f32[520,512]{1,0:T(8,128)S(1)}, f32[520,512]{1,0:T(8,128)S(1)}, u32[]{:S(2)}, u32[]{:S(2)}) collective-permute-start(f32[520,512]{1,0:T(8,128)S(1)} %get-tuple-element.39), channel_id=1, source_target_pairs={{0,16},{16,0},{1,17},{17,1},{2,18},{18,2},{3,19},{19,3},{4,20},{20... | collective-permute-start | bytes 3194888 | tf_op jit(solution)/shard_map/ppermute | solution.py:47
  5.3 21.2 %collective-permute-start.8 = (f32[520,512]{1,0:T(8,128)S(1)}, f32[520,512]{1,0:T(8,128)S(1)}, u32[]{:S(2)}, u32[]{:S(2)}) collective-permute-start(f32[520,512]{1,0:T(8,128)S(1)} %get-tuple-element.38), channel_id=1, source_target_pairs={{0,1},{16,17},{1,0},{17,16},{2,3},{18,19},{3,2},{19,18},{4,5},{20,... | collective-permute-start | bytes 3194888 | tf_op jit(solution)/shard_map/ppermute | solution.py:47
  6.0 20.4 %collective-permute-start.7 = (f32[520,512]{1,0:T(8,128)S(1)}, f32[520,512]{1,0:T(8,128)S(1)}, u32[]{:S(2)}, u32[]{:S(2)}) collective-permute-start(f32[520,512]{1,0:T(8,128)S(1)} %get-tuple-element.37), channel_id=1, source_target_pairs={{0,17},{16,1},{1,16},{17,0},{2,19},{18,3},{3,18},{19,2},{4,21},{20... | collective-permute-start | bytes 3194888 | tf_op jit(solution)/shard_map/ppermute | solution.py:47
  6.7 8.9 %collective-permute-start = (f32[128,512]{1,0:T(8,128)S(1)}, f32[128,512]{1,0:T(8,128)S(1)}, u32[]{:S(2)}, u32[]{:S(2)}) collective-permute-start(f32[128,512]{1,0:T(8,128)S(1)} %get-tuple-element.31.refs_4_.refs_2_), channel_id=1, source_target_pairs={{0,4},{8,12},{16,20},{24,28},{1,5},{9,13},{17,21},{25,29},{2,6},{1... | collective-permute-start | bytes 786440 | tf_op jit(solution)/shard_map/ppermute | solution.py:47
  6.9 8.8 %collective-permute-start.5 = (f32[128,512]{1,0:T(8,128)S(1)}, f32[128,512]{1,0:T(8,128)S(1)}, u32[]{:S(2)}, u32[]{:S(2)}) collective-permute-start(f32[128,512]{1,0:T(8,128)S(1)} %get-tuple-element.31.refs_4_.refs_2_), channel_id=1, source_target_pairs={{0,2},{8,10},{16,18},{24,26},{1,3},{9,11},{17,19},{25,27},{2,0},{1... | collective-permute-start | bytes 786440 | tf_op jit(solution)/shard_map/ppermute | solution.py:47
  15.6 10.8 %collective-permute-start.1 = (f32[128,512]{1,0:T(8,128)S(1)}, f32[128,512]{1,0:T(8,128)S(1)}, u32[]{:S(2)}, u32[]{:S(2)}) collective-permute-start(f32[128,512]{1,0:T(8,128)S(1)} %collective-permute-done.refs_6_.refs_4_), channel_id=1, source_target_pairs={{0,2},{8,10},{16,18},{24,26},{1,3},{9,11},{17,19},{25,27},{2,0},{1... | collective-permute-start | bytes 786440 | tf_op jit(solution)/shard_map/ppermute | solution.py:47
  26.5 40.5 %collective-permute-start.10 = (f32[2,2,520,512]{3,2,1,0:T(8,128)S(1)}, f32[2,2,520,512]{3,2,1,0:T(8,128)S(1)}, u32[]{:S(2)}, u32[]{:S(2)}) collective-permute-start(f32[2,2,520,512]{3,2,1,0:T(8,128)S(1)} %shard_map.39.refs_0_), channel_id=1, source_target_pairs={{0,8},{16,24},{1,9},{17,25},{2,10},{18,26},{3,11},{19,27},{4,12},{... | collective-permute-start | bytes 12779528 | tf_op jit(solution)/shard_map/ppermute | solution.py:47
  27.8 19.8 %collective-permute-start.2 = (f32[520,512]{1,0:T(8,128)S(1)}, f32[520,512]{1,0:T(8,128)S(1)}, u32[]{:S(2)}, u32[]{:S(2)}) collective-permute-start(f32[520,512]{1,0:T(8,128)S(1)} %get-tuple-element.37), channel_id=1, source_target_pairs={{8,25},{24,9},{9,24},{25,8},{10,27},{26,11},{11,26},{27,10},{12,29... | collective-permute-start | bytes 3194888 | tf_op jit(solution)/shard_map/ppermute | solution.py:47
  31.9 31.1 %collective-permute-start.3 = (f32[520,512]{1,0:T(8,128)S(1)}, f32[520,512]{1,0:T(8,128)S(1)}, u32[]{:S(2)}, u32[]{:S(2)}) collective-permute-start(f32[520,512]{1,0:T(8,128)S(1)} %get-tuple-element.38), channel_id=1, source_target_pairs={{8,9},{24,25},{9,8},{25,24},{10,11},{26,27},{11,10},{27,26},{12,13... | collective-permute-start | bytes 3194888 | tf_op jit(solution)/shard_map/ppermute | solution.py:47
  34.1 30.5 %collective-permute-start.4 = (f32[520,512]{1,0:T(8,128)S(1)}, f32[520,512]{1,0:T(8,128)S(1)}, u32[]{:S(2)}, u32[]{:S(2)}) collective-permute-start(f32[520,512]{1,0:T(8,128)S(1)} %get-tuple-element.39), channel_id=1, source_target_pairs={{8,24},{24,8},{9,25},{25,9},{10,26},{26,10},{11,27},{27,11},{12,28... | collective-permute-start | bytes 3194888 | tf_op jit(solution)/shard_map/ppermute | solution.py:47
  65.5 22.1 %collective-permute-start.6 = (f32[2,2,520,512]{3,2,1,0:T(8,128)S(1)}, f32[2,2,520,512]{3,2,1,0:T(8,128)S(1)}, u32[]{:S(2)}, u32[]{:S(2)}) collective-permute-start(f32[2,2,520,512]{3,2,1,0:T(8,128)S(1)} %shard_map.38.refs_6_.refs_1_), channel_id=1, source_target_pairs={{8,0},{24,16},{9,1},{25,17},{10,2},{26,18},{11,3},{27,19},{12,4},{... | collective-permute-start | bytes 12779528 | tf_op jit(solution)/shard_map/ppermute | solution.py:47
  69.6 6.3 %collective-permute-start.11 = (f32[128,512]{1,0:T(8,128)S(1)}, f32[128,512]{1,0:T(8,128)S(1)}, u32[]{:S(2)}, u32[]{:S(2)}) collective-permute-start(f32[128,512]{1,0:T(8,128)S(1)} %get-tuple-element.42), channel_id=1, source_target_pairs={{0,17},{8,25},{16,1},{24,9},{1,16},{9,24},{17,0},{25,8},{2,19},{10... | collective-permute-start | bytes 786440 | tf_op jit(solution)/shard_map/ppermute | solution.py:47
  71.8 7.2 %collective-permute-start.12 = (f32[128,512]{1,0:T(8,128)S(1)}, f32[128,512]{1,0:T(8,128)S(1)}, u32[]{:S(2)}, u32[]{:S(2)}) collective-permute-start(f32[128,512]{1,0:T(8,128)S(1)} %get-tuple-element.43), channel_id=1, source_target_pairs={{0,1},{8,9},{16,17},{24,25},{1,0},{9,8},{17,16},{25,24},{2,3},{10,... | collective-permute-start | bytes 786440 | tf_op jit(solution)/shard_map/ppermute | solution.py:47
  72.1 6.9 %collective-permute-start.13 = (f32[128,512]{1,0:T(8,128)S(1)}, f32[128,512]{1,0:T(8,128)S(1)}, u32[]{:S(2)}, u32[]{:S(2)}) collective-permute-start(f32[128,512]{1,0:T(8,128)S(1)} %get-tuple-element.44), channel_id=1, source_target_pairs={{0,16},{8,24},{16,0},{24,8},{1,17},{9,25},{17,1},{25,9},{2,18},{10... | collective-permute-start | bytes 786440 | tf_op jit(solution)/shard_map/ppermute | solution.py:47
  79.1 8.4 %collective-permute-start.15 = (f32[128,512]{1,0:T(8,128)S(1)}, f32[128,512]{1,0:T(8,128)S(1)}, u32[]{:S(2)}, u32[]{:S(2)}) collective-permute-start(f32[128,512]{1,0:T(8,128)S(1)} %add_add_fusion.3.refs_2_), channel_id=1, source_target_pairs={{0,4},{8,12},{16,20},{24,28},{1,5},{9,13},{17,21},{25,29},{2,6},{1... | collective-permute-start | bytes 786440 | tf_op jit(solution)/shard_map/ppermute | solution.py:47
  79.2 8.3 %collective-permute-start.14 = (f32[128,512]{1,0:T(8,128)S(1)}, f32[128,512]{1,0:T(8,128)S(1)}, u32[]{:S(2)}, u32[]{:S(2)}) collective-permute-start(f32[128,512]{1,0:T(8,128)S(1)} %add_add_fusion.3.refs_2_), channel_id=1, source_target_pairs={{0,2},{8,10},{16,18},{24,26},{1,3},{9,11},{17,19},{25,27},{2,0},{1... | collective-permute-start | bytes 786440 | tf_op jit(solution)/shard_map/ppermute | solution.py:47
  87.5 5.5 %collective-permute-start.16 = (f32[128,512]{1,0:T(8,128)S(1)}, f32[128,512]{1,0:T(8,128)S(1)}, u32[]{:S(2)}, u32[]{:S(2)}) collective-permute-start(f32[128,512]{1,0:T(8,128)S(1)} %collective-permute-done.15.refs_4_), channel_id=1, source_target_pairs={{0,2},{8,10},{16,18},{24,26},{1,3},{9,11},{17,19},{25,27},{2,0},{1... | collective-permute-start | bytes 786440 | tf_op jit(solution)/shard_map/ppermute | solution.py:47
  95.5 6.5 %collective-permute-start.17 = (f32[128,512]{1,0:T(8,128)S(1)}, f32[128,512]{1,0:T(8,128)S(1)}, u32[]{:S(2)}, u32[]{:S(2)}) collective-permute-start(f32[128,512]{1,0:T(8,128)S(1)} %get-tuple-element.46), channel_id=1, source_target_pairs={{0,17},{8,25},{16,1},{24,9},{1,16},{9,24},{17,0},{25,8},{2,19},{10... | collective-permute-start | bytes 786440 | tf_op jit(solution)/shard_map/ppermute | solution.py:47
  97.6 7.1 %collective-permute-start.18 = (f32[128,512]{1,0:T(8,128)S(1)}, f32[128,512]{1,0:T(8,128)S(1)}, u32[]{:S(2)}, u32[]{:S(2)}) collective-permute-start(f32[128,512]{1,0:T(8,128)S(1)} %get-tuple-element.47), channel_id=1, source_target_pairs={{0,1},{8,9},{16,17},{24,25},{1,0},{9,8},{17,16},{25,24},{2,3},{10,... | collective-permute-start | bytes 786440 | tf_op jit(solution)/shard_map/ppermute | solution.py:47
  97.9 6.9 %collective-permute-start.19 = (f32[128,512]{1,0:T(8,128)S(1)}, f32[128,512]{1,0:T(8,128)S(1)}, u32[]{:S(2)}, u32[]{:S(2)}) collective-permute-start(f32[128,512]{1,0:T(8,128)S(1)} %get-tuple-element.48), channel_id=1, source_target_pairs={{0,16},{8,24},{16,0},{24,8},{1,17},{9,25},{17,1},{25,9},{2,18},{10... | collective-permute-start | bytes 786440 | tf_op jit(solution)/shard_map/ppermute | solution.py:47
  104.9 7.3 %collective-permute-start.22 = (f32[128,512]{1,0:T(8,128)S(1)}, f32[128,512]{1,0:T(8,128)S(1)}, u32[]{:S(2)}, u32[]{:S(2)}) collective-permute-start(f32[128,512]{1,0:T(8,128)S(1)} %add_add_fusion.2.refs_2_), channel_id=1, source_target_pairs={{0,6},{8,14},{16,22},{24,30},{1,7},{9,15},{17,23},{25,31},{2,4},{1... | collective-permute-start | bytes 786440 | tf_op jit(solution)/shard_map/ppermute | solution.py:47
  105.6 13.9 %collective-permute-start.21 = (f32[128,512]{1,0:T(8,128)S(1)}, f32[128,512]{1,0:T(8,128)S(1)}, u32[]{:S(2)}, u32[]{:S(2)}) collective-permute-start(f32[128,512]{1,0:T(8,128)S(1)} %add_add_fusion.2.refs_2_), channel_id=1, source_target_pairs={{0,4},{8,12},{16,20},{24,28},{1,5},{9,13},{17,21},{25,29},{2,6},{1... | collective-permute-start | bytes 786440 | tf_op jit(solution)/shard_map/ppermute | solution.py:47
  106.1 13.4 %collective-permute-start.20 = (f32[128,512]{1,0:T(8,128)S(1)}, f32[128,512]{1,0:T(8,128)S(1)}, u32[]{:S(2)}, u32[]{:S(2)}) collective-permute-start(f32[128,512]{1,0:T(8,128)S(1)} %add_add_fusion.2.refs_2_), channel_id=1, source_target_pairs={{0,2},{8,10},{16,18},{24,26},{1,3},{9,11},{17,19},{25,27},{2,0},{1... | collective-permute-start | bytes 786440 | tf_op jit(solution)/shard_map/ppermute | solution.py:47
  122.0 8.5 %collective-permute-start.23 = (f32[128,512]{1,0:T(8,128)S(1)}, f32[128,512]{1,0:T(8,128)S(1)}, u32[]{:S(2)}, u32[]{:S(2)}) collective-permute-start(f32[128,512]{1,0:T(8,128)S(1)} %get-tuple-element.50), channel_id=1, source_target_pairs={{0,17},{8,25},{16,1},{24,9},{1,16},{9,24},{17,0},{25,8},{2,19},{10... | collective-permute-start | bytes 786440 | tf_op jit(solution)/shard_map/ppermute | solution.py:47
  124.0 7.2 %collective-permute-start.24 = (f32[128,512]{1,0:T(8,128)S(1)}, f32[128,512]{1,0:T(8,128)S(1)}, u32[]{:S(2)}, u32[]{:S(2)}) collective-permute-start(f32[128,512]{1,0:T(8,128)S(1)} %get-tuple-element.51), channel_id=1, source_target_pairs={{0,1},{8,9},{16,17},{24,25},{1,0},{9,8},{17,16},{25,24},{2,3},{10,... | collective-permute-start | bytes 786440 | tf_op jit(solution)/shard_map/ppermute | solution.py:47
  124.2 9.0 %collective-permute-start.25 = (f32[128,512]{1,0:T(8,128)S(1)}, f32[128,512]{1,0:T(8,128)S(1)}, u32[]{:S(2)}, u32[]{:S(2)}) collective-permute-start(f32[128,512]{1,0:T(8,128)S(1)} %get-tuple-element.52), channel_id=1, source_target_pairs={{0,16},{8,24},{16,0},{24,8},{1,17},{9,25},{17,1},{25,9},{2,18},{10... | collective-permute-start | bytes 786440 | tf_op jit(solution)/shard_map/ppermute | solution.py:47
  133.3 9.0 %collective-permute-start.27 = (f32[128,512]{1,0:T(8,128)S(1)}, f32[128,512]{1,0:T(8,128)S(1)}, u32[]{:S(2)}, u32[]{:S(2)}) collective-permute-start(f32[128,512]{1,0:T(8,128)S(1)} %add_add_fusion.1.refs_2_), channel_id=1, source_target_pairs={{0,4},{8,12},{16,20},{24,28},{1,5},{9,13},{17,21},{25,29},{2,6},{1... | collective-permute-start | bytes 786440 | tf_op jit(solution)/shard_map/ppermute | solution.py:47
  133.3 14.0 %collective-permute-start.26 = (f32[128,512]{1,0:T(8,128)S(1)}, f32[128,512]{1,0:T(8,128)S(1)}, u32[]{:S(2)}, u32[]{:S(2)}) collective-permute-start(f32[128,512]{1,0:T(8,128)S(1)} %add_add_fusion.1.refs_2_), channel_id=1, source_target_pairs={{0,2},{8,10},{16,18},{24,26},{1,3},{9,11},{17,19},{25,27},{2,0},{1... | collective-permute-start | bytes 786440 | tf_op jit(solution)/shard_map/ppermute | solution.py:47
  142.2 10.4 %collective-permute-start.28 = (f32[128,512]{1,0:T(8,128)S(1)}, f32[128,512]{1,0:T(8,128)S(1)}, u32[]{:S(2)}, u32[]{:S(2)}) collective-permute-start(f32[128,512]{1,0:T(8,128)S(1)} %collective-permute-done.27.refs_4_), channel_id=1, source_target_pairs={{0,2},{8,10},{16,18},{24,26},{1,3},{9,11},{17,19},{25,27},{2,0},{1... | collective-permute-start | bytes 786440 | tf_op jit(solution)/shard_map/ppermute | solution.py:47
  155.1 8.5 %collective-permute-start.29 = (f32[256,256]{1,0:T(8,128)S(1)}, f32[256,256]{1,0:T(8,128)S(1)}, u32[]{:S(2)}, u32[]{:S(2)}) collective-permute-start(f32[256,256]{1,0:T(8,128)S(1)} %get-tuple-element.54), channel_id=1, source_target_pairs={{0,17},{8,25},{16,1},{24,9},{1,16},{9,24},{17,0},{25,8},{2,19},{10... | collective-permute-start | bytes 786440 | tf_op jit(solution)/shard_map/ppermute | solution.py:47
  155.2 12.4 %collective-permute-start.30 = (f32[256,256]{1,0:T(8,128)S(1)}, f32[256,256]{1,0:T(8,128)S(1)}, u32[]{:S(2)}, u32[]{:S(2)}) collective-permute-start(f32[256,256]{1,0:T(8,128)S(1)} %get-tuple-element.55), channel_id=1, source_target_pairs={{0,1},{8,9},{16,17},{24,25},{1,0},{9,8},{17,16},{25,24},{2,3},{10,... | collective-permute-start | bytes 786440 | tf_op jit(solution)/shard_map/ppermute | solution.py:47
  155.5 14.4 %collective-permute-start.31 = (f32[256,256]{1,0:T(8,128)S(1)}, f32[256,256]{1,0:T(8,128)S(1)}, u32[]{:S(2)}, u32[]{:S(2)}) collective-permute-start(f32[256,256]{1,0:T(8,128)S(1)} %get-tuple-element.56), channel_id=1, source_target_pairs={{0,16},{8,24},{16,0},{24,8},{1,17},{9,25},{17,1},{25,9},{2,18},{10... | collective-permute-start | bytes 786440 | tf_op jit(solution)/shard_map/ppermute | solution.py:47
  (2 other events, 1.9 us)

commit v5 on v4

--- a/solution.py
+++ b/solution.py
@@ -319,18 +319,24 @@
         return own_samples(grid, value)
 
     def spread(which, pieces):
-        got = {(dx, dy): grid.send(pieces[dx * ny + dy], dx=dx, dy=dy, cores=[which]) for dx, dy in shifts[:0:-1]}
-        return {(0, 0): pieces[0], **got}
+        got, own = {}, pieces[0]
+        for dx, dy in shifts[:0:-1]:
+            if which and not (dx and dy) and (nx - 1, ny - 1) in got:
+                got[nx - 1, ny - 1], pieces = lax.optimization_barrier((got[nx - 1, ny - 1], pieces))
+            got[dx, dy] = grid.send(pieces[dx * ny + dy], dx=dx, dy=dy, cores=[which])
+        return {(0, 0): own, **got}
 
     mats = []
     for site in range(sites):
         gathered = grid.gather(state, relay=RELAY[min(site, 3)])
         token = []
         if site == 0:
+            after, later = [], pieces
             for which in range(cores):
                 if which:
-                    gathered[-1], later = lax.optimization_barrier((gathered[-1], pieces))
-                mine = collect(grid, range(which, sites, cores), spread(which, later if which else pieces), gathered)
+                    gathered, after, later = lax.optimization_barrier((gathered, list(got.values())[1:], pieces))
+                got = spread(which, later)
+                mine = collect(grid, range(which, sites, cores), got, gathered + after)
                 others = [grid.send(mine, dcore=d, cores=[which]) for d in range(1, cores)]
                 mats.append([([mine] + others)[(role - which) % cores] for role in range(cores)])
                 token += [mine] if which else []

time: 171 us -> 164 us (0.959)
  waiting for transfers between devices: 125 us -> 116 us
  starting transfers between devices: 28.6 us -> 30.7 us
    ppermute x32, waiting for transfers between devices: 125 us -> 116 us  [send(): return lax.ppermute(value, ('site', 'bond'), pairs)]
    ppermute x32, starting transfers between devices: 28.6 us -> 30.7 us  [send(): return lax.ppermute(value, ('site', 'bond'), pairs)]
  transfers between devices with their start and end apart: 32 -> 32, of which waited for: 22 -> 24; matrix products, arithmetic and copies ran while one was open for 0% -> 0% of each run, Pallas kernels for 2% -> 2%
where the time goes in v5:
time: 164 us; the launch traced here: 163 us
  waiting for transfers between devices  116 us (71%)
  starting transfers between devices  30.7 us (19%)
  Pallas kernels  13.5 us (8%)
  local copies, waits for them, and re-layouts  1.91 us (1%)
    ppermute x32, waiting for transfers between devices, send(): return lax.ppermute(value, ('site', 'bond'), pairs)  116 us
    ppermute x32, starting transfers between devices, send(): return lax.ppermute(value, ('site', 'bond'), pairs)  30.7 us
    pallas_call x4, Pallas kernels, site_product(): pl.pallas_call(functools.partial(site_kernel, grid, site, last, len(token...  9.94 us
  transfers between devices with their start and end apart: 32, of which 24 were waited for; matrix products, arithmetic and copies ran while one was open for 0% of the time, Pallas kernels for 2%

profile of v5, /device:TPU:25, one launch (start us, length us, event | category | flops | bytes accessed | tf_op | source)
XLA Modules:
  0.0 163.4 jit_solution(7786487794019177592)
XLA Ops:
  1.9 2.6 %shard_map.37 = (f32[520,512]{1,0:T(8,128)S(1)}, f32[520,512]{1,0:T(8,128)S(1)}, f32[520,512]{1,0:T(8,128)S(1)}, f32[520,512]{1,0:T(8,128)S(1)}, f32[128,512]{1,0:T(8,128)S(1)}) custom-call(s32[1,1024]{1,0:T(1,128)S(1)} %copy-done.1, f32[2,256,2048]{2,1,0:T(8,128)} %bitcast.1, f32[256,1024]{1,0:T(8,128)S(1)} %copy-done), custom_call_target="tpu_custom_call" | custom-call | bytes 8388608 | tf_op jit(solution)/shard_map/pallas_call | solution.py:124
  7.0 8.9 %collective-permute-done.1.refs_6_.refs_4_ = f32[128,512]{1,0:T(8,128)S(1)} collective-permute-done((f32[128,512]{1,0:T(8,128)S(1)}, f32[128,512]{1,0:T(8,128)S(1)}, u32[]{:S(2)}, u32[]{:S(2)}) %collective-permute-start.1) | collective-permute-done | bytes 262176 | tf_op jit(solution)/shard_map/ppermute | solution.py:47
  15.9 10.5 %collective-permute-done.2.refs_7_.refs_5_ = f32[128,512]{1,0:T(8,128)S(1)} collective-permute-done((f32[128,512]{1,0:T(8,128)S(1)}, f32[128,512]{1,0:T(8,128)S(1)}, u32[]{:S(2)}, u32[]{:S(2)}) %collective-permute-start.2) | collective-permute-done | bytes 262176 | tf_op jit(solution)/shard_map/ppermute | solution.py:47
  26.4 4.1 %collective-permute-start.6 = (f32[520,512]{1,0:T(8,128)S(1)}, f32[520,512]{1,0:T(8,128)S(1)}, u32[]{:S(2)}, u32[]{:S(2)}) collective-permute-start(f32[520,512]{1,0:T(8,128)S(1)} %get-tuple-element.50), channel_id=1, source_target_pairs={{8,25},{24,9},{9,24},{25,8},{10,27},{26,11},{11,26},{27,10},{12,29... | collective-permute-start | bytes 3194888 | tf_op jit(solution)/shard_map/ppermute | solution.py:47
  31.9 13.2 %collective-permute-done.6.refs_1_ = f32[520,512]{1,0:T(8,128)S(1)} collective-permute-done((f32[520,512]{1,0:T(8,128)S(1)}, f32[520,512]{1,0:T(8,128)S(1)}, u32[]{:S(2)}, u32[]{:S(2)}) %collective-permute-start.6) | collective-permute-done | bytes 1064992 | tf_op jit(solution)/shard_map/ppermute | solution.py:47
  45.1 3.1 %collective-permute-start.8 = (f32[520,512]{1,0:T(8,128)S(1)}, f32[520,512]{1,0:T(8,128)S(1)}, u32[]{:S(2)}, u32[]{:S(2)}) collective-permute-start(f32[520,512]{1,0:T(8,128)S(1)} %get-tuple-element.57), channel_id=1, source_target_pairs={{8,24},{24,8},{9,25},{25,9},{10,26},{26,10},{11,27},{27,11},{12,28... | collective-permute-start | bytes 3194888 | tf_op jit(solution)/shard_map/ppermute | solution.py:47
  48.3 3.1 %collective-permute-start.7 = (f32[520,512]{1,0:T(8,128)S(1)}, f32[520,512]{1,0:T(8,128)S(1)}, u32[]{:S(2)}, u32[]{:S(2)}) collective-permute-start(f32[520,512]{1,0:T(8,128)S(1)} %get-tuple-element.56), channel_id=1, source_target_pairs={{8,9},{24,25},{9,8},{25,24},{10,11},{26,27},{11,10},{27,26},{12,13... | collective-permute-start | bytes 3194888 | tf_op jit(solution)/shard_map/ppermute | solution.py:47
  51.4 15.1 %collective-permute-done.8.refs_3_ = f32[520,512]{1,0:T(8,128)S(1)} collective-permute-done((f32[520,512]{1,0:T(8,128)S(1)}, f32[520,512]{1,0:T(8,128)S(1)}, u32[]{:S(2)}, u32[]{:S(2)}) %collective-permute-start.8) | collective-permute-done | bytes 1064992 | tf_op jit(solution)/shard_map/ppermute | solution.py:47
  66.5 3.3 %collective-permute-done.7.refs_2_ = f32[520,512]{1,0:T(8,128)S(1)} collective-permute-done((f32[520,512]{1,0:T(8,128)S(1)}, f32[520,512]{1,0:T(8,128)S(1)}, u32[]{:S(2)}, u32[]{:S(2)}) %collective-permute-start.7) | collective-permute-done | bytes 1064992 | tf_op jit(solution)/shard_map/ppermute | solution.py:47
  70.7 1.6 collective-permute-start.9
  72.2 2.5 %shard_map.40 = (f32[128,512]{1,0:T(8,128)S(1)}, f32[128,512]{1,0:T(8,128)S(1)}, f32[128,512]{1,0:T(8,128)S(1)}, f32[128,512]{1,0:T(8,128)S(1)}) custom-call(f32[2,2,520,512]{3,2,1,0:T(8,128)S(1)} %shard_map.39.refs_0_, f32[2,2,520,512]{3,2,1,0:T(8,128)S(1)} %collective-permute-done.10.refs_1_, f32[128,512]{1,0:T(8,128)S(1)} %get-tuple-element.58.refs_4_.refs_2_, ...), custom_call_target="tpu_custom_call" | custom-call | flops 1610612736 | bytes 4227072 | tf_op jit(solution)/shard_map/pallas_call | solution.py:266
  77.5 3.6 %collective-permute-done.11 = f32[128,512]{1,0:T(8,128)S(1)} collective-permute-done((f32[128,512]{1,0:T(8,128)S(1)}, f32[128,512]{1,0:T(8,128)S(1)}, u32[]{:S(2)}, u32[]{:S(2)}) %collective-permute-start.11) | collective-permute-done | bytes 262176 | tf_op jit(solution)/shard_map/ppermute | solution.py:47
  81.0 1.9 %collective-permute-done.12 = f32[128,512]{1,0:T(8,128)S(1)} collective-permute-done((f32[128,512]{1,0:T(8,128)S(1)}, f32[128,512]{1,0:T(8,128)S(1)}, u32[]{:S(2)}, u32[]{:S(2)}) %collective-permute-start.12) | collective-permute-done | bytes 262176 | tf_op jit(solution)/shard_map/ppermute | solution.py:47
  84.3 8.6 %collective-permute-done.15.refs_4_ = f32[128,512]{1,0:T(8,128)S(1)} collective-permute-done((f32[128,512]{1,0:T(8,128)S(1)}, f32[128,512]{1,0:T(8,128)S(1)}, u32[]{:S(2)}, u32[]{:S(2)}) %collective-permute-start.15) | collective-permute-done | bytes 262176 | tf_op jit(solution)/shard_map/ppermute | solution.py:47
  92.8 5.2 %collective-permute-done.16.refs_5_ = f32[128,512]{1,0:T(8,128)S(1)} collective-permute-done((f32[128,512]{1,0:T(8,128)S(1)}, f32[128,512]{1,0:T(8,128)S(1)}, u32[]{:S(2)}, u32[]{:S(2)}) %collective-permute-start.16) | collective-permute-done | bytes 262176 | tf_op jit(solution)/shard_map/ppermute | solution.py:47
  98.1 2.5 %shard_map.41 = (f32[128,512]{1,0:T(8,128)S(1)}, f32[128,512]{1,0:T(8,128)S(1)}, f32[128,512]{1,0:T(8,128)S(1)}, f32[128,512]{1,0:T(8,128)S(1)}) custom-call(f32[2,2,520,512]{3,2,1,0:T(8,128)S(1)} %collective-permute-done.9.refs_0_, f32[2,2,520,512]{3,2,1,0:T(8,128)S(1)} %shard_map.38.refs_6_.refs_1_, f32[128,512]{1,0:T(8,128)S(1)} %add_add_fusion.3.refs_2_, ...), custom_call_target="tpu_custom_call" | custom-call | flops 1610612736 | bytes 4227072 | tf_op jit(solution)/shard_map/pallas_call | solution.py:266
  103.2 3.8 %collective-permute-done.17 = f32[128,512]{1,0:T(8,128)S(1)} collective-permute-done((f32[128,512]{1,0:T(8,128)S(1)}, f32[128,512]{1,0:T(8,128)S(1)}, u32[]{:S(2)}, u32[]{:S(2)}) %collective-permute-start.17) | collective-permute-done | bytes 262176 | tf_op jit(solution)/shard_map/ppermute | solution.py:47
  107.1 1.6 collective-permute-done.18
  109.8 2.2 %collective-permute-start.21 = (f32[128,512]{1,0:T(8,128)S(1)}, f32[128,512]{1,0:T(8,128)S(1)}, u32[]{:S(2)}, u32[]{:S(2)}) collective-permute-start(f32[128,512]{1,0:T(8,128)S(1)} %add_add_fusion.2.refs_2_), channel_id=1, source_target_pairs={{0,4},{8,12},{16,20},{24,28},{1,5},{9,13},{17,21},{25,29},{2,6},{1... | collective-permute-start | bytes 786440 | tf_op jit(solution)/shard_map/ppermute | solution.py:47
  113.2 3.7 %collective-permute-done.22.refs_5_ = f32[128,512]{1,0:T(8,128)S(1)} collective-permute-done((f32[128,512]{1,0:T(8,128)S(1)}, f32[128,512]{1,0:T(8,128)S(1)}, u32[]{:S(2)}, u32[]{:S(2)}) %collective-permute-start.22) | collective-permute-done | bytes 262176 | tf_op jit(solution)/shard_map/ppermute | solution.py:47
  116.9 10.9 %collective-permute-done.21.refs_4_ = f32[128,512]{1,0:T(8,128)S(1)} collective-permute-done((f32[128,512]{1,0:T(8,128)S(1)}, f32[128,512]{1,0:T(8,128)S(1)}, u32[]{:S(2)}, u32[]{:S(2)}) %collective-permute-start.21) | collective-permute-done | bytes 262176 | tf_op jit(solution)/shard_map/ppermute | solution.py:47
  127.8 2.5 %shard_map.42 = (f32[128,512]{1,0:T(8,128)S(1)}, f32[128,512]{1,0:T(8,128)S(1)}, f32[128,512]{1,0:T(8,128)S(1)}, f32[128,512]{1,0:T(8,128)S(1)}) custom-call(f32[2,2,520,512]{3,2,1,0:T(8,128)S(1)} %shard_map.39.refs_0_, f32[2,2,520,512]{3,2,1,0:T(8,128)S(1)} %collective-permute-done.10.refs_1_, f32[128,512]{1,0:T(8,128)S(1)} %add_add_fusion.2.refs_2_, ...), custom_call_target="tpu_custom_call" | custom-call | flops 1610612736 | bytes 4227072 | tf_op jit(solution)/shard_map/pallas_call | solution.py:266
  130.3 1.3 collective-permute-start.23
  133.0 3.6 %collective-permute-done.23 = f32[128,512]{1,0:T(8,128)S(1)} collective-permute-done((f32[128,512]{1,0:T(8,128)S(1)}, f32[128,512]{1,0:T(8,128)S(1)}, u32[]{:S(2)}, u32[]{:S(2)}) %collective-permute-start.23) | collective-permute-done | bytes 262176 | tf_op jit(solution)/shard_map/ppermute | solution.py:47
  136.6 1.9 %collective-permute-done.24 = f32[128,512]{1,0:T(8,128)S(1)} collective-permute-done((f32[128,512]{1,0:T(8,128)S(1)}, f32[128,512]{1,0:T(8,128)S(1)}, u32[]{:S(2)}, u32[]{:S(2)}) %collective-permute-start.24) | collective-permute-done | bytes 262176 | tf_op jit(solution)/shard_map/ppermute | solution.py:47
  139.5 6.4 %collective-permute-done.27.refs_4_ = f32[128,512]{1,0:T(8,128)S(1)} collective-permute-done((f32[128,512]{1,0:T(8,128)S(1)}, f32[128,512]{1,0:T(8,128)S(1)}, u32[]{:S(2)}, u32[]{:S(2)}) %collective-permute-start.27) | collective-permute-done | bytes 262176 | tf_op jit(solution)/shard_map/ppermute | solution.py:47
  145.9 1.9 %collective-permute-done.26.refs_3_ = f32[128,512]{1,0:T(8,128)S(1)} collective-permute-done((f32[128,512]{1,0:T(8,128)S(1)}, f32[128,512]{1,0:T(8,128)S(1)}, u32[]{:S(2)}, u32[]{:S(2)}) %collective-permute-start.26) | collective-permute-done | bytes 262176 | tf_op jit(solution)/shard_map/ppermute | solution.py:47
  147.9 3.3 %collective-permute-done.28.refs_5_ = f32[128,512]{1,0:T(8,128)S(1)} collective-permute-done((f32[128,512]{1,0:T(8,128)S(1)}, f32[128,512]{1,0:T(8,128)S(1)}, u32[]{:S(2)}, u32[]{:S(2)}) %collective-permute-start.28) | collective-permute-done | bytes 262176 | tf_op jit(solution)/shard_map/ppermute | solution.py:47
  151.1 2.5 %shard_map.43 = (f32[256,256]{1,0:T(8,128)S(1)}, f32[256,256]{1,0:T(8,128)S(1)}, f32[256,256]{1,0:T(8,128)S(1)}, f32[256,256]{1,0:T(8,128)S(1)}) custom-call(f32[2,2,520,512]{3,2,1,0:T(8,128)S(1)} %collective-permute-done.9.refs_0_, f32[2,2,520,512]{3,2,1,0:T(8,128)S(1)} %shard_map.38.refs_6_.refs_1_, f32[128,512]{1,0:T(8,128)S(1)} %add_add_fusion.1.refs_2_, ...), custom_call_target="tpu_custom_call" | custom-call | flops 1610612736 | bytes 4227072 | tf_op jit(solution)/shard_map/pallas_call | solution.py:266
  153.6 1.4 collective-permute-start.29
  156.4 3.6 %collective-permute-done.29 = f32[256,256]{1,0:T(8,128)S(1)} collective-permute-done((f32[256,256]{1,0:T(8,128)S(1)}, f32[256,256]{1,0:T(8,128)S(1)}, u32[]{:S(2)}, u32[]{:S(2)}) %collective-permute-start.29) | collective-permute-done | bytes 262176 | tf_op jit(solution)/shard_map/ppermute | solution.py:47
  159.9 1.9 %collective-permute-done.30 = f32[256,256]{1,0:T(8,128)S(1)} collective-permute-done((f32[256,256]{1,0:T(8,128)S(1)}, f32[256,256]{1,0:T(8,128)S(1)}, u32[]{:S(2)}, u32[]{:S(2)}) %collective-permute-start.30) | collective-permute-done | bytes 262176 | tf_op jit(solution)/shard_map/ppermute | solution.py:47
  (47 shorter events, 21.2 us)
Async XLA Ops:
  4.5 21.9 %collective-permute-start.3 = (f32[520,512]{1,0:T(8,128)S(1)}, f32[520,512]{1,0:T(8,128)S(1)}, u32[]{:S(2)}, u32[]{:S(2)}) collective-permute-start(f32[520,512]{1,0:T(8,128)S(1)} %get-tuple-element.50), channel_id=1, source_target_pairs={{0,17},{16,1},{1,16},{17,0},{2,19},{18,3},{3,18},{19,2},{4,21},{20... | collective-permute-start | bytes 3194888 | tf_op jit(solution)/shard_map/ppermute | solution.py:47
  5.3 21.2 %collective-permute-start.4 = (f32[520,512]{1,0:T(8,128)S(1)}, f32[520,512]{1,0:T(8,128)S(1)}, u32[]{:S(2)}, u32[]{:S(2)}) collective-permute-start(f32[520,512]{1,0:T(8,128)S(1)} %get-tuple-element.56), channel_id=1, source_target_pairs={{0,1},{16,17},{1,0},{17,16},{2,3},{18,19},{3,2},{19,18},{4,5},{20,... | collective-permute-start | bytes 3194888 | tf_op jit(solution)/shard_map/ppermute | solution.py:47
  6.0 20.4 %collective-permute-start.5 = (f32[520,512]{1,0:T(8,128)S(1)}, f32[520,512]{1,0:T(8,128)S(1)}, u32[]{:S(2)}, u32[]{:S(2)}) collective-permute-start(f32[520,512]{1,0:T(8,128)S(1)} %get-tuple-element.57), channel_id=1, source_target_pairs={{0,16},{16,0},{1,17},{17,1},{2,18},{18,2},{3,19},{19,3},{4,20},{20... | collective-permute-start | bytes 3194888 | tf_op jit(solution)/shard_map/ppermute | solution.py:47
  6.7 9.2 %collective-permute-start.1 = (f32[128,512]{1,0:T(8,128)S(1)}, f32[128,512]{1,0:T(8,128)S(1)}, u32[]{:S(2)}, u32[]{:S(2)}) collective-permute-start(f32[128,512]{1,0:T(8,128)S(1)} %get-tuple-element.58.refs_4_.refs_2_), channel_id=1, source_target_pairs={{0,4},{8,12},{16,20},{24,28},{1,5},{9,13},{17,21},{25,29},{2,6},{1... | collective-permute-start | bytes 786440 | tf_op jit(solution)/shard_map/ppermute | solution.py:47
  6.9 9.1 %collective-permute-start = (f32[128,512]{1,0:T(8,128)S(1)}, f32[128,512]{1,0:T(8,128)S(1)}, u32[]{:S(2)}, u32[]{:S(2)}) collective-permute-start(f32[128,512]{1,0:T(8,128)S(1)} %get-tuple-element.58.refs_4_.refs_2_), channel_id=1, source_target_pairs={{0,2},{8,10},{16,18},{24,26},{1,3},{9,11},{17,19},{25,27},{2,0},{1... | collective-permute-start | bytes 786440 | tf_op jit(solution)/shard_map/ppermute | solution.py:47
  15.9 10.5 %collective-permute-start.2 = (f32[128,512]{1,0:T(8,128)S(1)}, f32[128,512]{1,0:T(8,128)S(1)}, u32[]{:S(2)}, u32[]{:S(2)}) collective-permute-start(f32[128,512]{1,0:T(8,128)S(1)} %collective-permute-done.1.refs_6_.refs_4_), channel_id=1, source_target_pairs={{0,2},{8,10},{16,18},{24,26},{1,3},{9,11},{17,19},{25,27},{2,0},{1... | collective-permute-start | bytes 786440 | tf_op jit(solution)/shard_map/ppermute | solution.py:47
  26.4 18.7 %collective-permute-start.6 = (f32[520,512]{1,0:T(8,128)S(1)}, f32[520,512]{1,0:T(8,128)S(1)}, u32[]{:S(2)}, u32[]{:S(2)}) collective-permute-start(f32[520,512]{1,0:T(8,128)S(1)} %get-tuple-element.50), channel_id=1, source_target_pairs={{8,25},{24,9},{9,24},{25,8},{10,27},{26,11},{11,26},{27,10},{12,29... | collective-permute-start | bytes 3194888 | tf_op jit(solution)/shard_map/ppermute | solution.py:47
  30.6 41.6 %collective-permute-start.10 = (f32[2,2,520,512]{3,2,1,0:T(8,128)S(1)}, f32[2,2,520,512]{3,2,1,0:T(8,128)S(1)}, u32[]{:S(2)}, u32[]{:S(2)}) collective-permute-start(f32[2,2,520,512]{3,2,1,0:T(8,128)S(1)} %shard_map.39.refs_0_), channel_id=1, source_target_pairs={{0,8},{16,24},{1,9},{17,25},{2,10},{18,26},{3,11},{19,27},{4,12},{... | collective-permute-start | bytes 12779528 | tf_op jit(solution)/shard_map/ppermute | solution.py:47
  45.1 21.3 %collective-permute-start.8 = (f32[520,512]{1,0:T(8,128)S(1)}, f32[520,512]{1,0:T(8,128)S(1)}, u32[]{:S(2)}, u32[]{:S(2)}) collective-permute-start(f32[520,512]{1,0:T(8,128)S(1)} %get-tuple-element.57), channel_id=1, source_target_pairs={{8,24},{24,8},{9,25},{25,9},{10,26},{26,10},{11,27},{27,11},{12,28... | collective-permute-start | bytes 3194888 | tf_op jit(solution)/shard_map/ppermute | solution.py:47
  48.3 21.5 %collective-permute-start.7 = (f32[520,512]{1,0:T(8,128)S(1)}, f32[520,512]{1,0:T(8,128)S(1)}, u32[]{:S(2)}, u32[]{:S(2)}) collective-permute-start(f32[520,512]{1,0:T(8,128)S(1)} %get-tuple-element.56), channel_id=1, source_target_pairs={{8,9},{24,25},{9,8},{25,24},{10,11},{26,27},{11,10},{27,26},{12,13... | collective-permute-start | bytes 3194888 | tf_op jit(solution)/shard_map/ppermute | solution.py:47
  70.7 27.4 %collective-permute-start.9 = (f32[2,2,520,512]{3,2,1,0:T(8,128)S(1)}, f32[2,2,520,512]{3,2,1,0:T(8,128)S(1)}, u32[]{:S(2)}, u32[]{:S(2)}) collective-permute-start(f32[2,2,520,512]{3,2,1,0:T(8,128)S(1)} %shard_map.38.refs_6_.refs_1_), channel_id=1, source_target_pairs={{8,0},{24,16},{9,1},{25,17},{10,2},{26,18},{11,3},{27,19},{12,4},{... | collective-permute-start | bytes 12779528 | tf_op jit(solution)/shard_map/ppermute | solution.py:47
  74.8 6.3 %collective-permute-start.11 = (f32[128,512]{1,0:T(8,128)S(1)}, f32[128,512]{1,0:T(8,128)S(1)}, u32[]{:S(2)}, u32[]{:S(2)}) collective-permute-start(f32[128,512]{1,0:T(8,128)S(1)} %get-tuple-element.66), channel_id=1, source_target_pairs={{0,17},{8,25},{16,1},{24,9},{1,16},{9,24},{17,0},{25,8},{2,19},{10... | collective-permute-start | bytes 786440 | tf_op jit(solution)/shard_map/ppermute | solution.py:47
  76.1 6.8 %collective-permute-start.12 = (f32[128,512]{1,0:T(8,128)S(1)}, f32[128,512]{1,0:T(8,128)S(1)}, u32[]{:S(2)}, u32[]{:S(2)}) collective-permute-start(f32[128,512]{1,0:T(8,128)S(1)} %get-tuple-element.67), channel_id=1, source_target_pairs={{0,1},{8,9},{16,17},{24,25},{1,0},{9,8},{17,16},{25,24},{2,3},{10,... | collective-permute-start | bytes 786440 | tf_op jit(solution)/shard_map/ppermute | solution.py:47
  76.3 7.4 %collective-permute-start.13 = (f32[128,512]{1,0:T(8,128)S(1)}, f32[128,512]{1,0:T(8,128)S(1)}, u32[]{:S(2)}, u32[]{:S(2)}) collective-permute-start(f32[128,512]{1,0:T(8,128)S(1)} %get-tuple-element.68), channel_id=1, source_target_pairs={{0,16},{8,24},{16,0},{24,8},{1,17},{9,25},{17,1},{25,9},{2,18},{10... | collective-permute-start | bytes 786440 | tf_op jit(solution)/shard_map/ppermute | solution.py:47
  83.8 9.0 %collective-permute-start.15 = (f32[128,512]{1,0:T(8,128)S(1)}, f32[128,512]{1,0:T(8,128)S(1)}, u32[]{:S(2)}, u32[]{:S(2)}) collective-permute-start(f32[128,512]{1,0:T(8,128)S(1)} %add_add_fusion.3.refs_2_), channel_id=1, source_target_pairs={{0,4},{8,12},{16,20},{24,28},{1,5},{9,13},{17,21},{25,29},{2,6},{1... | collective-permute-start | bytes 786440 | tf_op jit(solution)/shard_map/ppermute | solution.py:47
  83.9 8.9 %collective-permute-start.14 = (f32[128,512]{1,0:T(8,128)S(1)}, f32[128,512]{1,0:T(8,128)S(1)}, u32[]{:S(2)}, u32[]{:S(2)}) collective-permute-start(f32[128,512]{1,0:T(8,128)S(1)} %add_add_fusion.3.refs_2_), channel_id=1, source_target_pairs={{0,2},{8,10},{16,18},{24,26},{1,3},{9,11},{17,19},{25,27},{2,0},{1... | collective-permute-start | bytes 786440 | tf_op jit(solution)/shard_map/ppermute | solution.py:47
  92.8 5.2 %collective-permute-start.16 = (f32[128,512]{1,0:T(8,128)S(1)}, f32[128,512]{1,0:T(8,128)S(1)}, u32[]{:S(2)}, u32[]{:S(2)}) collective-permute-start(f32[128,512]{1,0:T(8,128)S(1)} %collective-permute-done.15.refs_4_), channel_id=1, source_target_pairs={{0,2},{8,10},{16,18},{24,26},{1,3},{9,11},{17,19},{25,27},{2,0},{1... | collective-permute-start | bytes 786440 | tf_op jit(solution)/shard_map/ppermute | solution.py:47
  100.5 6.5 %collective-permute-start.17 = (f32[128,512]{1,0:T(8,128)S(1)}, f32[128,512]{1,0:T(8,128)S(1)}, u32[]{:S(2)}, u32[]{:S(2)}) collective-permute-start(f32[128,512]{1,0:T(8,128)S(1)} %get-tuple-element.70), channel_id=1, source_target_pairs={{0,17},{8,25},{16,1},{24,9},{1,16},{9,24},{17,0},{25,8},{2,19},{10... | collective-permute-start | bytes 786440 | tf_op jit(solution)/shard_map/ppermute | solution.py:47
  101.8 6.8 %collective-permute-start.18 = (f32[128,512]{1,0:T(8,128)S(1)}, f32[128,512]{1,0:T(8,128)S(1)}, u32[]{:S(2)}, u32[]{:S(2)}) collective-permute-start(f32[128,512]{1,0:T(8,128)S(1)} %get-tuple-element.71), channel_id=1, source_target_pairs={{0,1},{8,9},{16,17},{24,25},{1,0},{9,8},{17,16},{25,24},{2,3},{10,... | collective-permute-start | bytes 786440 | tf_op jit(solution)/shard_map/ppermute | solution.py:47
  102.1 7.4 %collective-permute-start.19 = (f32[128,512]{1,0:T(8,128)S(1)}, f32[128,512]{1,0:T(8,128)S(1)}, u32[]{:S(2)}, u32[]{:S(2)}) collective-permute-start(f32[128,512]{1,0:T(8,128)S(1)} %get-tuple-element.72), channel_id=1, source_target_pairs={{0,16},{8,24},{16,0},{24,8},{1,17},{9,25},{17,1},{25,9},{2,18},{10... | collective-permute-start | bytes 786440 | tf_op jit(solution)/shard_map/ppermute | solution.py:47
  109.6 7.3 %collective-permute-start.22 = (f32[128,512]{1,0:T(8,128)S(1)}, f32[128,512]{1,0:T(8,128)S(1)}, u32[]{:S(2)}, u32[]{:S(2)}) collective-permute-start(f32[128,512]{1,0:T(8,128)S(1)} %add_add_fusion.2.refs_2_), channel_id=1, source_target_pairs={{0,6},{8,14},{16,22},{24,30},{1,7},{9,15},{17,23},{25,31},{2,4},{1... | collective-permute-start | bytes 786440 | tf_op jit(solution)/shard_map/ppermute | solution.py:47
  109.8 18.0 %collective-permute-start.21 = (f32[128,512]{1,0:T(8,128)S(1)}, f32[128,512]{1,0:T(8,128)S(1)}, u32[]{:S(2)}, u32[]{:S(2)}) collective-permute-start(f32[128,512]{1,0:T(8,128)S(1)} %add_add_fusion.2.refs_2_), channel_id=1, source_target_pairs={{0,4},{8,12},{16,20},{24,28},{1,5},{9,13},{17,21},{25,29},{2,6},{1... | collective-permute-start | bytes 786440 | tf_op jit(solution)/shard_map/ppermute | solution.py:47
  112.0 15.8 %collective-permute-start.20 = (f32[128,512]{1,0:T(8,128)S(1)}, f32[128,512]{1,0:T(8,128)S(1)}, u32[]{:S(2)}, u32[]{:S(2)}) collective-permute-start(f32[128,512]{1,0:T(8,128)S(1)} %add_add_fusion.2.refs_2_), channel_id=1, source_target_pairs={{0,2},{8,10},{16,18},{24,26},{1,3},{9,11},{17,19},{25,27},{2,0},{1... | collective-permute-start | bytes 786440 | tf_op jit(solution)/shard_map/ppermute | solution.py:47
  130.3 6.3 %collective-permute-start.23 = (f32[128,512]{1,0:T(8,128)S(1)}, f32[128,512]{1,0:T(8,128)S(1)}, u32[]{:S(2)}, u32[]{:S(2)}) collective-permute-start(f32[128,512]{1,0:T(8,128)S(1)} %get-tuple-element.74), channel_id=1, source_target_pairs={{0,17},{8,25},{16,1},{24,9},{1,16},{9,24},{17,0},{25,8},{2,19},{10... | collective-permute-start | bytes 786440 | tf_op jit(solution)/shard_map/ppermute | solution.py:47
  131.6 6.8 %collective-permute-start.24 = (f32[128,512]{1,0:T(8,128)S(1)}, f32[128,512]{1,0:T(8,128)S(1)}, u32[]{:S(2)}, u32[]{:S(2)}) collective-permute-start(f32[128,512]{1,0:T(8,128)S(1)} %get-tuple-element.75), channel_id=1, source_target_pairs={{0,1},{8,9},{16,17},{24,25},{1,0},{9,8},{17,16},{25,24},{2,3},{10,... | collective-permute-start | bytes 786440 | tf_op jit(solution)/shard_map/ppermute | solution.py:47
  131.9 7.4 %collective-permute-start.25 = (f32[128,512]{1,0:T(8,128)S(1)}, f32[128,512]{1,0:T(8,128)S(1)}, u32[]{:S(2)}, u32[]{:S(2)}) collective-permute-start(f32[128,512]{1,0:T(8,128)S(1)} %get-tuple-element.76), channel_id=1, source_target_pairs={{0,16},{8,24},{16,0},{24,8},{1,17},{9,25},{17,1},{25,9},{2,18},{10... | collective-permute-start | bytes 786440 | tf_op jit(solution)/shard_map/ppermute | solution.py:47
  139.4 6.5 %collective-permute-start.27 = (f32[128,512]{1,0:T(8,128)S(1)}, f32[128,512]{1,0:T(8,128)S(1)}, u32[]{:S(2)}, u32[]{:S(2)}) collective-permute-start(f32[128,512]{1,0:T(8,128)S(1)} %add_add_fusion.1.refs_2_), channel_id=1, source_target_pairs={{0,4},{8,12},{16,20},{24,28},{1,5},{9,13},{17,21},{25,29},{2,6},{1... | collective-permute-start | bytes 786440 | tf_op jit(solution)/shard_map/ppermute | solution.py:47
  139.5 8.4 %collective-permute-start.26 = (f32[128,512]{1,0:T(8,128)S(1)}, f32[128,512]{1,0:T(8,128)S(1)}, u32[]{:S(2)}, u32[]{:S(2)}) collective-permute-start(f32[128,512]{1,0:T(8,128)S(1)} %add_add_fusion.1.refs_2_), channel_id=1, source_target_pairs={{0,2},{8,10},{16,18},{24,26},{1,3},{9,11},{17,19},{25,27},{2,0},{1... | collective-permute-start | bytes 786440 | tf_op jit(solution)/shard_map/ppermute | solution.py:47
  145.9 5.2 %collective-permute-start.28 = (f32[128,512]{1,0:T(8,128)S(1)}, f32[128,512]{1,0:T(8,128)S(1)}, u32[]{:S(2)}, u32[]{:S(2)}) collective-permute-start(f32[128,512]{1,0:T(8,128)S(1)} %collective-permute-done.27.refs_4_), channel_id=1, source_target_pairs={{0,2},{8,10},{16,18},{24,26},{1,3},{9,11},{17,19},{25,27},{2,0},{1... | collective-permute-start | bytes 786440 | tf_op jit(solution)/shard_map/ppermute | solution.py:47
  153.6 6.3 %collective-permute-start.29 = (f32[256,256]{1,0:T(8,128)S(1)}, f32[256,256]{1,0:T(8,128)S(1)}, u32[]{:S(2)}, u32[]{:S(2)}) collective-permute-start(f32[256,256]{1,0:T(8,128)S(1)} %get-tuple-element.78), channel_id=1, source_target_pairs={{0,17},{8,25},{16,1},{24,9},{1,16},{9,24},{17,0},{25,8},{2,19},{10... | collective-permute-start | bytes 786440 | tf_op jit(solution)/shard_map/ppermute | solution.py:47
  155.0 6.8 %collective-permute-start.30 = (f32[256,256]{1,0:T(8,128)S(1)}, f32[256,256]{1,0:T(8,128)S(1)}, u32[]{:S(2)}, u32[]{:S(2)}) collective-permute-start(f32[256,256]{1,0:T(8,128)S(1)} %get-tuple-element.79), channel_id=1, source_target_pairs={{0,1},{8,9},{16,17},{24,25},{1,0},{9,8},{17,16},{25,24},{2,3},{10,... | collective-permute-start | bytes 786440 | tf_op jit(solution)/shard_map/ppermute | solution.py:47
  155.2 7.4 %collective-permute-start.31 = (f32[256,256]{1,0:T(8,128)S(1)}, f32[256,256]{1,0:T(8,128)S(1)}, u32[]{:S(2)}, u32[]{:S(2)}) collective-permute-start(f32[256,256]{1,0:T(8,128)S(1)} %get-tuple-element.80), channel_id=1, source_target_pairs={{0,16},{8,24},{16,0},{24,8},{1,17},{9,25},{17,1},{25,9},{2,18},{10... | collective-permute-start | bytes 786440 | tf_op jit(solution)/shard_map/ppermute | solution.py:47
  (2 other events, 1.9 us)

commit v6 on v5

--- a/solution.py
+++ b/solution.py
@@ -10,7 +10,7 @@
 
 CLICK_ROWS = 8
 PACK_VMEM = 48 * 1024 * 1024
-RELAY = (True, True, False, True)
+RELAY = (True, True, False, False)
 
 
 class Grid:
@@ -326,21 +326,24 @@
             got[dx, dy] = grid.send(pieces[dx * ny + dy], dx=dx, dy=dy, cores=[which])
         return {(0, 0): own, **got}
 
+    def across(mine, which):
+        others = [grid.send(mine, dcore=d, cores=[which]) for d in range(1, cores)]
+        return [([mine] + others)[(role - which) % cores] for role in range(cores)]
+
     mats = []
     for site in range(sites):
         gathered = grid.gather(state, relay=RELAY[min(site, 3)])
         token = []
         if site == 0:
-            after, later = [], pieces
-            for which in range(cores):
-                if which:
-                    gathered, after, later = lax.optimization_barrier((gathered, list(got.values())[1:], pieces))
+            got = spread(0, pieces)
+            mats.append(across(collect(grid, range(0, sites, cores), got, gathered), 0))
+            for which in range(1, cores):
+                gathered, after, later = lax.optimization_barrier((gathered, list(got.values())[1:], pieces))
                 got = spread(which, later)
-                mine = collect(grid, range(which, sites, cores), got, gathered + after)
-                others = [grid.send(mine, dcore=d, cores=[which]) for d in range(1, cores)]
-                mats.append([([mine] + others)[(role - which) % cores] for role in range(cores)])
-                token += [mine] if which else []
+                token += [got[0, 1]] + after
         outs = site_product(grid, site, clicks_of(site), mats[site % cores], gathered, token)
+        if site == 0 and cores > 1:
+            mats.append(across(collect(grid, range(1, sites, cores), got, outs[:1]), 1))
         state = outs[0]
         for ex, ey in shifts[:0:-1]:
             state = state + grid.send(outs[ex * ny + ey], dx=ex, dy=ey)

time: 164 us -> 160 us (0.976); the launches traced: 163 us -> 157 us
  waiting for transfers between devices: 116 us -> 106 us
  starting transfers between devices: 30.7 us -> 34.7 us
    ppermute x32, waiting for transfers between devices: 116 us -> 106 us  [send(): return lax.ppermute(value, ('site', 'bond'), pairs)]
    ppermute x32, starting transfers between devices: 30.7 us -> 34.7 us  [send(): return lax.ppermute(value, ('site', 'bond'), pairs)]
  transfers between devices with their start and end apart: 32 -> 32, of which waited for: 24 -> 22; matrix products, arithmetic and copies ran while one was open for 0% -> 0% of each run, Pallas kernels for 2% -> 2%
where the time goes in v6:
time: 160 us; the launch traced here: 157 us
  waiting for transfers between devices  106 us (66%)
  starting transfers between devices  34.7 us (22%)
  Pallas kernels  13.5 us (8%)
  local copies, waits for them, and re-layouts  1.91 us (1%)
    ppermute x32, waiting for transfers between devices, send(): return lax.ppermute(value, ('site', 'bond'), pairs)  106 us
    ppermute x32, starting transfers between devices, send(): return lax.ppermute(value, ('site', 'bond'), pairs)  34.7 us
    pallas_call x4, Pallas kernels, site_product(): pl.pallas_call(functools.partial(site_kernel, grid, site, last, len(token...  9.92 us
  transfers between devices with their start and end apart: 32, of which 22 were waited for; matrix products, arithmetic and copies ran while one was open for 0% of the time, Pallas kernels for 2%

profile of v6, /device:TPU:25, one launch (start us, length us, event | category | flops | bytes accessed | tf_op | source)
XLA Modules:
  0.0 157.0 jit_solution(522951108016744357)
XLA Ops:
  1.9 2.6 %shard_map.37 = (f32[520,512]{1,0:T(8,128)S(1)}, f32[520,512]{1,0:T(8,128)S(1)}, f32[520,512]{1,0:T(8,128)S(1)}, f32[520,512]{1,0:T(8,128)S(1)}, f32[128,512]{1,0:T(8,128)S(1)}) custom-call(s32[1,1024]{1,0:T(1,128)S(1)} %copy-done.1, f32[2,256,2048]{2,1,0:T(8,128)} %bitcast.1, f32[256,1024]{1,0:T(8,128)S(1)} %copy-done), custom_call_target="tpu_custom_call" | custom-call | bytes 8388608 | tf_op jit(solution)/shard_map/pallas_call | solution.py:124
  7.0 8.9 %collective-permute-done.1.refs_6_.refs_4_ = f32[128,512]{1,0:T(8,128)S(1)} collective-permute-done((f32[128,512]{1,0:T(8,128)S(1)}, f32[128,512]{1,0:T(8,128)S(1)}, u32[]{:S(2)}, u32[]{:S(2)}) %collective-permute-start.1) | collective-permute-done | bytes 262176 | tf_op jit(solution)/shard_map/ppermute | solution.py:47
  15.9 10.5 %collective-permute-done.2.refs_7_.refs_5_ = f32[128,512]{1,0:T(8,128)S(1)} collective-permute-done((f32[128,512]{1,0:T(8,128)S(1)}, f32[128,512]{1,0:T(8,128)S(1)}, u32[]{:S(2)}, u32[]{:S(2)}) %collective-permute-start.2) | collective-permute-done | bytes 262176 | tf_op jit(solution)/shard_map/ppermute | solution.py:47
  27.8 4.1 %collective-permute-start.6 = (f32[520,512]{1,0:T(8,128)S(1)}, f32[520,512]{1,0:T(8,128)S(1)}, u32[]{:S(2)}, u32[]{:S(2)}) collective-permute-start(f32[520,512]{1,0:T(8,128)S(1)} %get-tuple-element.50), channel_id=1, source_target_pairs={{8,25},{24,9},{9,24},{25,8},{10,27},{26,11},{11,26},{27,10},{12,29... | collective-permute-start | bytes 3194888 | tf_op jit(solution)/shard_map/ppermute | solution.py:47
  31.9 13.2 %collective-permute-done.6.refs_1_ = f32[520,512]{1,0:T(8,128)S(1)} collective-permute-done((f32[520,512]{1,0:T(8,128)S(1)}, f32[520,512]{1,0:T(8,128)S(1)}, u32[]{:S(2)}, u32[]{:S(2)}) %collective-permute-start.6) | collective-permute-done | bytes 1064992 | tf_op jit(solution)/shard_map/ppermute | solution.py:47
  45.1 3.1 %collective-permute-start.8 = (f32[520,512]{1,0:T(8,128)S(1)}, f32[520,512]{1,0:T(8,128)S(1)}, u32[]{:S(2)}, u32[]{:S(2)}) collective-permute-start(f32[520,512]{1,0:T(8,128)S(1)} %get-tuple-element.57), channel_id=1, source_target_pairs={{8,24},{24,8},{9,25},{25,9},{10,26},{26,10},{11,27},{27,11},{12,28... | collective-permute-start | bytes 3194888 | tf_op jit(solution)/shard_map/ppermute | solution.py:47
  48.3 3.1 %collective-permute-start.7 = (f32[520,512]{1,0:T(8,128)S(1)}, f32[520,512]{1,0:T(8,128)S(1)}, u32[]{:S(2)}, u32[]{:S(2)}) collective-permute-start(f32[520,512]{1,0:T(8,128)S(1)} %get-tuple-element.56), channel_id=1, source_target_pairs={{8,9},{24,25},{9,8},{25,24},{10,11},{26,27},{11,10},{27,26},{12,13... | collective-permute-start | bytes 3194888 | tf_op jit(solution)/shard_map/ppermute | solution.py:47
  51.4 15.1 %collective-permute-done.8.refs_6_.refs_3_ = f32[520,512]{1,0:T(8,128)S(1)} collective-permute-done((f32[520,512]{1,0:T(8,128)S(1)}, f32[520,512]{1,0:T(8,128)S(1)}, u32[]{:S(2)}, u32[]{:S(2)}) %collective-permute-start.8) | collective-permute-done | bytes 1064992 | tf_op jit(solution)/shard_map/ppermute | solution.py:47
  66.5 2.5 %shard_map.39 = (f32[128,512]{1,0:T(8,128)S(1)}, f32[128,512]{1,0:T(8,128)S(1)}, f32[128,512]{1,0:T(8,128)S(1)}, f32[128,512]{1,0:T(8,128)S(1)}) custom-call(f32[2,2,520,512]{3,2,1,0:T(8,128)S(1)} %shard_map.38.refs_0_, f32[2,2,520,512]{3,2,1,0:T(8,128)S(1)} %collective-permute-done.9.refs_1_, f32[128,512]{1,0:T(8,128)S(1)} %get-tuple-element.58.refs_4_.refs_2_, ...), custom_call_target="tpu_custom_call" | custom-call | flops 1610612736 | bytes 4227072 | tf_op jit(solution)/shard_map/pallas_call | solution.py:266
  71.5 2.5 %collective-permute-start.11 = (f32[128,512]{1,0:T(8,128)S(1)}, f32[128,512]{1,0:T(8,128)S(1)}, u32[]{:S(2)}, u32[]{:S(2)}) collective-permute-start(f32[128,512]{1,0:T(8,128)S(1)} %get-tuple-element.66), channel_id=1, source_target_pairs={{0,17},{8,25},{16,1},{24,9},{1,16},{9,24},{17,0},{25,8},{2,19},{10... | collective-permute-start | bytes 786440 | tf_op jit(solution)/shard_map/ppermute | solution.py:47
  74.3 3.5 %collective-permute-done.11 = f32[128,512]{1,0:T(8,128)S(1)} collective-permute-done((f32[128,512]{1,0:T(8,128)S(1)}, f32[128,512]{1,0:T(8,128)S(1)}, u32[]{:S(2)}, u32[]{:S(2)}) %collective-permute-start.11) | collective-permute-done | bytes 262176 | tf_op jit(solution)/shard_map/ppermute | solution.py:47
  77.8 3.0 %collective-permute-done.12 = f32[128,512]{1,0:T(8,128)S(1)} collective-permute-done((f32[128,512]{1,0:T(8,128)S(1)}, f32[128,512]{1,0:T(8,128)S(1)}, u32[]{:S(2)}, u32[]{:S(2)}) %collective-permute-start.12) | collective-permute-done | bytes 262176 | tf_op jit(solution)/shard_map/ppermute | solution.py:47
  81.7 8.2 %collective-permute-done.15.refs_4_ = f32[128,512]{1,0:T(8,128)S(1)} collective-permute-done((f32[128,512]{1,0:T(8,128)S(1)}, f32[128,512]{1,0:T(8,128)S(1)}, u32[]{:S(2)}, u32[]{:S(2)}) %collective-permute-start.15) | collective-permute-done | bytes 262176 | tf_op jit(solution)/shard_map/ppermute | solution.py:47
  89.9 5.2 %collective-permute-done.16.refs_5_ = f32[128,512]{1,0:T(8,128)S(1)} collective-permute-done((f32[128,512]{1,0:T(8,128)S(1)}, f32[128,512]{1,0:T(8,128)S(1)}, u32[]{:S(2)}, u32[]{:S(2)}) %collective-permute-start.16) | collective-permute-done | bytes 262176 | tf_op jit(solution)/shard_map/ppermute | solution.py:47
  95.1 2.5 %shard_map.41 = (f32[128,512]{1,0:T(8,128)S(1)}, f32[128,512]{1,0:T(8,128)S(1)}, f32[128,512]{1,0:T(8,128)S(1)}, f32[128,512]{1,0:T(8,128)S(1)}) custom-call(f32[2,2,520,512]{3,2,1,0:T(8,128)S(1)} %collective-permute-done.10.refs_0_, f32[2,2,520,512]{3,2,1,0:T(8,128)S(1)} %shard_map.40.refs_1_, f32[128,512]{1,0:T(8,128)S(1)} %add_add_fusion.3.refs_2_, ...), custom_call_target="tpu_custom_call" | custom-call | flops 1610612736 | bytes 4227072 | tf_op jit(solution)/shard_map/pallas_call | solution.py:266
  97.6 1.7 %collective-permute-start.17 = (f32[128,512]{1,0:T(8,128)S(1)}, f32[128,512]{1,0:T(8,128)S(1)}, u32[]{:S(2)}, u32[]{:S(2)}) collective-permute-start(f32[128,512]{1,0:T(8,128)S(1)} %get-tuple-element.70), channel_id=1, source_target_pairs={{0,17},{8,25},{16,1},{24,9},{1,16},{9,24},{17,0},{25,8},{2,19},{10... | collective-permute-start | bytes 786440 | tf_op jit(solution)/shard_map/ppermute | solution.py:47
  100.3 3.8 %collective-permute-done.17 = f32[128,512]{1,0:T(8,128)S(1)} collective-permute-done((f32[128,512]{1,0:T(8,128)S(1)}, f32[128,512]{1,0:T(8,128)S(1)}, u32[]{:S(2)}, u32[]{:S(2)}) %collective-permute-start.17) | collective-permute-done | bytes 262176 | tf_op jit(solution)/shard_map/ppermute | solution.py:47
  104.1 2.4 %collective-permute-done.18 = f32[128,512]{1,0:T(8,128)S(1)} collective-permute-done((f32[128,512]{1,0:T(8,128)S(1)}, f32[128,512]{1,0:T(8,128)S(1)}, u32[]{:S(2)}, u32[]{:S(2)}) %collective-permute-start.18) | collective-permute-done | bytes 262176 | tf_op jit(solution)/shard_map/ppermute | solution.py:47
  107.9 2.4 %collective-permute-start.20 = (f32[128,512]{1,0:T(8,128)S(1)}, f32[128,512]{1,0:T(8,128)S(1)}, u32[]{:S(2)}, u32[]{:S(2)}) collective-permute-start(f32[128,512]{1,0:T(8,128)S(1)} %add_add_fusion.2.refs_2_), channel_id=1, source_target_pairs={{0,2},{8,10},{16,18},{24,26},{1,3},{9,11},{17,19},{25,27},{2,0},{1... | collective-permute-start | bytes 786440 | tf_op jit(solution)/shard_map/ppermute | solution.py:47
  110.3 3.7 %collective-permute-done.22.refs_5_ = f32[128,512]{1,0:T(8,128)S(1)} collective-permute-done((f32[128,512]{1,0:T(8,128)S(1)}, f32[128,512]{1,0:T(8,128)S(1)}, u32[]{:S(2)}, u32[]{:S(2)}) %collective-permute-start.22) | collective-permute-done | bytes 262176 | tf_op jit(solution)/shard_map/ppermute | solution.py:47
  114.0 6.1 %collective-permute-done.21.refs_4_ = f32[128,512]{1,0:T(8,128)S(1)} collective-permute-done((f32[128,512]{1,0:T(8,128)S(1)}, f32[128,512]{1,0:T(8,128)S(1)}, u32[]{:S(2)}, u32[]{:S(2)}) %collective-permute-start.21) | collective-permute-done | bytes 262176 | tf_op jit(solution)/shard_map/ppermute | solution.py:47
  120.1 2.5 %shard_map.42 = (f32[128,512]{1,0:T(8,128)S(1)}, f32[128,512]{1,0:T(8,128)S(1)}, f32[128,512]{1,0:T(8,128)S(1)}, f32[128,512]{1,0:T(8,128)S(1)}) custom-call(f32[2,2,520,512]{3,2,1,0:T(8,128)S(1)} %shard_map.38.refs_0_, f32[2,2,520,512]{3,2,1,0:T(8,128)S(1)} %collective-permute-done.9.refs_1_, f32[128,512]{1,0:T(8,128)S(1)} %add_add_fusion.2.refs_2_, ...), custom_call_target="tpu_custom_call" | custom-call | flops 1610612736 | bytes 4227072 | tf_op jit(solution)/shard_map/pallas_call | solution.py:266
  122.6 2.0 %collective-permute-start.23 = (f32[128,512]{1,0:T(8,128)S(1)}, f32[128,512]{1,0:T(8,128)S(1)}, u32[]{:S(2)}, u32[]{:S(2)}) collective-permute-start(f32[128,512]{1,0:T(8,128)S(1)} %get-tuple-element.74), channel_id=1, source_target_pairs={{0,17},{8,25},{16,1},{24,9},{1,16},{9,24},{17,0},{25,8},{2,19},{10... | collective-permute-start | bytes 786440 | tf_op jit(solution)/shard_map/ppermute | solution.py:47
  125.3 3.8 %collective-permute-done.23 = f32[128,512]{1,0:T(8,128)S(1)} collective-permute-done((f32[128,512]{1,0:T(8,128)S(1)}, f32[128,512]{1,0:T(8,128)S(1)}, u32[]{:S(2)}, u32[]{:S(2)}) %collective-permute-start.23) | collective-permute-done | bytes 262176 | tf_op jit(solution)/shard_map/ppermute | solution.py:47
  129.1 2.7 %collective-permute-done.24 = f32[128,512]{1,0:T(8,128)S(1)} collective-permute-done((f32[128,512]{1,0:T(8,128)S(1)}, f32[128,512]{1,0:T(8,128)S(1)}, u32[]{:S(2)}, u32[]{:S(2)}) %collective-permute-start.24) | collective-permute-done | bytes 262176 | tf_op jit(solution)/shard_map/ppermute | solution.py:47
  133.1 2.5 %collective-permute-start.26 = (f32[128,512]{1,0:T(8,128)S(1)}, f32[128,512]{1,0:T(8,128)S(1)}, u32[]{:S(2)}, u32[]{:S(2)}) collective-permute-start(f32[128,512]{1,0:T(8,128)S(1)} %add_add_fusion.1.refs_2_), channel_id=1, source_target_pairs={{0,2},{8,10},{16,18},{24,26},{1,3},{9,11},{17,19},{25,27},{2,0},{1... | collective-permute-start | bytes 786440 | tf_op jit(solution)/shard_map/ppermute | solution.py:47
  135.6 3.7 %collective-permute-done.28.refs_5_ = f32[128,512]{1,0:T(8,128)S(1)} collective-permute-done((f32[128,512]{1,0:T(8,128)S(1)}, f32[128,512]{1,0:T(8,128)S(1)}, u32[]{:S(2)}, u32[]{:S(2)}) %collective-permute-start.28) | collective-permute-done | bytes 262176 | tf_op jit(solution)/shard_map/ppermute | solution.py:47
  139.3 5.5 %collective-permute-done.27.refs_4_ = f32[128,512]{1,0:T(8,128)S(1)} collective-permute-done((f32[128,512]{1,0:T(8,128)S(1)}, f32[128,512]{1,0:T(8,128)S(1)}, u32[]{:S(2)}, u32[]{:S(2)}) %collective-permute-start.27) | collective-permute-done | bytes 262176 | tf_op jit(solution)/shard_map/ppermute | solution.py:47
  144.7 2.5 %shard_map.43 = (f32[256,256]{1,0:T(8,128)S(1)}, f32[256,256]{1,0:T(8,128)S(1)}, f32[256,256]{1,0:T(8,128)S(1)}, f32[256,256]{1,0:T(8,128)S(1)}) custom-call(f32[2,2,520,512]{3,2,1,0:T(8,128)S(1)} %collective-permute-done.10.refs_0_, f32[2,2,520,512]{3,2,1,0:T(8,128)S(1)} %shard_map.40.refs_1_, f32[128,512]{1,0:T(8,128)S(1)} %add_add_fusion.1.refs_2_, ...), custom_call_target="tpu_custom_call" | custom-call | flops 1610612736 | bytes 4227072 | tf_op jit(solution)/shard_map/pallas_call | solution.py:266
  147.2 2.0 %collective-permute-start.29 = (f32[256,256]{1,0:T(8,128)S(1)}, f32[256,256]{1,0:T(8,128)S(1)}, u32[]{:S(2)}, u32[]{:S(2)}) collective-permute-start(f32[256,256]{1,0:T(8,128)S(1)} %get-tuple-element.78), channel_id=1, source_target_pairs={{0,17},{8,25},{16,1},{24,9},{1,16},{9,24},{17,0},{25,8},{2,19},{10... | collective-permute-start | bytes 786440 | tf_op jit(solution)/shard_map/ppermute | solution.py:47
  150.0 3.6 %collective-permute-done.29 = f32[256,256]{1,0:T(8,128)S(1)} collective-permute-done((f32[256,256]{1,0:T(8,128)S(1)}, f32[256,256]{1,0:T(8,128)S(1)}, u32[]{:S(2)}, u32[]{:S(2)}) %collective-permute-start.29) | collective-permute-done | bytes 262176 | tf_op jit(solution)/shard_map/ppermute | solution.py:47
  153.5 2.6 %collective-permute-done.30 = f32[256,256]{1,0:T(8,128)S(1)} collective-permute-done((f32[256,256]{1,0:T(8,128)S(1)}, f32[256,256]{1,0:T(8,128)S(1)}, u32[]{:S(2)}, u32[]{:S(2)}) %collective-permute-start.30) | collective-permute-done | bytes 262176 | tf_op jit(solution)/shard_map/ppermute | solution.py:47
  (47 shorter events, 15.6 us)
Async XLA Ops:
  4.5 21.9 %collective-permute-start.3 = (f32[520,512]{1,0:T(8,128)S(1)}, f32[520,512]{1,0:T(8,128)S(1)}, u32[]{:S(2)}, u32[]{:S(2)}) collective-permute-start(f32[520,512]{1,0:T(8,128)S(1)} %get-tuple-element.50), channel_id=1, source_target_pairs={{0,17},{16,1},{1,16},{17,0},{2,19},{18,3},{3,18},{19,2},{4,21},{20... | collective-permute-start | bytes 3194888 | tf_op jit(solution)/shard_map/ppermute | solution.py:47
  5.3 21.2 %collective-permute-start.4 = (f32[520,512]{1,0:T(8,128)S(1)}, f32[520,512]{1,0:T(8,128)S(1)}, u32[]{:S(2)}, u32[]{:S(2)}) collective-permute-start(f32[520,512]{1,0:T(8,128)S(1)} %get-tuple-element.56), channel_id=1, source_target_pairs={{0,1},{16,17},{1,0},{17,16},{2,3},{18,19},{3,2},{19,18},{4,5},{20,... | collective-permute-start | bytes 3194888 | tf_op jit(solution)/shard_map/ppermute | solution.py:47
  6.0 20.4 %collective-permute-start.5 = (f32[520,512]{1,0:T(8,128)S(1)}, f32[520,512]{1,0:T(8,128)S(1)}, u32[]{:S(2)}, u32[]{:S(2)}) collective-permute-start(f32[520,512]{1,0:T(8,128)S(1)} %get-tuple-element.57), channel_id=1, source_target_pairs={{0,16},{16,0},{1,17},{17,1},{2,18},{18,2},{3,19},{19,3},{4,20},{20... | collective-permute-start | bytes 3194888 | tf_op jit(solution)/shard_map/ppermute | solution.py:47
  6.7 9.2 %collective-permute-start.1 = (f32[128,512]{1,0:T(8,128)S(1)}, f32[128,512]{1,0:T(8,128)S(1)}, u32[]{:S(2)}, u32[]{:S(2)}) collective-permute-start(f32[128,512]{1,0:T(8,128)S(1)} %get-tuple-element.58.refs_4_.refs_2_), channel_id=1, source_target_pairs={{0,4},{8,12},{16,20},{24,28},{1,5},{9,13},{17,21},{25,29},{2,6},{1... | collective-permute-start | bytes 786440 | tf_op jit(solution)/shard_map/ppermute | solution.py:47
  6.9 9.1 %collective-permute-start = (f32[128,512]{1,0:T(8,128)S(1)}, f32[128,512]{1,0:T(8,128)S(1)}, u32[]{:S(2)}, u32[]{:S(2)}) collective-permute-start(f32[128,512]{1,0:T(8,128)S(1)} %get-tuple-element.58.refs_4_.refs_2_), channel_id=1, source_target_pairs={{0,2},{8,10},{16,18},{24,26},{1,3},{9,11},{17,19},{25,27},{2,0},{1... | collective-permute-start | bytes 786440 | tf_op jit(solution)/shard_map/ppermute | solution.py:47
  15.9 10.5 %collective-permute-start.2 = (f32[128,512]{1,0:T(8,128)S(1)}, f32[128,512]{1,0:T(8,128)S(1)}, u32[]{:S(2)}, u32[]{:S(2)}) collective-permute-start(f32[128,512]{1,0:T(8,128)S(1)} %collective-permute-done.1.refs_6_.refs_4_), channel_id=1, source_target_pairs={{0,2},{8,10},{16,18},{24,26},{1,3},{9,11},{17,19},{25,27},{2,0},{1... | collective-permute-start | bytes 786440 | tf_op jit(solution)/shard_map/ppermute | solution.py:47
  26.5 39.9 %collective-permute-start.9 = (f32[2,2,520,512]{3,2,1,0:T(8,128)S(1)}, f32[2,2,520,512]{3,2,1,0:T(8,128)S(1)}, u32[]{:S(2)}, u32[]{:S(2)}) collective-permute-start(f32[2,2,520,512]{3,2,1,0:T(8,128)S(1)} %shard_map.38.refs_0_), channel_id=1, source_target_pairs={{0,8},{16,24},{1,9},{17,25},{2,10},{18,26},{3,11},{19,27},{4,12},{... | collective-permute-start | bytes 12779528 | tf_op jit(solution)/shard_map/ppermute | solution.py:47
  27.8 17.3 %collective-permute-start.6 = (f32[520,512]{1,0:T(8,128)S(1)}, f32[520,512]{1,0:T(8,128)S(1)}, u32[]{:S(2)}, u32[]{:S(2)}) collective-permute-start(f32[520,512]{1,0:T(8,128)S(1)} %get-tuple-element.50), channel_id=1, source_target_pairs={{8,25},{24,9},{9,24},{25,8},{10,27},{26,11},{11,26},{27,10},{12,29... | collective-permute-start | bytes 3194888 | tf_op jit(solution)/shard_map/ppermute | solution.py:47
  45.1 21.3 %collective-permute-start.8 = (f32[520,512]{1,0:T(8,128)S(1)}, f32[520,512]{1,0:T(8,128)S(1)}, u32[]{:S(2)}, u32[]{:S(2)}) collective-permute-start(f32[520,512]{1,0:T(8,128)S(1)} %get-tuple-element.57), channel_id=1, source_target_pairs={{8,24},{24,8},{9,25},{25,9},{10,26},{26,10},{11,27},{27,11},{12,28... | collective-permute-start | bytes 3194888 | tf_op jit(solution)/shard_map/ppermute | solution.py:47
  48.3 20.8 %collective-permute-start.7 = (f32[520,512]{1,0:T(8,128)S(1)}, f32[520,512]{1,0:T(8,128)S(1)}, u32[]{:S(2)}, u32[]{:S(2)}) collective-permute-start(f32[520,512]{1,0:T(8,128)S(1)} %get-tuple-element.56), channel_id=1, source_target_pairs={{8,9},{24,25},{9,8},{25,24},{10,11},{26,27},{11,10},{27,26},{12,13... | collective-permute-start | bytes 3194888 | tf_op jit(solution)/shard_map/ppermute | solution.py:47
  69.9 25.2 %collective-permute-start.10 = (f32[2,2,520,512]{3,2,1,0:T(8,128)S(1)}, f32[2,2,520,512]{3,2,1,0:T(8,128)S(1)}, u32[]{:S(2)}, u32[]{:S(2)}) collective-permute-start(f32[2,2,520,512]{3,2,1,0:T(8,128)S(1)} %shard_map.40.refs_1_), channel_id=1, source_target_pairs={{8,0},{24,16},{9,1},{25,17},{10,2},{26,18},{11,3},{27,19},{12,4},{... | collective-permute-start | bytes 12779528 | tf_op jit(solution)/shard_map/ppermute | solution.py:47
  71.5 6.3 %collective-permute-start.11 = (f32[128,512]{1,0:T(8,128)S(1)}, f32[128,512]{1,0:T(8,128)S(1)}, u32[]{:S(2)}, u32[]{:S(2)}) collective-permute-start(f32[128,512]{1,0:T(8,128)S(1)} %get-tuple-element.66), channel_id=1, source_target_pairs={{0,17},{8,25},{16,1},{24,9},{1,16},{9,24},{17,0},{25,8},{2,19},{10... | collective-permute-start | bytes 786440 | tf_op jit(solution)/shard_map/ppermute | solution.py:47
  73.9 6.9 %collective-permute-start.12 = (f32[128,512]{1,0:T(8,128)S(1)}, f32[128,512]{1,0:T(8,128)S(1)}, u32[]{:S(2)}, u32[]{:S(2)}) collective-permute-start(f32[128,512]{1,0:T(8,128)S(1)} %get-tuple-element.67), channel_id=1, source_target_pairs={{0,1},{8,9},{16,17},{24,25},{1,0},{9,8},{17,16},{25,24},{2,3},{10,... | collective-permute-start | bytes 786440 | tf_op jit(solution)/shard_map/ppermute | solution.py:47
  74.2 6.6 %collective-permute-start.13 = (f32[128,512]{1,0:T(8,128)S(1)}, f32[128,512]{1,0:T(8,128)S(1)}, u32[]{:S(2)}, u32[]{:S(2)}) collective-permute-start(f32[128,512]{1,0:T(8,128)S(1)} %get-tuple-element.68), channel_id=1, source_target_pairs={{0,16},{8,24},{16,0},{24,8},{1,17},{9,25},{17,1},{25,9},{2,18},{10... | collective-permute-start | bytes 786440 | tf_op jit(solution)/shard_map/ppermute | solution.py:47
  80.9 9.0 %collective-permute-start.15 = (f32[128,512]{1,0:T(8,128)S(1)}, f32[128,512]{1,0:T(8,128)S(1)}, u32[]{:S(2)}, u32[]{:S(2)}) collective-permute-start(f32[128,512]{1,0:T(8,128)S(1)} %add_add_fusion.3.refs_2_), channel_id=1, source_target_pairs={{0,4},{8,12},{16,20},{24,28},{1,5},{9,13},{17,21},{25,29},{2,6},{1... | collective-permute-start | bytes 786440 | tf_op jit(solution)/shard_map/ppermute | solution.py:47
  81.2 8.6 %collective-permute-start.14 = (f32[128,512]{1,0:T(8,128)S(1)}, f32[128,512]{1,0:T(8,128)S(1)}, u32[]{:S(2)}, u32[]{:S(2)}) collective-permute-start(f32[128,512]{1,0:T(8,128)S(1)} %add_add_fusion.3.refs_2_), channel_id=1, source_target_pairs={{0,2},{8,10},{16,18},{24,26},{1,3},{9,11},{17,19},{25,27},{2,0},{1... | collective-permute-start | bytes 786440 | tf_op jit(solution)/shard_map/ppermute | solution.py:47
  89.9 5.2 %collective-permute-start.16 = (f32[128,512]{1,0:T(8,128)S(1)}, f32[128,512]{1,0:T(8,128)S(1)}, u32[]{:S(2)}, u32[]{:S(2)}) collective-permute-start(f32[128,512]{1,0:T(8,128)S(1)} %collective-permute-done.15.refs_4_), channel_id=1, source_target_pairs={{0,2},{8,10},{16,18},{24,26},{1,3},{9,11},{17,19},{25,27},{2,0},{1... | collective-permute-start | bytes 786440 | tf_op jit(solution)/shard_map/ppermute | solution.py:47
  97.6 6.5 %collective-permute-start.17 = (f32[128,512]{1,0:T(8,128)S(1)}, f32[128,512]{1,0:T(8,128)S(1)}, u32[]{:S(2)}, u32[]{:S(2)}) collective-permute-start(f32[128,512]{1,0:T(8,128)S(1)} %get-tuple-element.70), channel_id=1, source_target_pairs={{0,17},{8,25},{16,1},{24,9},{1,16},{9,24},{17,0},{25,8},{2,19},{10... | collective-permute-start | bytes 786440 | tf_op jit(solution)/shard_map/ppermute | solution.py:47
  99.3 7.1 %collective-permute-start.18 = (f32[128,512]{1,0:T(8,128)S(1)}, f32[128,512]{1,0:T(8,128)S(1)}, u32[]{:S(2)}, u32[]{:S(2)}) collective-permute-start(f32[128,512]{1,0:T(8,128)S(1)} %get-tuple-element.71), channel_id=1, source_target_pairs={{0,1},{8,9},{16,17},{24,25},{1,0},{9,8},{17,16},{25,24},{2,3},{10,... | collective-permute-start | bytes 786440 | tf_op jit(solution)/shard_map/ppermute | solution.py:47
  99.6 7.0 %collective-permute-start.19 = (f32[128,512]{1,0:T(8,128)S(1)}, f32[128,512]{1,0:T(8,128)S(1)}, u32[]{:S(2)}, u32[]{:S(2)}) collective-permute-start(f32[128,512]{1,0:T(8,128)S(1)} %get-tuple-element.72), channel_id=1, source_target_pairs={{0,16},{8,24},{16,0},{24,8},{1,17},{9,25},{17,1},{25,9},{2,18},{10... | collective-permute-start | bytes 786440 | tf_op jit(solution)/shard_map/ppermute | solution.py:47
  106.7 7.3 %collective-permute-start.22 = (f32[128,512]{1,0:T(8,128)S(1)}, f32[128,512]{1,0:T(8,128)S(1)}, u32[]{:S(2)}, u32[]{:S(2)}) collective-permute-start(f32[128,512]{1,0:T(8,128)S(1)} %add_add_fusion.2.refs_2_), channel_id=1, source_target_pairs={{0,6},{8,14},{16,22},{24,30},{1,7},{9,15},{17,23},{25,31},{2,4},{1... | collective-permute-start | bytes 786440 | tf_op jit(solution)/shard_map/ppermute | solution.py:47
  107.6 12.6 %collective-permute-start.21 = (f32[128,512]{1,0:T(8,128)S(1)}, f32[128,512]{1,0:T(8,128)S(1)}, u32[]{:S(2)}, u32[]{:S(2)}) collective-permute-start(f32[128,512]{1,0:T(8,128)S(1)} %add_add_fusion.2.refs_2_), channel_id=1, source_target_pairs={{0,4},{8,12},{16,20},{24,28},{1,5},{9,13},{17,21},{25,29},{2,6},{1... | collective-permute-start | bytes 786440 | tf_op jit(solution)/shard_map/ppermute | solution.py:47
  107.9 12.2 %collective-permute-start.20 = (f32[128,512]{1,0:T(8,128)S(1)}, f32[128,512]{1,0:T(8,128)S(1)}, u32[]{:S(2)}, u32[]{:S(2)}) collective-permute-start(f32[128,512]{1,0:T(8,128)S(1)} %add_add_fusion.2.refs_2_), channel_id=1, source_target_pairs={{0,2},{8,10},{16,18},{24,26},{1,3},{9,11},{17,19},{25,27},{2,0},{1... | collective-permute-start | bytes 786440 | tf_op jit(solution)/shard_map/ppermute | solution.py:47
  122.6 6.5 %collective-permute-start.23 = (f32[128,512]{1,0:T(8,128)S(1)}, f32[128,512]{1,0:T(8,128)S(1)}, u32[]{:S(2)}, u32[]{:S(2)}) collective-permute-start(f32[128,512]{1,0:T(8,128)S(1)} %get-tuple-element.74), channel_id=1, source_target_pairs={{0,17},{8,25},{16,1},{24,9},{1,16},{9,24},{17,0},{25,8},{2,19},{10... | collective-permute-start | bytes 786440 | tf_op jit(solution)/shard_map/ppermute | solution.py:47
  124.6 7.2 %collective-permute-start.24 = (f32[128,512]{1,0:T(8,128)S(1)}, f32[128,512]{1,0:T(8,128)S(1)}, u32[]{:S(2)}, u32[]{:S(2)}) collective-permute-start(f32[128,512]{1,0:T(8,128)S(1)} %get-tuple-element.75), channel_id=1, source_target_pairs={{0,1},{8,9},{16,17},{24,25},{1,0},{9,8},{17,16},{25,24},{2,3},{10,... | collective-permute-start | bytes 786440 | tf_op jit(solution)/shard_map/ppermute | solution.py:47
  124.9 7.0 %collective-permute-start.25 = (f32[128,512]{1,0:T(8,128)S(1)}, f32[128,512]{1,0:T(8,128)S(1)}, u32[]{:S(2)}, u32[]{:S(2)}) collective-permute-start(f32[128,512]{1,0:T(8,128)S(1)} %get-tuple-element.76), channel_id=1, source_target_pairs={{0,16},{8,24},{16,0},{24,8},{1,17},{9,25},{17,1},{25,9},{2,18},{10... | collective-permute-start | bytes 786440 | tf_op jit(solution)/shard_map/ppermute | solution.py:47
  132.0 7.3 %collective-permute-start.28 = (f32[128,512]{1,0:T(8,128)S(1)}, f32[128,512]{1,0:T(8,128)S(1)}, u32[]{:S(2)}, u32[]{:S(2)}) collective-permute-start(f32[128,512]{1,0:T(8,128)S(1)} %add_add_fusion.1.refs_2_), channel_id=1, source_target_pairs={{0,6},{8,14},{16,22},{24,30},{1,7},{9,15},{17,23},{25,31},{2,4},{1... | collective-permute-start | bytes 786440 | tf_op jit(solution)/shard_map/ppermute | solution.py:47
  133.1 11.6 %collective-permute-start.27 = (f32[128,512]{1,0:T(8,128)S(1)}, f32[128,512]{1,0:T(8,128)S(1)}, u32[]{:S(2)}, u32[]{:S(2)}) collective-permute-start(f32[128,512]{1,0:T(8,128)S(1)} %add_add_fusion.1.refs_2_), channel_id=1, source_target_pairs={{0,4},{8,12},{16,20},{24,28},{1,5},{9,13},{17,21},{25,29},{2,6},{1... | collective-permute-start | bytes 786440 | tf_op jit(solution)/shard_map/ppermute | solution.py:47
  133.1 11.6 %collective-permute-start.26 = (f32[128,512]{1,0:T(8,128)S(1)}, f32[128,512]{1,0:T(8,128)S(1)}, u32[]{:S(2)}, u32[]{:S(2)}) collective-permute-start(f32[128,512]{1,0:T(8,128)S(1)} %add_add_fusion.1.refs_2_), channel_id=1, source_target_pairs={{0,2},{8,10},{16,18},{24,26},{1,3},{9,11},{17,19},{25,27},{2,0},{1... | collective-permute-start | bytes 786440 | tf_op jit(solution)/shard_map/ppermute | solution.py:47
  147.2 6.3 %collective-permute-start.29 = (f32[256,256]{1,0:T(8,128)S(1)}, f32[256,256]{1,0:T(8,128)S(1)}, u32[]{:S(2)}, u32[]{:S(2)}) collective-permute-start(f32[256,256]{1,0:T(8,128)S(1)} %get-tuple-element.78), channel_id=1, source_target_pairs={{0,17},{8,25},{16,1},{24,9},{1,16},{9,24},{17,0},{25,8},{2,19},{10... | collective-permute-start | bytes 786440 | tf_op jit(solution)/shard_map/ppermute | solution.py:47
  149.3 6.9 %collective-permute-start.30 = (f32[256,256]{1,0:T(8,128)S(1)}, f32[256,256]{1,0:T(8,128)S(1)}, u32[]{:S(2)}, u32[]{:S(2)}) collective-permute-start(f32[256,256]{1,0:T(8,128)S(1)} %get-tuple-element.79), channel_id=1, source_target_pairs={{0,1},{8,9},{16,17},{24,25},{1,0},{9,8},{17,16},{25,24},{2,3},{10,... | collective-permute-start | bytes 786440 | tf_op jit(solution)/shard_map/ppermute | solution.py:47
  149.5 6.7 %collective-permute-start.31 = (f32[256,256]{1,0:T(8,128)S(1)}, f32[256,256]{1,0:T(8,128)S(1)}, u32[]{:S(2)}, u32[]{:S(2)}) collective-permute-start(f32[256,256]{1,0:T(8,128)S(1)} %get-tuple-element.80), channel_id=1, source_target_pairs={{0,16},{8,24},{16,0},{24,8},{1,17},{9,25},{17,1},{25,9},{2,18},{10... | collective-permute-start | bytes 786440 | tf_op jit(solution)/shard_map/ppermute | solution.py:47
  (2 other events, 1.9 us)

commit v7 on v6

--- a/solution.py
+++ b/solution.py
@@ -150,7 +150,7 @@
 
 
 def collect_kernel(grid, sites, keys, *refs):
-    pieces, (out_ref, held_ref, in_sems, out_sems) = dict(zip(keys, refs)), refs[-4:]
+    pieces, (out_ref, in_sems) = dict(zip(keys, refs)), refs[-2:]
     _, _, y, core = grid.here()
 
     @pl.when(core == sites[0] % grid.cores)
@@ -161,16 +161,11 @@
 
                 @pl.when(behind == dy)
                 def _():
-                    pltpu.make_async_copy(pieces[dx, dy], held_ref.at[k, dx], in_sems.at[k, dx]).start()
-
-        outward = []
+                    pltpu.make_async_copy(pieces[dx, dy], out_ref.at[k, dx], in_sems.at[k, dx]).start()
+
         for k in range(len(sites)):
             for dx in range(grid.nx):
-                pltpu.make_async_copy(refs[0], held_ref.at[k, dx], in_sems.at[k, dx]).wait()
-                outward.append(pltpu.make_async_copy(held_ref.at[k, dx], out_ref.at[k, dx], out_sems.at[k, dx]))
-                outward[-1].start()
-        for copy in outward:
-            copy.wait()
+                pltpu.make_async_copy(refs[0], out_ref.at[k, dx], in_sems.at[k, dx]).wait()
 
 
 def collect(grid, sites, pieces, token=()):
@@ -185,10 +180,8 @@
             functools.partial(collect_kernel, grid, tuple(sites), keys),
             out_shape=jax.ShapeDtypeStruct(shape, jnp.float32),
             in_specs=[hbm] * len(operands),
-            out_specs=hbm,
+            out_specs=pl.BlockSpec(memory_space=pltpu.VMEM),
             scratch_shapes=[
-                pltpu.VMEM(shape, jnp.float32),
-                pltpu.SemaphoreType.DMA(shape[:2]),
                 pltpu.SemaphoreType.DMA(shape[:2]),
             ],
             compiler_params=pltpu.CompilerParams(vmem_limit_bytes=32 * 1024 * 1024),

time: 160 us -> 159 us (level)
  transfers between devices with their start and end apart: 32 -> 32, of which waited for: 22 -> 20; matrix products, arithmetic and copies ran while one was open for 0% -> 0% of each run, Pallas kernels for 2% -> 2%
where the time goes in v7:
time: 159 us; the launch traced here: 157 us
  waiting for transfers between devices  106 us (67%)
  starting transfers between devices  34.6 us (22%)
  Pallas kernels  13 us (8%)
  local copies, waits for them, and re-layouts  1.91 us (1%)
    ppermute x32, waiting for transfers between devices, send(): return lax.ppermute(value, ('site', 'bond'), pairs)  106 us
    ppermute x32, starting transfers between devices, send(): return lax.ppermute(value, ('site', 'bond'), pairs)  34.6 us
    pallas_call x4, Pallas kernels, site_product(): pl.pallas_call(functools.partial(site_kernel, grid, site, last, len(token...  9.92 us
  transfers between devices with their start and end apart: 32, of which 20 were waited for; matrix products, arithmetic and copies ran while one was open for 0% of the time, Pallas kernels for 2%

profile of v7, /device:TPU:25, one launch (start us, length us, event | category | flops | bytes accessed | tf_op | source)
XLA Modules:
  0.0 156.6 jit_solution(14832708527722221521)
XLA Ops:
  1.9 2.6 %shard_map.37 = (f32[520,512]{1,0:T(8,128)S(1)}, f32[520,512]{1,0:T(8,128)S(1)}, f32[520,512]{1,0:T(8,128)S(1)}, f32[520,512]{1,0:T(8,128)S(1)}, f32[128,512]{1,0:T(8,128)S(1)}) custom-call(s32[1,1024]{1,0:T(1,128)S(1)} %copy-done.1, f32[2,256,2048]{2,1,0:T(8,128)} %bitcast.1, f32[256,1024]{1,0:T(8,128)S(1)} %copy-done), custom_call_target="tpu_custom_call" | custom-call | bytes 8388608 | tf_op jit(solution)/shard_map/pallas_call | solution.py:124
  7.0 8.9 %collective-permute-done.1.refs_6_.refs_4_ = f32[128,512]{1,0:T(8,128)S(1)} collective-permute-done((f32[128,512]{1,0:T(8,128)S(1)}, f32[128,512]{1,0:T(8,128)S(1)}, u32[]{:S(2)}, u32[]{:S(2)}) %collective-permute-start.1) | collective-permute-done | bytes 262176 | tf_op jit(solution)/shard_map/ppermute | solution.py:47
  15.9 10.5 %collective-permute-done.2.refs_7_.refs_5_ = f32[128,512]{1,0:T(8,128)S(1)} collective-permute-done((f32[128,512]{1,0:T(8,128)S(1)}, f32[128,512]{1,0:T(8,128)S(1)}, u32[]{:S(2)}, u32[]{:S(2)}) %collective-permute-start.2) | collective-permute-done | bytes 262176 | tf_op jit(solution)/shard_map/ppermute | solution.py:47
  27.8 4.1 %collective-permute-start.6 = (f32[520,512]{1,0:T(8,128)S(1)}, f32[520,512]{1,0:T(8,128)S(1)}, u32[]{:S(2)}, u32[]{:S(2)}) collective-permute-start(f32[520,512]{1,0:T(8,128)S(1)} %get-tuple-element.50), channel_id=1, source_target_pairs={{8,25},{24,9},{9,24},{25,8},{10,27},{26,11},{11,26},{27,10},{12,29... | collective-permute-start | bytes 3194888 | tf_op jit(solution)/shard_map/ppermute | solution.py:47
  31.9 13.2 %collective-permute-done.6.refs_1_ = f32[520,512]{1,0:T(8,128)S(1)} collective-permute-done((f32[520,512]{1,0:T(8,128)S(1)}, f32[520,512]{1,0:T(8,128)S(1)}, u32[]{:S(2)}, u32[]{:S(2)}) %collective-permute-start.6) | collective-permute-done | bytes 1064992 | tf_op jit(solution)/shard_map/ppermute | solution.py:47
  45.1 3.1 %collective-permute-start.8 = (f32[520,512]{1,0:T(8,128)S(1)}, f32[520,512]{1,0:T(8,128)S(1)}, u32[]{:S(2)}, u32[]{:S(2)}) collective-permute-start(f32[520,512]{1,0:T(8,128)S(1)} %get-tuple-element.57), channel_id=1, source_target_pairs={{8,24},{24,8},{9,25},{25,9},{10,26},{26,10},{11,27},{27,11},{12,28... | collective-permute-start | bytes 3194888 | tf_op jit(solution)/shard_map/ppermute | solution.py:47
  48.3 3.1 %collective-permute-start.7 = (f32[520,512]{1,0:T(8,128)S(1)}, f32[520,512]{1,0:T(8,128)S(1)}, u32[]{:S(2)}, u32[]{:S(2)}) collective-permute-start(f32[520,512]{1,0:T(8,128)S(1)} %get-tuple-element.56), channel_id=1, source_target_pairs={{8,9},{24,25},{9,8},{25,24},{10,11},{26,27},{11,10},{27,26},{12,13... | collective-permute-start | bytes 3194888 | tf_op jit(solution)/shard_map/ppermute | solution.py:47
  51.4 15.1 %collective-permute-done.8.refs_6_.refs_3_ = f32[520,512]{1,0:T(8,128)S(1)} collective-permute-done((f32[520,512]{1,0:T(8,128)S(1)}, f32[520,512]{1,0:T(8,128)S(1)}, u32[]{:S(2)}, u32[]{:S(2)}) %collective-permute-start.8) | collective-permute-done | bytes 1064992 | tf_op jit(solution)/shard_map/ppermute | solution.py:47
  66.5 2.5 %shard_map.39 = (f32[128,512]{1,0:T(8,128)S(1)}, f32[128,512]{1,0:T(8,128)S(1)}, f32[128,512]{1,0:T(8,128)S(1)}, f32[128,512]{1,0:T(8,128)S(1)}) custom-call(f32[2,2,520,512]{3,2,1,0:T(8,128)S(1)} %shard_map.38.refs_0_, f32[2,2,520,512]{3,2,1,0:T(8,128)S(1)} %collective-permute-done.9.refs_1_, f32[128,512]{1,0:T(8,128)S(1)} %get-tuple-element.58.refs_4_.refs_2_, ...), custom_call_target="tpu_custom_call" | custom-call | flops 1610612736 | bytes 4227072 | tf_op jit(solution)/shard_map/pallas_call | solution.py:259
  71.0 2.5 %collective-permute-start.11 = (f32[128,512]{1,0:T(8,128)S(1)}, f32[128,512]{1,0:T(8,128)S(1)}, u32[]{:S(2)}, u32[]{:S(2)}) collective-permute-start(f32[128,512]{1,0:T(8,128)S(1)} %get-tuple-element.66), channel_id=1, source_target_pairs={{0,17},{8,25},{16,1},{24,9},{1,16},{9,24},{17,0},{25,8},{2,19},{10... | collective-permute-start | bytes 786440 | tf_op jit(solution)/shard_map/ppermute | solution.py:47
  73.9 3.5 %collective-permute-done.11 = f32[128,512]{1,0:T(8,128)S(1)} collective-permute-done((f32[128,512]{1,0:T(8,128)S(1)}, f32[128,512]{1,0:T(8,128)S(1)}, u32[]{:S(2)}, u32[]{:S(2)}) %collective-permute-start.11) | collective-permute-done | bytes 262176 | tf_op jit(solution)/shard_map/ppermute | solution.py:47
  77.4 3.0 %collective-permute-done.12 = f32[128,512]{1,0:T(8,128)S(1)} collective-permute-done((f32[128,512]{1,0:T(8,128)S(1)}, f32[128,512]{1,0:T(8,128)S(1)}, u32[]{:S(2)}, u32[]{:S(2)}) %collective-permute-start.12) | collective-permute-done | bytes 262176 | tf_op jit(solution)/shard_map/ppermute | solution.py:47
  81.1 8.3 %collective-permute-done.15.refs_4_ = f32[128,512]{1,0:T(8,128)S(1)} collective-permute-done((f32[128,512]{1,0:T(8,128)S(1)}, f32[128,512]{1,0:T(8,128)S(1)}, u32[]{:S(2)}, u32[]{:S(2)}) %collective-permute-start.15) | collective-permute-done | bytes 262176 | tf_op jit(solution)/shard_map/ppermute | solution.py:47
  89.5 5.2 %collective-permute-done.16.refs_5_ = f32[128,512]{1,0:T(8,128)S(1)} collective-permute-done((f32[128,512]{1,0:T(8,128)S(1)}, f32[128,512]{1,0:T(8,128)S(1)}, u32[]{:S(2)}, u32[]{:S(2)}) %collective-permute-start.16) | collective-permute-done | bytes 262176 | tf_op jit(solution)/shard_map/ppermute | solution.py:47
  94.7 2.5 %shard_map.41 = (f32[128,512]{1,0:T(8,128)S(1)}, f32[128,512]{1,0:T(8,128)S(1)}, f32[128,512]{1,0:T(8,128)S(1)}, f32[128,512]{1,0:T(8,128)S(1)}) custom-call(f32[2,2,520,512]{3,2,1,0:T(8,128)S(1)} %collective-permute-done.10.refs_0_, f32[2,2,520,512]{3,2,1,0:T(8,128)S(1)} %shard_map.40.refs_1_, f32[128,512]{1,0:T(8,128)S(1)} %add_add_fusion.3.refs_2_, ...), custom_call_target="tpu_custom_call" | custom-call | flops 1610612736 | bytes 4227072 | tf_op jit(solution)/shard_map/pallas_call | solution.py:259
  97.2 1.7 %collective-permute-start.17 = (f32[128,512]{1,0:T(8,128)S(1)}, f32[128,512]{1,0:T(8,128)S(1)}, u32[]{:S(2)}, u32[]{:S(2)}) collective-permute-start(f32[128,512]{1,0:T(8,128)S(1)} %get-tuple-element.70), channel_id=1, source_target_pairs={{0,17},{8,25},{16,1},{24,9},{1,16},{9,24},{17,0},{25,8},{2,19},{10... | collective-permute-start | bytes 786440 | tf_op jit(solution)/shard_map/ppermute | solution.py:47
  99.9 3.8 %collective-permute-done.17 = f32[128,512]{1,0:T(8,128)S(1)} collective-permute-done((f32[128,512]{1,0:T(8,128)S(1)}, f32[128,512]{1,0:T(8,128)S(1)}, u32[]{:S(2)}, u32[]{:S(2)}) %collective-permute-start.17) | collective-permute-done | bytes 262176 | tf_op jit(solution)/shard_map/ppermute | solution.py:47
  103.7 2.4 %collective-permute-done.18 = f32[128,512]{1,0:T(8,128)S(1)} collective-permute-done((f32[128,512]{1,0:T(8,128)S(1)}, f32[128,512]{1,0:T(8,128)S(1)}, u32[]{:S(2)}, u32[]{:S(2)}) %collective-permute-start.18) | collective-permute-done | bytes 262176 | tf_op jit(solution)/shard_map/ppermute | solution.py:47
  107.5 2.4 %collective-permute-start.20 = (f32[128,512]{1,0:T(8,128)S(1)}, f32[128,512]{1,0:T(8,128)S(1)}, u32[]{:S(2)}, u32[]{:S(2)}) collective-permute-start(f32[128,512]{1,0:T(8,128)S(1)} %add_add_fusion.2.refs_2_), channel_id=1, source_target_pairs={{0,2},{8,10},{16,18},{24,26},{1,3},{9,11},{17,19},{25,27},{2,0},{1... | collective-permute-start | bytes 786440 | tf_op jit(solution)/shard_map/ppermute | solution.py:47
  109.9 3.7 %collective-permute-done.22.refs_5_ = f32[128,512]{1,0:T(8,128)S(1)} collective-permute-done((f32[128,512]{1,0:T(8,128)S(1)}, f32[128,512]{1,0:T(8,128)S(1)}, u32[]{:S(2)}, u32[]{:S(2)}) %collective-permute-start.22) | collective-permute-done | bytes 262176 | tf_op jit(solution)/shard_map/ppermute | solution.py:47
  113.6 6.1 %collective-permute-done.21.refs_4_ = f32[128,512]{1,0:T(8,128)S(1)} collective-permute-done((f32[128,512]{1,0:T(8,128)S(1)}, f32[128,512]{1,0:T(8,128)S(1)}, u32[]{:S(2)}, u32[]{:S(2)}) %collective-permute-start.21) | collective-permute-done | bytes 262176 | tf_op jit(solution)/shard_map/ppermute | solution.py:47
  119.7 2.5 %shard_map.42 = (f32[128,512]{1,0:T(8,128)S(1)}, f32[128,512]{1,0:T(8,128)S(1)}, f32[128,512]{1,0:T(8,128)S(1)}, f32[128,512]{1,0:T(8,128)S(1)}) custom-call(f32[2,2,520,512]{3,2,1,0:T(8,128)S(1)} %shard_map.38.refs_0_, f32[2,2,520,512]{3,2,1,0:T(8,128)S(1)} %collective-permute-done.9.refs_1_, f32[128,512]{1,0:T(8,128)S(1)} %add_add_fusion.2.refs_2_, ...), custom_call_target="tpu_custom_call" | custom-call | flops 1610612736 | bytes 4227072 | tf_op jit(solution)/shard_map/pallas_call | solution.py:259
  122.2 2.2 %collective-permute-start.23 = (f32[128,512]{1,0:T(8,128)S(1)}, f32[128,512]{1,0:T(8,128)S(1)}, u32[]{:S(2)}, u32[]{:S(2)}) collective-permute-start(f32[128,512]{1,0:T(8,128)S(1)} %get-tuple-element.74), channel_id=1, source_target_pairs={{0,17},{8,25},{16,1},{24,9},{1,16},{9,24},{17,0},{25,8},{2,19},{10... | collective-permute-start | bytes 786440 | tf_op jit(solution)/shard_map/ppermute | solution.py:47
  124.9 3.8 %collective-permute-done.23 = f32[128,512]{1,0:T(8,128)S(1)} collective-permute-done((f32[128,512]{1,0:T(8,128)S(1)}, f32[128,512]{1,0:T(8,128)S(1)}, u32[]{:S(2)}, u32[]{:S(2)}) %collective-permute-start.23) | collective-permute-done | bytes 262176 | tf_op jit(solution)/shard_map/ppermute | solution.py:47
  128.7 2.8 %collective-permute-done.24 = f32[128,512]{1,0:T(8,128)S(1)} collective-permute-done((f32[128,512]{1,0:T(8,128)S(1)}, f32[128,512]{1,0:T(8,128)S(1)}, u32[]{:S(2)}, u32[]{:S(2)}) %collective-permute-start.24) | collective-permute-done | bytes 262176 | tf_op jit(solution)/shard_map/ppermute | solution.py:47
  132.6 2.5 %collective-permute-start.26 = (f32[128,512]{1,0:T(8,128)S(1)}, f32[128,512]{1,0:T(8,128)S(1)}, u32[]{:S(2)}, u32[]{:S(2)}) collective-permute-start(f32[128,512]{1,0:T(8,128)S(1)} %add_add_fusion.1.refs_2_), channel_id=1, source_target_pairs={{0,2},{8,10},{16,18},{24,26},{1,3},{9,11},{17,19},{25,27},{2,0},{1... | collective-permute-start | bytes 786440 | tf_op jit(solution)/shard_map/ppermute | solution.py:47
  135.2 3.7 %collective-permute-done.28.refs_5_ = f32[128,512]{1,0:T(8,128)S(1)} collective-permute-done((f32[128,512]{1,0:T(8,128)S(1)}, f32[128,512]{1,0:T(8,128)S(1)}, u32[]{:S(2)}, u32[]{:S(2)}) %collective-permute-start.28) | collective-permute-done | bytes 262176 | tf_op jit(solution)/shard_map/ppermute | solution.py:47
  138.9 5.5 %collective-permute-done.27.refs_4_ = f32[128,512]{1,0:T(8,128)S(1)} collective-permute-done((f32[128,512]{1,0:T(8,128)S(1)}, f32[128,512]{1,0:T(8,128)S(1)}, u32[]{:S(2)}, u32[]{:S(2)}) %collective-permute-start.27) | collective-permute-done | bytes 262176 | tf_op jit(solution)/shard_map/ppermute | solution.py:47
  144.3 2.5 %shard_map.43 = (f32[256,256]{1,0:T(8,128)S(1)}, f32[256,256]{1,0:T(8,128)S(1)}, f32[256,256]{1,0:T(8,128)S(1)}, f32[256,256]{1,0:T(8,128)S(1)}) custom-call(f32[2,2,520,512]{3,2,1,0:T(8,128)S(1)} %collective-permute-done.10.refs_0_, f32[2,2,520,512]{3,2,1,0:T(8,128)S(1)} %shard_map.40.refs_1_, f32[128,512]{1,0:T(8,128)S(1)} %add_add_fusion.1.refs_2_, ...), custom_call_target="tpu_custom_call" | custom-call | flops 1610612736 | bytes 4227072 | tf_op jit(solution)/shard_map/pallas_call | solution.py:259
  146.8 2.1 %collective-permute-start.29 = (f32[256,256]{1,0:T(8,128)S(1)}, f32[256,256]{1,0:T(8,128)S(1)}, u32[]{:S(2)}, u32[]{:S(2)}) collective-permute-start(f32[256,256]{1,0:T(8,128)S(1)} %get-tuple-element.78), channel_id=1, source_target_pairs={{0,17},{8,25},{16,1},{24,9},{1,16},{9,24},{17,0},{25,8},{2,19},{10... | collective-permute-start | bytes 786440 | tf_op jit(solution)/shard_map/ppermute | solution.py:47
  149.5 3.6 %collective-permute-done.29 = f32[256,256]{1,0:T(8,128)S(1)} collective-permute-done((f32[256,256]{1,0:T(8,128)S(1)}, f32[256,256]{1,0:T(8,128)S(1)}, u32[]{:S(2)}, u32[]{:S(2)}) %collective-permute-start.29) | collective-permute-done | bytes 262176 | tf_op jit(solution)/shard_map/ppermute | solution.py:47
  153.1 2.7 %collective-permute-done.30 = f32[256,256]{1,0:T(8,128)S(1)} collective-permute-done((f32[256,256]{1,0:T(8,128)S(1)}, f32[256,256]{1,0:T(8,128)S(1)}, u32[]{:S(2)}, u32[]{:S(2)}) %collective-permute-start.30) | collective-permute-done | bytes 262176 | tf_op jit(solution)/shard_map/ppermute | solution.py:47
  (47 shorter events, 14.5 us)
Async XLA Ops:
  4.5 21.9 %collective-permute-start.3 = (f32[520,512]{1,0:T(8,128)S(1)}, f32[520,512]{1,0:T(8,128)S(1)}, u32[]{:S(2)}, u32[]{:S(2)}) collective-permute-start(f32[520,512]{1,0:T(8,128)S(1)} %get-tuple-element.50), channel_id=1, source_target_pairs={{0,17},{16,1},{1,16},{17,0},{2,19},{18,3},{3,18},{19,2},{4,21},{20... | collective-permute-start | bytes 3194888 | tf_op jit(solution)/shard_map/ppermute | solution.py:47
  5.3 21.2 %collective-permute-start.4 = (f32[520,512]{1,0:T(8,128)S(1)}, f32[520,512]{1,0:T(8,128)S(1)}, u32[]{:S(2)}, u32[]{:S(2)}) collective-permute-start(f32[520,512]{1,0:T(8,128)S(1)} %get-tuple-element.56), channel_id=1, source_target_pairs={{0,1},{16,17},{1,0},{17,16},{2,3},{18,19},{3,2},{19,18},{4,5},{20,... | collective-permute-start | bytes 3194888 | tf_op jit(solution)/shard_map/ppermute | solution.py:47
  6.0 20.4 %collective-permute-start.5 = (f32[520,512]{1,0:T(8,128)S(1)}, f32[520,512]{1,0:T(8,128)S(1)}, u32[]{:S(2)}, u32[]{:S(2)}) collective-permute-start(f32[520,512]{1,0:T(8,128)S(1)} %get-tuple-element.57), channel_id=1, source_target_pairs={{0,16},{16,0},{1,17},{17,1},{2,18},{18,2},{3,19},{19,3},{4,20},{20... | collective-permute-start | bytes 3194888 | tf_op jit(solution)/shard_map/ppermute | solution.py:47
  6.7 9.2 %collective-permute-start.1 = (f32[128,512]{1,0:T(8,128)S(1)}, f32[128,512]{1,0:T(8,128)S(1)}, u32[]{:S(2)}, u32[]{:S(2)}) collective-permute-start(f32[128,512]{1,0:T(8,128)S(1)} %get-tuple-element.58.refs_4_.refs_2_), channel_id=1, source_target_pairs={{0,4},{8,12},{16,20},{24,28},{1,5},{9,13},{17,21},{25,29},{2,6},{1... | collective-permute-start | bytes 786440 | tf_op jit(solution)/shard_map/ppermute | solution.py:47
  6.9 9.1 %collective-permute-start = (f32[128,512]{1,0:T(8,128)S(1)}, f32[128,512]{1,0:T(8,128)S(1)}, u32[]{:S(2)}, u32[]{:S(2)}) collective-permute-start(f32[128,512]{1,0:T(8,128)S(1)} %get-tuple-element.58.refs_4_.refs_2_), channel_id=1, source_target_pairs={{0,2},{8,10},{16,18},{24,26},{1,3},{9,11},{17,19},{25,27},{2,0},{1... | collective-permute-start | bytes 786440 | tf_op jit(solution)/shard_map/ppermute | solution.py:47
  15.9 10.5 %collective-permute-start.2 = (f32[128,512]{1,0:T(8,128)S(1)}, f32[128,512]{1,0:T(8,128)S(1)}, u32[]{:S(2)}, u32[]{:S(2)}) collective-permute-start(f32[128,512]{1,0:T(8,128)S(1)} %collective-permute-done.1.refs_6_.refs_4_), channel_id=1, source_target_pairs={{0,2},{8,10},{16,18},{24,26},{1,3},{9,11},{17,19},{25,27},{2,0},{1... | collective-permute-start | bytes 786440 | tf_op jit(solution)/shard_map/ppermute | solution.py:47
  26.5 40.0 %collective-permute-start.9 = (f32[2,2,520,512]{3,2,1,0:T(8,128)S(1)}, f32[2,2,520,512]{3,2,1,0:T(8,128)S(1)}, u32[]{:S(2)}, u32[]{:S(2)}) collective-permute-start(f32[2,2,520,512]{3,2,1,0:T(8,128)S(1)} %shard_map.38.refs_0_), channel_id=1, source_target_pairs={{0,8},{16,24},{1,9},{17,25},{2,10},{18,26},{3,11},{19,27},{4,12},{... | collective-permute-start | bytes 12779528 | tf_op jit(solution)/shard_map/ppermute | solution.py:47
  27.8 17.3 %collective-permute-start.6 = (f32[520,512]{1,0:T(8,128)S(1)}, f32[520,512]{1,0:T(8,128)S(1)}, u32[]{:S(2)}, u32[]{:S(2)}) collective-permute-start(f32[520,512]{1,0:T(8,128)S(1)} %get-tuple-element.50), channel_id=1, source_target_pairs={{8,25},{24,9},{9,24},{25,8},{10,27},{26,11},{11,26},{27,10},{12,29... | collective-permute-start | bytes 3194888 | tf_op jit(solution)/shard_map/ppermute | solution.py:47
  45.1 21.3 %collective-permute-start.8 = (f32[520,512]{1,0:T(8,128)S(1)}, f32[520,512]{1,0:T(8,128)S(1)}, u32[]{:S(2)}, u32[]{:S(2)}) collective-permute-start(f32[520,512]{1,0:T(8,128)S(1)} %get-tuple-element.57), channel_id=1, source_target_pairs={{8,24},{24,8},{9,25},{25,9},{10,26},{26,10},{11,27},{27,11},{12,28... | collective-permute-start | bytes 3194888 | tf_op jit(solution)/shard_map/ppermute | solution.py:47
  48.3 20.7 %collective-permute-start.7 = (f32[520,512]{1,0:T(8,128)S(1)}, f32[520,512]{1,0:T(8,128)S(1)}, u32[]{:S(2)}, u32[]{:S(2)}) collective-permute-start(f32[520,512]{1,0:T(8,128)S(1)} %get-tuple-element.56), channel_id=1, source_target_pairs={{8,9},{24,25},{9,8},{25,24},{10,11},{26,27},{11,10},{27,26},{12,13... | collective-permute-start | bytes 3194888 | tf_op jit(solution)/shard_map/ppermute | solution.py:47
  69.4 25.3 %collective-permute-start.10 = (f32[2,2,520,512]{3,2,1,0:T(8,128)S(1)}, f32[2,2,520,512]{3,2,1,0:T(8,128)S(1)}, u32[]{:S(2)}, u32[]{:S(2)}) collective-permute-start(f32[2,2,520,512]{3,2,1,0:T(8,128)S(1)} %shard_map.40.refs_1_), channel_id=1, source_target_pairs={{8,0},{24,16},{9,1},{25,17},{10,2},{26,18},{11,3},{27,19},{12,4},{... | collective-permute-start | bytes 12779528 | tf_op jit(solution)/shard_map/ppermute | solution.py:47
  71.0 6.4 %collective-permute-start.11 = (f32[128,512]{1,0:T(8,128)S(1)}, f32[128,512]{1,0:T(8,128)S(1)}, u32[]{:S(2)}, u32[]{:S(2)}) collective-permute-start(f32[128,512]{1,0:T(8,128)S(1)} %get-tuple-element.66), channel_id=1, source_target_pairs={{0,17},{8,25},{16,1},{24,9},{1,16},{9,24},{17,0},{25,8},{2,19},{10... | collective-permute-start | bytes 786440 | tf_op jit(solution)/shard_map/ppermute | solution.py:47
  73.5 6.9 %collective-permute-start.12 = (f32[128,512]{1,0:T(8,128)S(1)}, f32[128,512]{1,0:T(8,128)S(1)}, u32[]{:S(2)}, u32[]{:S(2)}) collective-permute-start(f32[128,512]{1,0:T(8,128)S(1)} %get-tuple-element.67), channel_id=1, source_target_pairs={{0,1},{8,9},{16,17},{24,25},{1,0},{9,8},{17,16},{25,24},{2,3},{10,... | collective-permute-start | bytes 786440 | tf_op jit(solution)/shard_map/ppermute | solution.py:47
  73.8 6.6 %collective-permute-start.13 = (f32[128,512]{1,0:T(8,128)S(1)}, f32[128,512]{1,0:T(8,128)S(1)}, u32[]{:S(2)}, u32[]{:S(2)}) collective-permute-start(f32[128,512]{1,0:T(8,128)S(1)} %get-tuple-element.68), channel_id=1, source_target_pairs={{0,16},{8,24},{16,0},{24,8},{1,17},{9,25},{17,1},{25,9},{2,18},{10... | collective-permute-start | bytes 786440 | tf_op jit(solution)/shard_map/ppermute | solution.py:47
  80.5 9.0 %collective-permute-start.15 = (f32[128,512]{1,0:T(8,128)S(1)}, f32[128,512]{1,0:T(8,128)S(1)}, u32[]{:S(2)}, u32[]{:S(2)}) collective-permute-start(f32[128,512]{1,0:T(8,128)S(1)} %add_add_fusion.3.refs_2_), channel_id=1, source_target_pairs={{0,4},{8,12},{16,20},{24,28},{1,5},{9,13},{17,21},{25,29},{2,6},{1... | collective-permute-start | bytes 786440 | tf_op jit(solution)/shard_map/ppermute | solution.py:47
  81.1 8.4 %collective-permute-start.14 = (f32[128,512]{1,0:T(8,128)S(1)}, f32[128,512]{1,0:T(8,128)S(1)}, u32[]{:S(2)}, u32[]{:S(2)}) collective-permute-start(f32[128,512]{1,0:T(8,128)S(1)} %add_add_fusion.3.refs_2_), channel_id=1, source_target_pairs={{0,2},{8,10},{16,18},{24,26},{1,3},{9,11},{17,19},{25,27},{2,0},{1... | collective-permute-start | bytes 786440 | tf_op jit(solution)/shard_map/ppermute | solution.py:47
  89.5 5.2 %collective-permute-start.16 = (f32[128,512]{1,0:T(8,128)S(1)}, f32[128,512]{1,0:T(8,128)S(1)}, u32[]{:S(2)}, u32[]{:S(2)}) collective-permute-start(f32[128,512]{1,0:T(8,128)S(1)} %collective-permute-done.15.refs_4_), channel_id=1, source_target_pairs={{0,2},{8,10},{16,18},{24,26},{1,3},{9,11},{17,19},{25,27},{2,0},{1... | collective-permute-start | bytes 786440 | tf_op jit(solution)/shard_map/ppermute | solution.py:47
  97.2 6.5 %collective-permute-start.17 = (f32[128,512]{1,0:T(8,128)S(1)}, f32[128,512]{1,0:T(8,128)S(1)}, u32[]{:S(2)}, u32[]{:S(2)}) collective-permute-start(f32[128,512]{1,0:T(8,128)S(1)} %get-tuple-element.70), channel_id=1, source_target_pairs={{0,17},{8,25},{16,1},{24,9},{1,16},{9,24},{17,0},{25,8},{2,19},{10... | collective-permute-start | bytes 786440 | tf_op jit(solution)/shard_map/ppermute | solution.py:47
  98.9 7.2 %collective-permute-start.18 = (f32[128,512]{1,0:T(8,128)S(1)}, f32[128,512]{1,0:T(8,128)S(1)}, u32[]{:S(2)}, u32[]{:S(2)}) collective-permute-start(f32[128,512]{1,0:T(8,128)S(1)} %get-tuple-element.71), channel_id=1, source_target_pairs={{0,1},{8,9},{16,17},{24,25},{1,0},{9,8},{17,16},{25,24},{2,3},{10,... | collective-permute-start | bytes 786440 | tf_op jit(solution)/shard_map/ppermute | solution.py:47
  99.2 7.0 %collective-permute-start.19 = (f32[128,512]{1,0:T(8,128)S(1)}, f32[128,512]{1,0:T(8,128)S(1)}, u32[]{:S(2)}, u32[]{:S(2)}) collective-permute-start(f32[128,512]{1,0:T(8,128)S(1)} %get-tuple-element.72), channel_id=1, source_target_pairs={{0,16},{8,24},{16,0},{24,8},{1,17},{9,25},{17,1},{25,9},{2,18},{10... | collective-permute-start | bytes 786440 | tf_op jit(solution)/shard_map/ppermute | solution.py:47
  106.3 7.3 %collective-permute-start.22 = (f32[128,512]{1,0:T(8,128)S(1)}, f32[128,512]{1,0:T(8,128)S(1)}, u32[]{:S(2)}, u32[]{:S(2)}) collective-permute-start(f32[128,512]{1,0:T(8,128)S(1)} %add_add_fusion.2.refs_2_), channel_id=1, source_target_pairs={{0,6},{8,14},{16,22},{24,30},{1,7},{9,15},{17,23},{25,31},{2,4},{1... | collective-permute-start | bytes 786440 | tf_op jit(solution)/shard_map/ppermute | solution.py:47
  106.7 13.0 %collective-permute-start.21 = (f32[128,512]{1,0:T(8,128)S(1)}, f32[128,512]{1,0:T(8,128)S(1)}, u32[]{:S(2)}, u32[]{:S(2)}) collective-permute-start(f32[128,512]{1,0:T(8,128)S(1)} %add_add_fusion.2.refs_2_), channel_id=1, source_target_pairs={{0,4},{8,12},{16,20},{24,28},{1,5},{9,13},{17,21},{25,29},{2,6},{1... | collective-permute-start | bytes 786440 | tf_op jit(solution)/shard_map/ppermute | solution.py:47
  107.5 12.2 %collective-permute-start.20 = (f32[128,512]{1,0:T(8,128)S(1)}, f32[128,512]{1,0:T(8,128)S(1)}, u32[]{:S(2)}, u32[]{:S(2)}) collective-permute-start(f32[128,512]{1,0:T(8,128)S(1)} %add_add_fusion.2.refs_2_), channel_id=1, source_target_pairs={{0,2},{8,10},{16,18},{24,26},{1,3},{9,11},{17,19},{25,27},{2,0},{1... | collective-permute-start | bytes 786440 | tf_op jit(solution)/shard_map/ppermute | solution.py:47
  122.2 6.5 %collective-permute-start.23 = (f32[128,512]{1,0:T(8,128)S(1)}, f32[128,512]{1,0:T(8,128)S(1)}, u32[]{:S(2)}, u32[]{:S(2)}) collective-permute-start(f32[128,512]{1,0:T(8,128)S(1)} %get-tuple-element.74), channel_id=1, source_target_pairs={{0,17},{8,25},{16,1},{24,9},{1,16},{9,24},{17,0},{25,8},{2,19},{10... | collective-permute-start | bytes 786440 | tf_op jit(solution)/shard_map/ppermute | solution.py:47
  124.4 7.1 %collective-permute-start.24 = (f32[128,512]{1,0:T(8,128)S(1)}, f32[128,512]{1,0:T(8,128)S(1)}, u32[]{:S(2)}, u32[]{:S(2)}) collective-permute-start(f32[128,512]{1,0:T(8,128)S(1)} %get-tuple-element.75), channel_id=1, source_target_pairs={{0,1},{8,9},{16,17},{24,25},{1,0},{9,8},{17,16},{25,24},{2,3},{10,... | collective-permute-start | bytes 786440 | tf_op jit(solution)/shard_map/ppermute | solution.py:47
  124.5 7.0 %collective-permute-start.25 = (f32[128,512]{1,0:T(8,128)S(1)}, f32[128,512]{1,0:T(8,128)S(1)}, u32[]{:S(2)}, u32[]{:S(2)}) collective-permute-start(f32[128,512]{1,0:T(8,128)S(1)} %get-tuple-element.76), channel_id=1, source_target_pairs={{0,16},{8,24},{16,0},{24,8},{1,17},{9,25},{17,1},{25,9},{2,18},{10... | collective-permute-start | bytes 786440 | tf_op jit(solution)/shard_map/ppermute | solution.py:47
  131.6 7.3 %collective-permute-start.28 = (f32[128,512]{1,0:T(8,128)S(1)}, f32[128,512]{1,0:T(8,128)S(1)}, u32[]{:S(2)}, u32[]{:S(2)}) collective-permute-start(f32[128,512]{1,0:T(8,128)S(1)} %add_add_fusion.1.refs_2_), channel_id=1, source_target_pairs={{0,6},{8,14},{16,22},{24,30},{1,7},{9,15},{17,23},{25,31},{2,4},{1... | collective-permute-start | bytes 786440 | tf_op jit(solution)/shard_map/ppermute | solution.py:47
  132.6 11.7 %collective-permute-start.27 = (f32[128,512]{1,0:T(8,128)S(1)}, f32[128,512]{1,0:T(8,128)S(1)}, u32[]{:S(2)}, u32[]{:S(2)}) collective-permute-start(f32[128,512]{1,0:T(8,128)S(1)} %add_add_fusion.1.refs_2_), channel_id=1, source_target_pairs={{0,4},{8,12},{16,20},{24,28},{1,5},{9,13},{17,21},{25,29},{2,6},{1... | collective-permute-start | bytes 786440 | tf_op jit(solution)/shard_map/ppermute | solution.py:47
  132.6 11.7 %collective-permute-start.26 = (f32[128,512]{1,0:T(8,128)S(1)}, f32[128,512]{1,0:T(8,128)S(1)}, u32[]{:S(2)}, u32[]{:S(2)}) collective-permute-start(f32[128,512]{1,0:T(8,128)S(1)} %add_add_fusion.1.refs_2_), channel_id=1, source_target_pairs={{0,2},{8,10},{16,18},{24,26},{1,3},{9,11},{17,19},{25,27},{2,0},{1... | collective-permute-start | bytes 786440 | tf_op jit(solution)/shard_map/ppermute | solution.py:47
  146.8 6.3 %collective-permute-start.29 = (f32[256,256]{1,0:T(8,128)S(1)}, f32[256,256]{1,0:T(8,128)S(1)}, u32[]{:S(2)}, u32[]{:S(2)}) collective-permute-start(f32[256,256]{1,0:T(8,128)S(1)} %get-tuple-element.78), channel_id=1, source_target_pairs={{0,17},{8,25},{16,1},{24,9},{1,16},{9,24},{17,0},{25,8},{2,19},{10... | collective-permute-start | bytes 786440 | tf_op jit(solution)/shard_map/ppermute | solution.py:47
  149.0 6.8 %collective-permute-start.30 = (f32[256,256]{1,0:T(8,128)S(1)}, f32[256,256]{1,0:T(8,128)S(1)}, u32[]{:S(2)}, u32[]{:S(2)}) collective-permute-start(f32[256,256]{1,0:T(8,128)S(1)} %get-tuple-element.79), channel_id=1, source_target_pairs={{0,1},{8,9},{16,17},{24,25},{1,0},{9,8},{17,16},{25,24},{2,3},{10,... | collective-permute-start | bytes 786440 | tf_op jit(solution)/shard_map/ppermute | solution.py:47
  149.2 6.6 %collective-permute-start.31 = (f32[256,256]{1,0:T(8,128)S(1)}, f32[256,256]{1,0:T(8,128)S(1)}, u32[]{:S(2)}, u32[]{:S(2)}) collective-permute-start(f32[256,256]{1,0:T(8,128)S(1)} %get-tuple-element.80), channel_id=1, source_target_pairs={{0,16},{8,24},{16,0},{24,8},{1,17},{9,25},{17,1},{25,9},{2,18},{10... | collective-permute-start | bytes 786440 | tf_op jit(solution)/shard_map/ppermute | solution.py:47
  (2 other events, 1.9 us)
